TPU v7x, 128 devices: a whole 4x4x4 slice. The times are simulated.
128 devices in a mesh: wide: 32 (over x, z, core), narrow: 4 (over y).
Axes of the slice: x: 4, y: 4, z: 4, core: 2. Of those that a mesh axis runs over, the one named last changes fastest.
Arguments:
- points: bfloat16 [131072, 256], P('wide'), may hold values from -6 to 6
- q_init: float32 [16, 131072], P(None, 'wide'), may hold values from -80 to 80
- pairs: int32 [2, 8192], P(None, ('wide', 'narrow')), may hold values from 0 to 1023, as said below
Outputs:
- basis: float32 [16, 131072], P(None, 'wide')
- coeffs: float32 [3, 2, 16, 16], replicated
Inputs may be any that keep to these rules, and one draw needn't show every extreme that they name: `pairs`: pair number g * 4 * 64 + m * 64 + o * 2 + c (g < 32, m < 4, o < 32, c < 2) has its first block in g * 32 .. (g + 1) * 32 - 1 and its second block in o * 32 .. (o + 1) * 32 - 1; the two ends of a pair differ.
All inputs are finite; a program needn't handle non-finite values.
Results may differ from a plain program's by a relative error of at most 0.0015.
Values may be sent and summed in bfloat16 or wider, within the bound.
No kernel may reach another device: no remote copies, remote signals or barrier semaphores. Data moves between devices by JAX's collectives and lax.ppermute only.
A program may use at most 64 MiB of HBM per device.

v0:
```python
import jax
import jax.numpy as jnp
from jax import lax
from jax.sharding import PartitionSpec as P

BS = 128
STEPS = 3


KERNEL_FACTOR = 3.0
EPSILON = 1e-06
HIGH = lax.Precision.HIGHEST
pair_group = 32


def unit_rows(points):
    wide32 = points.astype(jnp.float32)
    scaled = wide32 * lax.rsqrt(jnp.sum(wide32 * wide32, axis=-1, keepdims=True) + EPSILON)
    return scaled.astype(jnp.bfloat16)


def tile_terms(first_pts, second_pts, first_vec, second_vec):
    inner_products = jnp.einsum(
        "paf,pbf->pab", first_pts, second_pts, preferred_element_type=jnp.float32
    )
    kernel_values = jnp.exp(KERNEL_FACTOR * (inner_products - 1.0))
    to_first = jnp.einsum("pab,prb->pra", kernel_values, second_vec, precision=HIGH)
    to_second = jnp.einsum("pab,pra->prb", kernel_values, first_vec, precision=HIGH)
    return (to_first, to_second)


def per_device(points, q_init, pairs):
    wide_count = lax.axis_size("wide")
    wide_pos = lax.axis_index("wide")
    own_blocks = points.shape[0] // BS
    width = points.shape[1]
    vec_rows = q_init.shape[0]
    pair_count = pairs.shape[1]
    capacity = pair_count // wide_count
    total_points = own_blocks * BS * wide_count
    unit = unit_rows(points).reshape(own_blocks, BS, width)
    first_local = pairs[0] - wide_pos * own_blocks
    wanted = pairs[1].reshape(wide_count, capacity)
    local_ids = (
        lax.all_to_all(wanted, "wide", split_axis=0, concat_axis=0, tiled=True)
        - wide_pos * own_blocks
    )
    replies = lax.all_to_all(unit[local_ids], "wide", split_axis=0, concat_axis=0, tiled=True)
    second_pts = replies
    second_pts = second_pts.reshape(pair_count, BS, width)
    targets = jnp.concatenate([first_local, local_ids.reshape(pair_count)], axis=0)
    owners = (jnp.arange(own_blocks, dtype=jnp.int32)[:, None] == targets[None, :]).astype(
        jnp.float32
    )

    def grouped(values):
        return values.reshape((pair_count // pair_group, pair_group) + values.shape[1:])

    def single_group(items):
        first_ids, second_p, first_v, second_v = items
        return tile_terms(unit[first_ids], second_p, first_v, second_v)

    def gram_sums(values):
        return lax.psum(values, "wide")

    gram0 = gram_sums(jnp.dot(q_init, q_init.T, precision=HIGH)) / total_points
    factor0 = jnp.linalg.cholesky(gram0)
    present_portion = lax.linalg.triangular_solve(factor0, q_init, left_side=True, lower=True)
    current = present_portion
    previous = jnp.zeros_like(present_portion)
    last = jnp.zeros((vec_rows, vec_rows), jnp.float32)
    records = []
    for step in range(STEPS):
        rows = current.reshape(vec_rows, own_blocks, BS).transpose(1, 0, 2)
        second_vec = lax.all_to_all(
            rows[local_ids], "wide", split_axis=0, concat_axis=0, tiled=True
        ).reshape(pair_count, vec_rows, BS)
        first_vec = rows[first_local]
        to_first, to_second = lax.map(
            single_group,
            (grouped(first_local), grouped(second_pts), grouped(first_vec), grouped(second_vec)),
        )
        to_first = to_first.reshape(pair_count, vec_rows * BS)
        returned = lax.all_to_all(
            to_second.reshape(wide_count, capacity, vec_rows * BS),
            "wide",
            split_axis=0,
            concat_axis=0,
            tiled=True,
        )
        terms = jnp.concatenate([to_first, returned.reshape(pair_count, vec_rows * BS)], axis=0)
        summed_blocks = jnp.dot(owners, terms, precision=HIGH)
        summed_blocks = lax.psum(summed_blocks, "narrow")
        image = summed_blocks.reshape(-1, vec_rows, BS).transpose(1, 0, 2).reshape(vec_rows, -1)
        residual = image - jnp.dot(last.T, previous, precision=HIGH)
        along = gram_sums(jnp.dot(present_portion, residual.T, precision=HIGH)) / total_points
        remainder = residual - jnp.dot(along.T, present_portion, precision=HIGH)
        gram = gram_sums(jnp.dot(remainder, remainder.T, precision=HIGH)) / total_points
        factor = jnp.linalg.cholesky(gram)
        records.append(jnp.stack([along, factor]))
        previous = present_portion
        last = factor
        present_portion = lax.linalg.triangular_solve(factor, remainder, left_side=True, lower=True)
        current = present_portion
    return (current, jnp.stack(records))


def solution(mesh):
    placed = (P("wide", None), P(None, "wide"), P(None, ("wide", "narrow")))
    return jax.shard_map(
        per_device, mesh=mesh, in_specs=placed, out_specs=(P(None, "wide"), P()), check_vma=False
    )
```

profile of v0, /device:TPU:1, one launch (start us, length us, event | category | flops | bytes accessed | tf_op | source)
XLA Modules:
  0.0 886.6 jit_solution(6009941300447082096)
XLA Ops:
  8.7 9.4 %all-to-all-start = ((s32[32,1,2]{2,1,0:T(1,128)}), s32[32,1,2]{2,1,0:T(1,128)S(1)}, u32[]{:S(2)}, u32[]{:S(2)}) async-start(s32[32,1,2]{2,1,0:T(1,128)} %bitcast.22), calls=%async_computation | async-start | bytes 32768 | tf_op jit(solution)/shard_map/all_to_all | solution.py:45
  18.6 63.5 %psum.70 = f32[16,16]{1,0:T(8,128)S(1)} all-reduce(f32[16,16]{1,0:T(8,128)S(1)} %fusion.152), channel_id=1, replica_groups=mesh['wide'=32,'narrow'=4] {'wide'}, use_global_device_ids=true, to_apply=%region_1.0 | all-reduce | flops 256 | bytes 2048 | tf_op jit(solution)/shard_map/psum | solution.py:64
  86.7 2.2 fusion.78
  91.9 8.9 %all-to-all-start.1 = ((f32[32,2,16,128]{3,2,1,0:T(8,128)}), f32[32,2,16,128]{3,2,1,0:T(8,128)S(1)}, u32[]{:S(2)}, u32[]{:S(2)}) async-start(f32[32,2,16,128]{3,2,1,0:T(8,128)} %bitcast.28), calls=%async_computation.1 | async-start | bytes 1048576 | tf_op jit(solution)/shard_map/all_to_all | solution.py:75
  100.8 1.9 fusion.79
  102.8 2.8 gather_fusion.4
  105.6 7.0 all-to-all-done.1
  112.6 4.8 all-to-all-start.2
  119.0 50.3 %all-to-all-done.2 = bf16[32,2,128,256]{3,2,1,0:T(8,128)(2,1)} async-done(((bf16[32,2,128,256]{3,2,1,0:T(8,128)(2,1)}), bf16[32,2,128,256]{3,2,1,0:T(8,128)(2,1)}, u32[]{:S(2)}, u32[]{:S(2)}) %all-to-all-start.2) | async-done | bytes 4194336 | tf_op jit(solution)/shard_map/all_to_all | solution.py:48
  170.9 23.6 %while.42 = (s32[]{:T(128)}, f32[2,32,16,128]{3,2,1,0:T(8,128)}, f32[2,32,16,128]{3,2,1,0:T(8,128)}, f32[2,32,16,128]{3,2,1,0:T(8,128)S(1)}, s32[2,32]{1,0:T(2,1...) while((s32[]{:T(128)}, f32[2,32,16,128]{3,2,1,0:T(8,128)}, ...), condition=%wide.region_5.8_spmd, body=%wide.region_4.7_spmd.sunk | while | flops 471860320 | bytes 17833084 | solution.py:79
  170.9 2.0 gather_fusion
  173.0 2.9 fusion.217
  175.9 4.1 fusion.218
  180.0 2.8 fusion.219
  182.7 2.0 gather_fusion
  184.8 2.9 fusion.217
  187.7 4.1 fusion.218
  191.8 2.8 fusion.219
  194.5 2.1 reshape.254
  196.7 7.2 all-to-all-start.3
  205.5 10.1 %all-to-all-done.3 = f32[32,2,2048]{2,1,0:T(2,128)} async-done(((f32[32,2,2048]{2,1,0:T(2,128)}), f32[32,2,2048]{2,1,0:T(2,128)}, u32[]{:S(2)}, u32[]{:S(2)}) %all-to-all-start.3) | async-done | bytes 524320 | tf_op jit(solution)/shard_map/all_to_all | solution.py:84
  215.5 2.2 reshape.255
  217.7 1.5 convolution_bitcast_fusion.2
  220.1 37.1 %all-reduce.4.cloned.1.call-done = f32[16,4096]{1,0:T(8,128)} async-done(((f32[16,4096]{1,0:T(8,128)}), f32[16,4096]{1,0:T(8,128)}) %all-reduce.4.cloned.1.call-update) | async-done | bytes 262160 | tf_op jit(solution)/shard_map/psum | solution.py:93
  258.8 65.9 %psum.72 = f32[16,16]{1,0:T(8,128)S(1)} all-reduce(f32[16,16]{1,0:T(8,128)S(1)} %fusion.153), channel_id=1, replica_groups=mesh['wide'=32,'narrow'=4] {'wide'}, use_global_device_ids=true, to_apply=%region_7.10 | all-reduce | flops 256 | bytes 2048 | tf_op jit(solution)/shard_map/psum | solution.py:64
  325.7 65.9 %psum.73 = f32[16,16]{1,0:T(8,128)S(1)} all-reduce(f32[16,16]{1,0:T(8,128)S(1)} %fusion.154), channel_id=1, replica_groups=mesh['wide'=32,'narrow'=4] {'wide'}, use_global_device_ids=true, to_apply=%region_8.11 | all-reduce | flops 256 | bytes 2048 | tf_op jit(solution)/shard_map/psum | solution.py:64
  397.6 4.9 all-to-all-start.4
  403.9 10.3 %all-to-all-done.4 = f32[32,2,16,128]{3,2,1,0:T(8,128)} async-done(((f32[32,2,16,128]{3,2,1,0:T(8,128)}), f32[32,2,16,128]{3,2,1,0:T(8,128)}, u32[]{:S(2)}, u32[]{:S(2)}) %all-to-all-start.4) | async-done | bytes 524320 | tf_op jit(solution)/shard_map/all_to_all | solution.py:75
  415.9 25.6 %while.43 = (s32[]{:T(128)}, f32[2,32,16,128]{3,2,1,0:T(8,128)}, f32[2,32,16,128]{3,2,1,0:T(8,128)}, f32[2,32,16,128]{3,2,1,0:T(8,128)}, s32[2,32]{1,0:T(2,128)S...) while((s32[]{:T(128)}, f32[2,32,16,128]{3,2,1,0:T(8,128)}, ...), condition=%wide.region_10.13_spmd, body=%wide.region_9.12_spmd.sunk | while | flops 471860320 | bytes 17833084 | solution.py:79
  415.9 2.0 gather_fusion.1
  417.9 2.9 fusion.225
  420.9 5.1 fusion.226
  425.9 2.7 fusion.227
  428.7 2.0 gather_fusion.1
  430.7 2.9 fusion.225
  433.6 5.1 fusion.226
  438.7 2.8 fusion.227
  441.5 2.1 reshape.261
  443.6 4.4 all-to-all-start.5
  449.3 10.1 %all-to-all-done.5 = f32[32,2,2048]{2,1,0:T(2,128)} async-done(((f32[32,2,2048]{2,1,0:T(2,128)}), f32[32,2,2048]{2,1,0:T(2,128)}, u32[]{:S(2)}, u32[]{:S(2)}) %all-to-all-start.5) | async-done | bytes 524320 | tf_op jit(solution)/shard_map/all_to_all | solution.py:84
  459.4 2.2 reshape.262
  461.6 1.5 convolution_bitcast_fusion.1
  463.9 36.3 %all-reduce.6.cloned.1.call-done = f32[16,4096]{1,0:T(8,128)} async-done(((f32[16,4096]{1,0:T(8,128)}), f32[16,4096]{1,0:T(8,128)}) %all-reduce.6.cloned.1.call-update) | async-done | bytes 262160 | tf_op jit(solution)/shard_map/psum | solution.py:93
  500.2 1.9 convolution_subtract_fusion.3
  502.6 66.2 %psum.75 = f32[16,16]{1,0:T(8,128)S(1)} all-reduce(f32[16,16]{1,0:T(8,128)S(1)} %fusion.155), channel_id=1, replica_groups=mesh['wide'=32,'narrow'=4] {'wide'}, use_global_device_ids=true, to_apply=%region_12.15 | all-reduce | flops 256 | bytes 2048 | tf_op jit(solution)/shard_map/psum | solution.py:64
  569.7 65.9 %psum.76 = f32[16,16]{1,0:T(8,128)S(1)} all-reduce(f32[16,16]{1,0:T(8,128)S(1)} %fusion.156), channel_id=1, replica_groups=mesh['wide'=32,'narrow'=4] {'wide'}, use_global_device_ids=true, to_apply=%region_13.16 | all-reduce | flops 256 | bytes 2048 | tf_op jit(solution)/shard_map/psum | solution.py:64
  642.4 4.2 all-to-all-start.6
  648.1 10.3 %all-to-all-done.6 = f32[32,2,16,128]{3,2,1,0:T(8,128)S(1)} async-done(((f32[32,2,16,128]{3,2,1,0:T(8,128)}), f32[32,2,16,128]{3,2,1,0:T(8,128)S(1)}, u32[]{:S(2)}, u32[]{:S(2)}) %all-to-all-start.6) | async-done | bytes 524320 | tf_op jit(solution)/shard_map/all_to_all | solution.py:75
  660.0 23.6 %while.44 = (s32[]{:T(128)}, f32[2,32,16,128]{3,2,1,0:T(8,128)}, f32[2,32,16,128]{3,2,1,0:T(8,128)}, f32[2,32,16,128]{3,2,1,0:T(8,128)S(1)}, s32[2,32]{1,0:T(2,1...) while((s32[]{:T(128)}, f32[2,32,16,128]{3,2,1,0:T(8,128)}, ...), condition=%wide.region_15.18_spmd, body=%wide.region_14.17_spmd.sunk | while | flops 471860320 | bytes 17833084 | solution.py:79
  660.0 2.0 gather_fusion.2
  662.0 2.9 fusion.233
  665.0 4.1 fusion.234
  669.1 2.7 fusion.235
  671.8 2.0 gather_fusion.2
  673.8 2.9 fusion.233
  676.8 4.1 fusion.234
  680.9 2.7 fusion.235
  683.6 2.1 reshape.268
  685.7 3.7 all-to-all-start.7
  690.7 10.2 %all-to-all-done.7 = f32[32,2,2048]{2,1,0:T(2,128)S(1)} async-done(((f32[32,2,2048]{2,1,0:T(2,128)}), f32[32,2,2048]{2,1,0:T(2,128)S(1)}, u32[]{:S(2)}, u32[]{:S(2)}) %all-to-all-start.7) | async-done | bytes 524320 | tf_op jit(solution)/shard_map/all_to_all | solution.py:84
  702.6 36.3 %all-reduce.8.cloned.1.call-done = f32[16,4096]{1,0:T(8,128)} async-done(((f32[16,4096]{1,0:T(8,128)}), f32[16,4096]{1,0:T(8,128)}) %all-reduce.8.cloned.1.call-update) | async-done | bytes 262160 | tf_op jit(solution)/shard_map/psum | solution.py:93
  738.9 2.0 convolution_subtract_fusion.1
  741.4 66.0 %psum.78 = f32[16,16]{1,0:T(8,128)S(1)} all-reduce(f32[16,16]{1,0:T(8,128)S(1)} %fusion.157), channel_id=1, replica_groups=mesh['wide'=32,'narrow'=4] {'wide'}, use_global_device_ids=true, to_apply=%region_17.20 | all-reduce | flops 256 | bytes 2048 | tf_op jit(solution)/shard_map/psum | solution.py:64
  808.2 65.9 %psum.79 = f32[16,16]{1,0:T(8,128)S(1)} all-reduce(f32[16,16]{1,0:T(8,128)S(1)} %fusion.158), channel_id=1, replica_groups=mesh['wide'=32,'narrow'=4] {'wide'}, use_global_device_ids=true, to_apply=%region_18.21 | all-reduce | flops 256 | bytes 2048 | tf_op jit(solution)/shard_map/psum | solution.py:64
  (138 shorter events, 50.2 us)
Async XLA Ops:
  7.2 11.0 %copy-start = (f32[16,4096]{1,0:T(8,128)S(1)}, f32[16,4096]{1,0:T(8,128)}, u32[]{:S(2)}) copy-start(f32[16,4096]{1,0:T(8,128)} %param.13) | copy-start | bytes 786436
  8.7 80.3 %all-to-all-start = ((s32[32,1,2]{2,1,0:T(1,128)}), s32[32,1,2]{2,1,0:T(1,128)S(1)}, u32[]{:S(2)}, u32[]{:S(2)}) async-start(s32[32,1,2]{2,1,0:T(1,128)} %bitcast.22), calls=%async_computation | async-start | bytes 32768 | tf_op jit(solution)/shard_map/all_to_all | solution.py:45
  91.9 20.7 %all-to-all-start.1 = ((f32[32,2,16,128]{3,2,1,0:T(8,128)}), f32[32,2,16,128]{3,2,1,0:T(8,128)S(1)}, u32[]{:S(2)}, u32[]{:S(2)}) async-start(f32[32,2,16,128]{3,2,1,0:T(8,128)} %bitcast.28), calls=%async_computation.1 | async-start | bytes 1048576 | tf_op jit(solution)/shard_map/all_to_all | solution.py:75
  112.6 4.8 copy-start.6
  112.6 56.7 %all-to-all-start.2 = ((bf16[32,2,128,256]{3,2,1,0:T(8,128)(2,1)}), bf16[32,2,128,256]{3,2,1,0:T(8,128)(2,1)}, u32[]{:S(2)}, u32[]{:S(2)}) async-start(bf16[32,2,128,256]{3,2,1,0:T(8,128)(2,1)} %bitcast.297), calls=%async_computation.2 | async-start | bytes 8388608 | tf_op jit(solution)/shard_map/all_to_all | solution.py:48
  175.9 4.1 copy-start.2
  187.7 4.1 copy-start.2
  196.7 18.9 %all-to-all-start.3 = ((f32[32,2,2048]{2,1,0:T(2,128)}), f32[32,2,2048]{2,1,0:T(2,128)}, u32[]{:S(2)}, u32[]{:S(2)}) async-start(f32[32,2,2048]{2,1,0:T(2,128)} %reshape.254), calls=%async_computation.3 | async-start | bytes 1048576 | tf_op jit(solution)/shard_map/all_to_all | solution.py:84
  203.9 53.3 %all-reduce.4.cloned.1.call-start = ((), (), s32[]{:S(2)}) async-start(), calls=%async_computation.8 | async-start | bytes 524288 | tf_op jit(solution)/shard_map/psum | solution.py:93
  397.6 16.7 %all-to-all-start.4 = ((f32[32,2,16,128]{3,2,1,0:T(8,128)}), f32[32,2,16,128]{3,2,1,0:T(8,128)}, u32[]{:S(2)}, u32[]{:S(2)}) async-start(f32[32,2,16,128]{3,2,1,0:T(8,128)} %bitcast.307), calls=%async_computation.4 | async-start | bytes 1048576 | tf_op jit(solution)/shard_map/all_to_all | solution.py:75
  420.9 5.1 copy-start.3
  433.6 5.1 copy-start.3
  443.6 15.8 %all-to-all-start.5 = ((f32[32,2,2048]{2,1,0:T(2,128)}), f32[32,2,2048]{2,1,0:T(2,128)}, u32[]{:S(2)}, u32[]{:S(2)}) async-start(f32[32,2,2048]{2,1,0:T(2,128)} %reshape.261), calls=%async_computation.5 | async-start | bytes 1048576 | tf_op jit(solution)/shard_map/all_to_all | solution.py:84
  448.0 52.2 %all-reduce.6.cloned.1.call-start = ((), (), s32[]{:S(2)}) async-start(), calls=%async_computation.9 | async-start | bytes 524288 | tf_op jit(solution)/shard_map/psum | solution.py:93
  640.2 0.7 copy-start.4
  642.4 16.0 %all-to-all-start.6 = ((f32[32,2,16,128]{3,2,1,0:T(8,128)}), f32[32,2,16,128]{3,2,1,0:T(8,128)S(1)}, u32[]{:S(2)}, u32[]{:S(2)}) async-start(f32[32,2,16,128]{3,2,1,0:T(8,128)} %bitcast.306), calls=%async_computation.6 | async-start | bytes 1048576 | tf_op jit(solution)/shard_map/all_to_all | solution.py:75
  665.0 4.1 copy-start.1
  676.8 4.1 copy-start.1
  685.7 15.2 %all-to-all-start.7 = ((f32[32,2,2048]{2,1,0:T(2,128)}), f32[32,2,2048]{2,1,0:T(2,128)S(1)}, u32[]{:S(2)}, u32[]{:S(2)}) async-start(f32[32,2,2048]{2,1,0:T(2,128)} %reshape.268), calls=%async_computation.7 | async-start | bytes 1048576 | tf_op jit(solution)/shard_map/all_to_all | solution.py:84
  689.4 49.5 %all-reduce.8.cloned.1.call-start = ((), (), s32[]{:S(2)}) async-start(), calls=%async_computation.10 | async-start | bytes 524288 | tf_op jit(solution)/shard_map/psum | solution.py:93
  690.7 50.3 %copy-start.5 = (f32[16,4096]{1,0:T(8,128)S(1)}, f32[16,4096]{1,0:T(8,128)}, u32[]{:S(2)}) copy-start(f32[16,4096]{1,0:T(8,128)} %copy-done.4) | copy-start | bytes 786436
Sparse Core Ops, SparseCore 0:
  220.2 36.9 all-reduce.3
  464.0 36.1 all-reduce.5
  702.7 36.1 all-reduce.7
where the time goes:
time: 888 us; the launch traced here: 887 us
  blocking collectives  459 us (52%)
  waiting for transfers between devices  218 us (25%)
  matrix products  76 us (9%)
  local copies, waits for them, and re-layouts  48.6 us (5%)
  starting transfers between devices  47.8 us (5%)
  other arithmetic  22.4 us (3%)
  between operations  14.3 us (2%)
    psum x7, blocking collectives, gram_sums(): return lax.psum(values, 'wide')  459 us
    psum x3, waiting for transfers between devices, per_device(): summed_blocks = lax.psum(summed_blocks, 'narrow')  110 us
    all_to_all x1, waiting for transfers between devices, per_device(): lax.all_to_all(unit[local_ids], 'wide', split_axis=0, concat_axis=0, tile...  50.3 us
    all_to_all x3, waiting for transfers between devices, per_device(): lax.all_to_all(to_second.reshape(wide_count, capacity, vec_rows * BS), 'w...  30.4 us
    all_to_all x3, waiting for transfers between devices, per_device(): lax.all_to_all(rows[local_ids], 'wide', split_axis=0, concat_axis=0, tile...  27.6 us
    dot_general x6, matrix products, tile_terms(): jnp.einsum('pab,prb->pra', kernel_values, second_vec, precision=HIGH)  26.5 us
    all_to_all x3, starting transfers between devices, per_device(): lax.all_to_all(rows[local_ids], 'wide', split_axis=0, concat_axis=0, tile...  18 us
  transfers between devices with their start and end apart: 11, of which 10 were waited for; matrix products, arithmetic and copies ran while one was open for 2% of the time, Pallas kernels for 0%

commit v1 on v0

v1 whole, which is shorter than its diff:
```python
import functools

import jax
import jax.numpy as jnp
from jax import lax
from jax.experimental import pallas as pl
from jax.experimental.pallas import tpu as pltpu
from jax.sharding import PartitionSpec as P

BS = 128
STEPS = 3
KERNEL_FACTOR = 3.0
EPSILON = 1e-06
HIGH = lax.Precision.HIGHEST
VMEM_LIMIT = 48 * 2**20
TAIL = 8
BF = jnp.bfloat16
F32 = jnp.float32
NT = (((1,), (1,)), ((), ()))
TN = (((0,), (0,)), ((), ()))
NN = (((1,), (0,)), ((), ()))


def mm(a, b, dims):
    return lax.dot_general(a, b, dims, precision=HIGH, preferred_element_type=F32)


def mb(a, b, dims):
    return lax.dot_general(a, b, dims, preferred_element_type=F32)


def split(x):
    high = x.astype(BF)
    return high, (x - high.astype(F32)).astype(BF)


def fold(m):
    return jnp.concatenate([m[:8], m[8:], jnp.zeros((8, 96), F32)], axis=1)


def unfold(t):
    return jnp.concatenate([t[:, :16], t[:, 16:32]], axis=0)


def block(i):
    return pl.ds(pl.multiple_of(i * BS, BS), BS)


def factor_of(gram):
    n = gram.shape[0]
    rows = lax.broadcasted_iota(jnp.int32, (n, n), 0)
    cols = lax.broadcasted_iota(jnp.int32, (n, n), 1)
    low = jnp.zeros((n, n), F32)
    inverse = (rows == cols).astype(F32)
    left = gram
    for j in range(n):
        root = jnp.sqrt(left[j : j + 1, j : j + 1])
        scale = 1.0 / root
        column = jnp.where(rows >= j, left[:, j : j + 1] * scale, 0.0)
        low = jnp.where(cols == j, column, low)
        line = inverse[j : j + 1, :] * scale
        below = jnp.where(rows > j, column, 0.0)
        left = left - below * (left[j : j + 1, :] * scale)
        inverse = jnp.where(rows == j, line, inverse - below * line)
    return low, inverse


def pair_terms(tile, first, second):
    t_high, t_low = split(tile)
    f_high, f_low = first
    s_high, s_low = second
    rows = f_high.shape[0]
    a = mb(jnp.concatenate([s_high, s_low], axis=0), t_high, NT)
    to_first = a[:rows] + a[rows:] + mb(s_high, t_low, NT)
    b = mb(jnp.concatenate([f_high, f_low], axis=0), t_high, NN)
    to_second = b[:rows] + b[rows:] + mb(f_high, t_low, NN)
    return to_first, to_second


def start_kernel(wide, cap, first_ids, second_ids, points, q, unit, out, vec, meta, sem):
    own_blocks = points.shape[0] // BS
    slot_rows = BS + q.shape[0]

    def normalise(b, carry):
        rows = block(b)
        x = points[rows, :].astype(F32)
        x = x * lax.rsqrt(jnp.sum(x * x, axis=-1, keepdims=True) + EPSILON)
        unit[rows, :] = x.astype(BF)
        high, low = split(q[:, rows])
        vec[b] = jnp.concatenate([high, low], axis=1)
        return carry

    lax.fori_loop(0, own_blocks, normalise, 0, unroll=4)

    def send(p, carry):
        ids = [jnp.full((16, BS), second_ids[p * cap + c].astype(F32)) for c in range(2)]
        meta[p] = jnp.concatenate(ids, axis=1).astype(BF)
        for c in range(cap):
            i = first_ids[p * cap + c]
            pltpu.make_async_copy(
                unit.at[block(i), :], out.at[p, pl.ds(c * slot_rows, BS), :], sem
            ).start()
            pltpu.make_async_copy(
                vec.at[i], out.at[p, pl.ds(c * slot_rows + BS, 16), :], sem
            ).start()
        pltpu.make_async_copy(meta.at[p], out.at[p, pl.ds(cap * slot_rows, 16), :], sem).start()
        return carry

    lax.fori_loop(0, wide, send, 0)
    pltpu.make_async_copy(out, out, sem).wait()


def tiles_kernel(peers, cap, ids, got, unit, q, tiles, back, total, gram):
    step = pl.program_id(0)
    vec_rows = q.shape[0]
    slot_rows = BS + vec_rows

    @pl.when(step == 0)
    def _():
        total[...] = jnp.zeros_like(total)
        gram[...] = fold(mm(q[...], q[...], NT))

    for p in range(peers):
        for c in range(cap):
            j = ids[(step * peers + p) * cap + c]
            at = c * slot_rows
            inner = mb(got[p, at : at + BS, :], unit[block(j), :], NT)
            tile = jnp.exp(KERNEL_FACTOR * (inner - 1.0))
            tiles[p * cap + c] = tile
            first = (got[p, at + BS : at + slot_rows, :BS], got[p, at + BS : at + slot_rows, BS:])
            to_first, to_second = pair_terms(tile, first, split(q[:, block(j)]))
            back[p, c * vec_rows : (c + 1) * vec_rows, :] = to_first
            total[:, block(j)] += to_second
        back[p, cap * vec_rows :, :] = gram[...]


def terms_kernel(peers, cap, points, ids, got, tiles, w0, q, back, total, w1, along, gram):
    step = pl.program_id(0)
    vec_rows = q.shape[0]

    @pl.when(step == 0)
    def _():
        total[...] = jnp.zeros_like(total)
        a = unfold(jnp.sum(got[:, cap * vec_rows :, :], axis=0)) * (1.0 / points)
        along[...] = a
        rest = w0[...] - mm(a, q[...], TN)
        w1[...] = rest
        gram[...] = fold(mm(rest, rest, NT))

    for p in range(peers):
        for c in range(cap):
            slot = step * peers + p
            j = ids[slot * cap + c]
            first = split(got[slot, pl.ds(c * vec_rows, vec_rows), :])
            to_first, to_second = pair_terms(tiles[p * cap + c], first, split(w0[:, block(j)]))
            back[p, c * vec_rows : (c + 1) * vec_rows, :] = to_first
            total[:, block(j)] += to_second
        back[p, cap * vec_rows :, :] = gram[...]


def sum_kernel(cap, ids, got, total, out, gram):
    wide = got.shape[0]
    vec_rows = total.shape[0]
    out[...] = total[...]

    def add(p, carry):
        for c in range(cap):
            out[:, block(ids[p * cap + c])] += got[p, c * vec_rows : (c + 1) * vec_rows, :]
        return carry

    lax.fori_loop(0, wide, add, 0, unroll=4)
    gram[...] = jnp.sum(got[:, cap * vec_rows :, :], axis=0)


def factor_kernel(points, gram, low, inverse):
    low[...], inverse[...] = factor_of(unfold(gram[...]) * (1.0 / points))


def pack(cap, ids, out, vectors, matrix):
    vec_rows = vectors.shape[0]
    wide = out.shape[0]

    def put(p, carry):
        for c in range(cap):
            out[p, c * vec_rows : (c + 1) * vec_rows, :] = vectors[:, block(ids[p * cap + c])]
        out[p, cap * vec_rows :, :] = matrix
        return carry

    lax.fori_loop(0, wide, put, 0, unroll=4)


def first_update_kernel(cap, ids, t0, t1, t2, t3, q_init, inverse, q, w0, out):
    image = (t0[...] + t2[...]) + (t1[...] + t3[...])
    inv = inverse[...]
    current = mm(inv, q_init[...], NN)
    image = mm(inv, image, NN)
    q[...] = current
    w0[...] = image
    pack(cap, ids, out, w0, fold(mm(current, image, NT)))


def update_kernel(cap, ids, t0, t1, t2, t3, w1, y_old, q_old, along, low, inverse, q, w0, y, out):
    image = (t0[...] + t2[...]) + (t1[...] + t3[...])
    inv = inverse[...]
    current = mm(inv, w1[...], NN)
    image = mm(inv, image - mm(along[...], y_old[...], TN), NN)
    residual = image - mm(low[...], q_old[...], TN)
    q[...] = current
    w0[...] = residual
    y[...] = image
    matrix = fold(mm(current, residual, NT))
    if cap:
        pack(cap, ids, out, w0, matrix)
    else:
        out[...] = jnp.broadcast_to(matrix[None], out.shape)


def last_along_kernel(points, got, w0, q, w1, along, out):
    a = unfold(jnp.sum(got[...], axis=0)) * (1.0 / points)
    along[...] = a
    rest = w0[...] - mm(a, q[...], TN)
    w1[...] = rest
    out[...] = jnp.broadcast_to(fold(mm(rest, rest, NT))[None], out.shape)


def finish_kernel(points, got, w1, a0, l0, a1, l1, a2, basis, coeffs):
    low, inv = factor_of(unfold(jnp.sum(got[...], axis=0)) * (1.0 / points))
    basis[...] = mm(inv, w1[...], NN)
    for k, m in enumerate((a0, l0, a1, l1, a2)):
        coeffs[k // 2, k % 2] = m[...]
    coeffs[2, 1] = low


def call(kernel, outs, n_ids=0, **more):
    params = pltpu.CompilerParams(vmem_limit_bytes=VMEM_LIMIT)
    shapes = tuple(jax.ShapeDtypeStruct(s, d) for s, d in outs)
    if "grid" in more:
        return pl.pallas_call(
            kernel,
            out_shape=shapes,
            grid_spec=pltpu.PrefetchScalarGridSpec(num_scalar_prefetch=n_ids, **more),
            compiler_params=params,
        )

    def run(*args):
        places = [pl.BlockSpec(memory_space=pltpu.SMEM)] * n_ids
        places += [pl.BlockSpec(memory_space=pltpu.VMEM)] * (len(args) - n_ids)
        given = dict(more)
        given.setdefault("out_specs", tuple(pl.BlockSpec(memory_space=pltpu.VMEM) for _ in outs))
        return pl.pallas_call(
            kernel, out_shape=shapes, in_specs=places, compiler_params=params, **given
        )(*args)

    return run


def per_device(points, q_init, pairs):
    wide = lax.axis_size("wide")
    narrow = lax.axis_size("narrow")
    own_points, width = points.shape
    own_blocks = own_points // BS
    vec_rows = q_init.shape[0]
    pair_count = pairs.shape[1]
    cap = pair_count // wide
    total_points = own_points * wide
    local = pairs % own_blocks
    first_ids, second_ids = local[0], local[1]
    slot_rows = BS + vec_rows
    start_rows = cap * slot_rows + 16
    back_rows = cap * vec_rows + TAIL
    peers = min(4, wide)
    vectors = ((vec_rows, own_points), F32)
    small = ((vec_rows, vec_rows), F32)
    payload = ((wide, back_rows, BS), F32)
    tail = ((wide, TAIL, BS), F32)

    def exchange(x):
        return lax.all_to_all(x, "wide", split_axis=0, concat_axis=0, tiled=True)

    unit, sent = call(
        functools.partial(start_kernel, wide, cap),
        [((own_points, width), BF), ((wide, start_rows, width), BF)],
        2,
        out_specs=(pl.BlockSpec(memory_space=pltpu.VMEM), pl.BlockSpec(memory_space=pl.ANY)),
        scratch_shapes=[
            pltpu.VMEM((own_blocks, vec_rows, 2 * BS), BF),
            pltpu.VMEM((wide, 16, width), BF),
            pltpu.SemaphoreType.DMA,
        ],
    )(first_ids, second_ids, points, q_init)
    got = exchange(sent)
    ids = got[:, cap * slot_rows, ::BS].astype(jnp.int32).reshape(pair_count)

    def whole(shape):
        return pl.BlockSpec(shape, lambda i, *_: (0,) * len(shape))

    def part(shape):
        return pl.BlockSpec(shape, lambda i, *_: (i,) + (0,) * (len(shape) - 1))

    tile_part = part((peers * cap, BS, BS))
    back_part = part((peers, back_rows, BS))
    gram_scratch = [pltpu.VMEM((TAIL, BS), F32)]
    tiles, back, total = call(
        functools.partial(tiles_kernel, peers, cap),
        [((pair_count, BS, BS), F32), payload, vectors],
        1,
        grid=(wide // peers,),
        in_specs=[part((peers, start_rows, width)), whole(unit.shape), whole(q_init.shape)],
        out_specs=(tile_part, back_part, whole(q_init.shape)),
        scratch_shapes=gram_scratch,
    )(ids, got, unit, q_init)

    def gathered_sums(back, total):
        total, gram = call(
            functools.partial(sum_kernel, cap), [vectors, ((TAIL, BS), F32)], 1
        )(first_ids, exchange(back), total)
        others = [
            lax.ppermute(total, "narrow", [(i, (i + s) % narrow) for i in range(narrow)])
            for s in range(1, narrow)
        ]
        low, inverse = call(functools.partial(factor_kernel, total_points), [small, small])(gram)
        return (total, *others), low, inverse

    sums, _, inverse = gathered_sums(back, total)
    q, w0, out = call(
        functools.partial(first_update_kernel, cap), [vectors, vectors, payload], 1
    )(first_ids, *sums, q_init, inverse)
    y = w0
    records = []
    for step in range(1, STEPS):
        back, total, w1, along = call(
            functools.partial(terms_kernel, peers, cap, total_points),
            [payload, vectors, vectors, small],
            1,
            grid=(wide // peers,),
            in_specs=[
                whole(payload[0]),
                tile_part,
                whole(q_init.shape),
                whole(q_init.shape),
            ],
            out_specs=(back_part, whole(q_init.shape), whole(q_init.shape), whole(small[0])),
            scratch_shapes=gram_scratch,
        )(ids, exchange(out), tiles, w0, q)
        sums, low, inverse = gathered_sums(back, total)
        last = step == STEPS - 1
        q, w0, y, out = call(
            functools.partial(update_kernel, 0 if last else cap),
            [vectors, vectors, vectors, tail if last else payload],
            1,
        )(first_ids, *sums, w1, y, q, along, low, inverse)
        records += [along, low]
    w1, along, out = call(
        functools.partial(last_along_kernel, total_points), [vectors, small, tail]
    )(exchange(out), w0, q)
    return call(
        functools.partial(finish_kernel, total_points),
        [vectors, ((STEPS, 2, vec_rows, vec_rows), F32)],
    )(exchange(out), w1, *records, along)


def solution(mesh):
    placed = (P("wide", None), P(None, "wide"), P(None, ("wide", "narrow")))
    return jax.shard_map(
        per_device, mesh=mesh, in_specs=placed, out_specs=(P(None, "wide"), P()), check_vma=False
    )
```

time: 888 us -> 283 us (0.32)
  blocking collectives: 459 us -> 174 us
  waiting for transfers between devices: 218 us -> 38.2 us
  matrix products: 76 us -> 0 us
  Pallas kernels: 0 us -> 58 us
  local copies, waits for them, and re-layouts: 48.6 us -> 3.7 us
  starting transfers between devices: 47.8 us -> 6.94 us
  other arithmetic: 22.4 us -> 0.74 us
  between operations: 14.3 us -> 0.75 us
    psum x7 -> x0, blocking collectives: 459 us -> none  [gram_sums(): return lax.psum(values, 'wide')]
    all_to_all x0 -> x8, blocking collectives: none -> 174 us  [exchange(): return lax.all_to_all(x, 'wide', split_axis=0, concat_axis=0, tiled=True)]
    psum x3 -> x0, waiting for transfers between devices: 110 us -> none  [per_device(): summed_blocks = lax.psum(summed_blocks, 'narrow')]
    all_to_all x8 -> x0, waiting for transfers between devices: 108 us -> none  [the longest x1 50.3 us: per_device(): lax.all_to_all(unit[local_ids], 'wide', split_axis=0, concat_axis=0, tile...]
    dot_general x34 -> x0, matrix products: 73.6 us -> none  [the longest x6 26.5 us: tile_terms(): jnp.einsum('pab,prb->pra', kernel_values, second_vec, precision=HIGH)]
    pallas_call x0 -> x15, Pallas kernels: none -> 58 us  [the longest x12 23.7 us: run(): pl.pallas_call(kernel, out_shape=shapes, in_specs=places, compiler_params...]
    all_to_all x8 -> x0, starting transfers between devices: 47.5 us -> none  [the longest x3 18 us: per_device(): lax.all_to_all(rows[local_ids], 'wide', split_axis=0, concat_axis=0, tile...]
    ppermute x0 -> x9, waiting for transfers between devices: none -> 38.2 us  [gathered_sums(): lax.ppermute(total, 'narrow', [(i, (i + s) % narrow) for i in range(narro...]
  transfers between devices with their start and end apart: 11 -> 9, of which waited for: 10 -> 8; matrix products, arithmetic and copies ran while one was open for 2% -> 0% of each run, Pallas kernels for 0% -> 2%
where the time goes in v1:
time: 283 us; the launch traced here: 282 us
  blocking collectives  174 us (61%)
  Pallas kernels  58 us (20%)
  waiting for transfers between devices  38.2 us (13%)
  starting transfers between devices  6.94 us (2%)
  local copies, waits for them, and re-layouts  3.7 us (1%)
    all_to_all x8, blocking collectives, exchange(): return lax.all_to_all(x, 'wide', split_axis=0, concat_axis=0, tiled=True)  174 us
    ppermute x9, waiting for transfers between devices, gathered_sums(): lax.ppermute(total, 'narrow', [(i, (i + s) % narrow) for i in range(narro...  38.2 us
    pallas_call x12, Pallas kernels, run(): pl.pallas_call(kernel, out_shape=shapes, in_specs=places, compiler_params...  23.7 us
    pallas_call x2, Pallas kernels, per_device(): call(functools.partial(terms_kernel, peers, cap, total_points), [payload,...  17.7 us
    pallas_call x1, Pallas kernels, per_device(): call(functools.partial(tiles_kernel, peers, cap), [((pair_count, BS, BS),...  16.6 us
    ppermute x9, starting transfers between devices, gathered_sums(): lax.ppermute(total, 'narrow', [(i, (i + s) % narrow) for i in range(narro...  6.94 us
  transfers between devices with their start and end apart: 9, of which 8 were waited for; matrix products, arithmetic and copies ran while one was open for 0% of the time, Pallas kernels for 2%

profile of v1, /device:TPU:1, one launch (start us, length us, event | category | flops | bytes accessed | tf_op | source)
XLA Modules:
  0.0 282.5 jit_solution(2509412483983162456)
XLA Ops:
  0.6 0.7 and_select_fusion
  1.3 0.0 copy-start
  1.3 0.9 copy-done
  2.3 0.0 copy-start.2
  2.3 1.6 copy-done.2
  3.9 4.0 %shard_map.50 = (bf16[4096,256]{1,0:T(8,128)(2,1)S(1)}, bf16[32,304,256]{2,1,0:T(8,128)(2,1)}) custom-call(s32[64]{0:T(128)S(1)} %get-tuple-element.77.first_ids.ids, s32[64]{0:T(128)S(1)} %get-tuple-element.76.second_ids, bf16[4096,256]{1,0:T(8,128)(2,1)S(1)} %copy-done.2, f32[16,4096]{1,0:T(8,128)S(1)} %copy-done), custom_call_target="tpu_custom_call" | custom-call | tf_op jit(solution)/shard_map/pallas_call | solution.py:250
  7.9 0.0 copy-start.1
  7.9 68.8 %all_to_all.40.got = bf16[32,304,256]{2,1,0:T(8,128)(2,1)} all-to-all(bf16[32,304,256]{2,1,0:T(8,128)(2,1)} %get-tuple-element.39), channel_id=1, replica_groups=mesh['wide'=32,'narrow'=4] {'wide'}, dimensions={0} | all-to-all | bytes 9961472 | tf_op jit(solution)/shard_map/all_to_all | solution.py:278
  76.8 1.1 slice.11
  77.8 0.1 convert_reduce_fusion
  77.9 0.1 reshape.8.ids
  78.0 0.0 copy-done.1
  78.0 16.6 %shard_map.51 = (f32[64,128,128]{2,1,0:T(8,128)}, f32[32,40,128]{2,1,0:T(8,128)S(1)}, f32[16,4096]{1,0:T(8,128)S(1)}) custom-call(s32[64]{0:T(128)S(1)} %reshape.8.ids, bf16[32,304,256]{2,1,0:T(8,128)(2,1)} %all_to_all.40.got, bf16[4096,256]{1,0:T(8,128)(2,1)S(1)} %get-tuple-element.40.unit, f32[16,4096]{1,0:T(8,128)S(1)} %copy-done.1), custom_call_target="tpu_custom_call" | custom-call | tf_op jit(solution)/shard_map/pallas_call | solution.py:303
  94.6 16.6 %all_to_all.41.got = f32[32,40,128]{2,1,0:T(8,128)S(1)} all-to-all(f32[32,40,128]{2,1,0:T(8,128)S(1)} %get-tuple-element.41), channel_id=1, replica_groups=mesh['wide'=32,'narrow'=4] {'wide'}, dimensions={0} | all-to-all | bytes 1310720 | tf_op jit(solution)/shard_map/all_to_all | solution.py:278
  111.2 0.9 shard_map.52
  112.0 2.8 collective-permute-start.2
  114.8 0.4 collective-permute-start.1
  115.2 0.7 collective-permute-start
  115.9 2.0 shard_map.53
  117.9 8.2 %collective-permute-done.2.t3 = f32[16,4096]{1,0:T(8,128)S(1)} collective-permute-done((f32[16,4096]{1,0:T(8,128)S(1)}, f32[16,4096]{1,0:T(8,128)S(1)}, u32[]{:S(2)}, u32[]{:S(2)}) %collective-permute-start.2) | collective-permute-done | bytes 262176 | tf_op jit(solution)/shard_map/ppermute | solution.py:318
  126.1 0.0 collective-permute-done.1.t2
  126.1 4.1 %collective-permute-done.t1 = f32[16,4096]{1,0:T(8,128)S(1)} collective-permute-done((f32[16,4096]{1,0:T(8,128)S(1)}, f32[16,4096]{1,0:T(8,128)S(1)}, u32[]{:S(2)}, u32[]{:S(2)}) %collective-permute-start) | collective-permute-done | bytes 262176 | tf_op jit(solution)/shard_map/ppermute | solution.py:318
  130.2 2.3 shard_map.54
  132.6 16.6 %all_to_all.42.got = f32[32,40,128]{2,1,0:T(8,128)S(1)} all-to-all(f32[32,40,128]{2,1,0:T(8,128)S(1)} %get-tuple-element.46), channel_id=1, replica_groups=mesh['wide'=32,'narrow'=4] {'wide'}, dimensions={0} | all-to-all | bytes 1310720 | tf_op jit(solution)/shard_map/all_to_all | solution.py:278
  149.1 8.8 %shard_map.55 = (f32[32,40,128]{2,1,0:T(8,128)S(1)}, f32[16,4096]{1,0:T(8,128)S(1)}, f32[16,4096]{1,0:T(8,128)S(1)}, f32[16,16]{1,0:T(8,128)S(1)}) custom-call(s32[64]{0:T(128)S(1)} %reshape.8.ids, f32[32,40,128]{2,1,0:T(8,128)S(1)} %all_to_all.42.got, f32[64,128,128]{2,1,0:T(8,128)} %get-tuple-element.47.tiles, f32[16,4096]{1,0:T(8,128)S(1)} %get-tuple-element.48.w0.y_old, ...), custom_call_target="tpu_custom_call" | custom-call | tf_op jit(solution)/shard_map/pallas_call | solution.py:331
  158.0 16.5 %all_to_all.43.got = f32[32,40,128]{2,1,0:T(8,128)S(1)} all-to-all(f32[32,40,128]{2,1,0:T(8,128)S(1)} %get-tuple-element.50), channel_id=1, replica_groups=mesh['wide'=32,'narrow'=4] {'wide'}, dimensions={0} | all-to-all | bytes 1310720 | tf_op jit(solution)/shard_map/all_to_all | solution.py:278
  174.5 0.9 shard_map.56
  175.3 0.4 collective-permute-start.5
  175.7 0.4 collective-permute-start.4
  176.1 0.8 collective-permute-start.3
  176.9 1.4 shard_map.57
  178.3 5.1 %collective-permute-done.5.t3 = f32[16,4096]{1,0:T(8,128)S(1)} collective-permute-done((f32[16,4096]{1,0:T(8,128)S(1)}, f32[16,4096]{1,0:T(8,128)S(1)}, u32[]{:S(2)}, u32[]{:S(2)}) %collective-permute-start.5) | collective-permute-done | bytes 262176 | tf_op jit(solution)/shard_map/ppermute | solution.py:318
  183.4 1.7 collective-permute-done.4.t2
  185.1 6.0 %collective-permute-done.3.t1 = f32[16,4096]{1,0:T(8,128)S(1)} collective-permute-done((f32[16,4096]{1,0:T(8,128)S(1)}, f32[16,4096]{1,0:T(8,128)S(1)}, u32[]{:S(2)}, u32[]{:S(2)}) %collective-permute-start.3) | collective-permute-done | bytes 262176 | tf_op jit(solution)/shard_map/ppermute | solution.py:318
  191.1 3.1 %shard_map.58 = (f32[16,4096]{1,0:T(8,128)S(1)}, f32[16,4096]{1,0:T(8,128)S(1)}, f32[16,4096]{1,0:T(8,128)S(1)}, f32[32,40,128]{2,1,0:T(8,128)S(1)}) custom-call(s32[64]{0:T(128)S(1)} %get-tuple-element.77.first_ids.ids, f32[16,4096]{1,0:T(8,128)S(1)} %get-tuple-element.52.t0, f32[16,4096]{1,0:T(8,128)S(1)} %collective-permute-done.3.t1, ...), custom_call_target="tpu_custom_call" | custom-call | tf_op jit(solution)/shard_map/pallas_call | solution.py:250
  194.2 16.6 %all_to_all.44.got = f32[32,40,128]{2,1,0:T(8,128)S(1)} all-to-all(f32[32,40,128]{2,1,0:T(8,128)S(1)} %get-tuple-element.58), channel_id=1, replica_groups=mesh['wide'=32,'narrow'=4] {'wide'}, dimensions={0} | all-to-all | bytes 1310720 | tf_op jit(solution)/shard_map/all_to_all | solution.py:278
  210.8 8.8 %shard_map.59 = (f32[32,40,128]{2,1,0:T(8,128)S(1)}, f32[16,4096]{1,0:T(8,128)S(1)}, f32[16,4096]{1,0:T(8,128)S(1)}, f32[16,16]{1,0:T(8,128)S(1)}) custom-call(s32[64]{0:T(128)S(1)} %reshape.8.ids, f32[32,40,128]{2,1,0:T(8,128)S(1)} %all_to_all.44.got, f32[64,128,128]{2,1,0:T(8,128)} %get-tuple-element.47.tiles, f32[16,4096]{1,0:T(8,128)S(1)} %get-tuple-element.59.w0, ...), custom_call_target="tpu_custom_call" | custom-call | tf_op jit(solution)/shard_map/pallas_call | solution.py:331
  219.6 16.5 %all_to_all.45.got = f32[32,40,128]{2,1,0:T(8,128)S(1)} all-to-all(f32[32,40,128]{2,1,0:T(8,128)S(1)} %get-tuple-element.61), channel_id=1, replica_groups=mesh['wide'=32,'narrow'=4] {'wide'}, dimensions={0} | all-to-all | bytes 1310720 | tf_op jit(solution)/shard_map/all_to_all | solution.py:278
  236.1 0.9 shard_map.60
  237.0 0.6 collective-permute-start.8
  237.6 0.1 collective-permute-start.7
  237.7 0.8 collective-permute-start.6
  238.5 1.4 shard_map.61
  239.9 5.1 %collective-permute-done.8.t3 = f32[16,4096]{1,0:T(8,128)S(1)} collective-permute-done((f32[16,4096]{1,0:T(8,128)S(1)}, f32[16,4096]{1,0:T(8,128)S(1)}, u32[]{:S(2)}, u32[]{:S(2)}) %collective-permute-start.8) | collective-permute-done | bytes 262176 | tf_op jit(solution)/shard_map/ppermute | solution.py:318
  245.1 1.9 collective-permute-done.7.t2
  247.0 6.0 %collective-permute-done.6.t1 = f32[16,4096]{1,0:T(8,128)S(1)} collective-permute-done((f32[16,4096]{1,0:T(8,128)S(1)}, f32[16,4096]{1,0:T(8,128)S(1)}, u32[]{:S(2)}, u32[]{:S(2)}) %collective-permute-start.6) | collective-permute-done | bytes 262176 | tf_op jit(solution)/shard_map/ppermute | solution.py:318
  253.0 2.9 %shard_map.62 = (f32[16,4096]{1,0:T(8,128)S(1)}, f32[16,4096]{1,0:T(8,128)S(1)}, f32[16,4096]{1,0:T(8,128)}, f32[32,8,128]{2,1,0:T(8,128)S(1)}) custom-call(s32[64]{0:T(128)S(1)} %get-tuple-element.77.first_ids.ids, f32[16,4096]{1,0:T(8,128)S(1)} %get-tuple-element.63.t0, f32[16,4096]{1,0:T(8,128)S(1)} %collective-permute-done.6.t1, ...), custom_call_target="tpu_custom_call" | custom-call | tf_op jit(solution)/shard_map/pallas_call | solution.py:250
  256.0 11.3 %all_to_all.46.got = f32[32,8,128]{2,1,0:T(8,128)S(1)} all-to-all(f32[32,8,128]{2,1,0:T(8,128)S(1)} %get-tuple-element.70), channel_id=1, replica_groups=mesh['wide'=32,'narrow'=4] {'wide'}, dimensions={0} | all-to-all | bytes 262144 | tf_op jit(solution)/shard_map/all_to_all | solution.py:278
  267.3 1.3 shard_map.63
  268.6 11.3 %all_to_all.47.got = f32[32,8,128]{2,1,0:T(8,128)S(1)} all-to-all(f32[32,8,128]{2,1,0:T(8,128)S(1)} %get-tuple-element.73), channel_id=1, replica_groups=mesh['wide'=32,'narrow'=4] {'wide'}, dimensions={0} | all-to-all | bytes 262144 | tf_op jit(solution)/shard_map/all_to_all | solution.py:278
  279.8 2.6 shard_map.64
  (1 shorter events, 0.0 us)
Async XLA Ops:
  1.3 0.9 copy-start
  2.3 1.6 copy-start.2
  7.9 70.1 %copy-start.1 = (f32[16,4096]{1,0:T(8,128)S(1)}, f32[16,4096]{1,0:T(8,128)}, u32[]{:S(2)}) copy-start(f32[16,4096]{1,0:T(8,128)} %q_init.1) | copy-start | bytes 786436
  112.0 14.1 %collective-permute-start.2 = (f32[16,4096]{1,0:T(8,128)S(1)}, f32[16,4096]{1,0:T(8,128)S(1)}, u32[]{:S(2)}, u32[]{:S(2)}) collective-permute-start(f32[16,4096]{1,0:T(8,128)S(1)} %get-tuple-element.43.t0), channel_id=1, source_target_pairs={{0,3},{1,0},{2,1},{3,2},{4,7},{5,4},{6,5},{7,6},{8,11},{9,8},{10,9... | collective-permute-start | bytes 786440 | tf_op jit(solution)/shard_map/ppermute | solution.py:318
  114.8 11.3 %collective-permute-start.1 = (f32[16,4096]{1,0:T(8,128)S(1)}, f32[16,4096]{1,0:T(8,128)S(1)}, u32[]{:S(2)}, u32[]{:S(2)}) collective-permute-start(f32[16,4096]{1,0:T(8,128)S(1)} %get-tuple-element.43.t0), channel_id=1, source_target_pairs={{0,2},{1,3},{2,0},{3,1},{4,6},{5,7},{6,4},{7,5},{8,10},{9,11},{10,... | collective-permute-start | bytes 786440 | tf_op jit(solution)/shard_map/ppermute | solution.py:318
  115.2 15.0 %collective-permute-start = (f32[16,4096]{1,0:T(8,128)S(1)}, f32[16,4096]{1,0:T(8,128)S(1)}, u32[]{:S(2)}, u32[]{:S(2)}) collective-permute-start(f32[16,4096]{1,0:T(8,128)S(1)} %get-tuple-element.43.t0), channel_id=1, source_target_pairs={{0,1},{1,2},{2,3},{3,0},{4,5},{5,6},{6,7},{7,4},{8,9},{9,10},{10,1... | collective-permute-start | bytes 786440 | tf_op jit(solution)/shard_map/ppermute | solution.py:318
  175.3 8.1 %collective-permute-start.5 = (f32[16,4096]{1,0:T(8,128)S(1)}, f32[16,4096]{1,0:T(8,128)S(1)}, u32[]{:S(2)}, u32[]{:S(2)}) collective-permute-start(f32[16,4096]{1,0:T(8,128)S(1)} %get-tuple-element.52.t0), channel_id=1, source_target_pairs={{0,3},{1,0},{2,1},{3,2},{4,7},{5,4},{6,5},{7,6},{8,11},{9,8},{10,9... | collective-permute-start | bytes 786440 | tf_op jit(solution)/shard_map/ppermute | solution.py:318
  175.7 9.4 %collective-permute-start.4 = (f32[16,4096]{1,0:T(8,128)S(1)}, f32[16,4096]{1,0:T(8,128)S(1)}, u32[]{:S(2)}, u32[]{:S(2)}) collective-permute-start(f32[16,4096]{1,0:T(8,128)S(1)} %get-tuple-element.52.t0), channel_id=1, source_target_pairs={{0,2},{1,3},{2,0},{3,1},{4,6},{5,7},{6,4},{7,5},{8,10},{9,11},{10,... | collective-permute-start | bytes 786440 | tf_op jit(solution)/shard_map/ppermute | solution.py:318
  176.1 15.0 %collective-permute-start.3 = (f32[16,4096]{1,0:T(8,128)S(1)}, f32[16,4096]{1,0:T(8,128)S(1)}, u32[]{:S(2)}, u32[]{:S(2)}) collective-permute-start(f32[16,4096]{1,0:T(8,128)S(1)} %get-tuple-element.52.t0), channel_id=1, source_target_pairs={{0,1},{1,2},{2,3},{3,0},{4,5},{5,6},{6,7},{7,4},{8,9},{9,10},{10,1... | collective-permute-start | bytes 786440 | tf_op jit(solution)/shard_map/ppermute | solution.py:318
  237.0 8.1 %collective-permute-start.8 = (f32[16,4096]{1,0:T(8,128)S(1)}, f32[16,4096]{1,0:T(8,128)S(1)}, u32[]{:S(2)}, u32[]{:S(2)}) collective-permute-start(f32[16,4096]{1,0:T(8,128)S(1)} %get-tuple-element.63.t0), channel_id=1, source_target_pairs={{0,3},{1,0},{2,1},{3,2},{4,7},{5,4},{6,5},{7,6},{8,11},{9,8},{10,9... | collective-permute-start | bytes 786440 | tf_op jit(solution)/shard_map/ppermute | solution.py:318
  237.6 9.4 %collective-permute-start.7 = (f32[16,4096]{1,0:T(8,128)S(1)}, f32[16,4096]{1,0:T(8,128)S(1)}, u32[]{:S(2)}, u32[]{:S(2)}) collective-permute-start(f32[16,4096]{1,0:T(8,128)S(1)} %get-tuple-element.63.t0), channel_id=1, source_target_pairs={{0,2},{1,3},{2,0},{3,1},{4,6},{5,7},{6,4},{7,5},{8,10},{9,11},{10,... | collective-permute-start | bytes 786440 | tf_op jit(solution)/shard_map/ppermute | solution.py:318
  237.7 15.3 %collective-permute-start.6 = (f32[16,4096]{1,0:T(8,128)S(1)}, f32[16,4096]{1,0:T(8,128)S(1)}, u32[]{:S(2)}, u32[]{:S(2)}) collective-permute-start(f32[16,4096]{1,0:T(8,128)S(1)} %get-tuple-element.63.t0), channel_id=1, source_target_pairs={{0,1},{1,2},{2,3},{3,0},{4,5},{5,6},{6,7},{7,4},{8,9},{9,10},{10,1... | collective-permute-start | bytes 786440 | tf_op jit(solution)/shard_map/ppermute | solution.py:318

commit v2 on v1

v2 whole, which is shorter than its diff:
```python
import functools

import jax
import jax.numpy as jnp
from jax import lax
from jax.experimental import pallas as pl
from jax.experimental.pallas import tpu as pltpu
from jax.sharding import PartitionSpec as P

BS = 128
STEPS = 3
KERNEL_FACTOR = 3.0
EPSILON = 1e-06
HIGH = lax.Precision.HIGHEST
VMEM_LIMIT = 40 * 2**20
TAIL = 8
CHUNKS = 8
BF = jnp.bfloat16
F32 = jnp.float32
NT = (((1,), (1,)), ((), ()))
TN = (((0,), (0,)), ((), ()))
NN = (((1,), (0,)), ((), ()))
cat = jnp.concatenate


def mm(a, b, dims):
    return lax.dot_general(a, b, dims, precision=HIGH, preferred_element_type=F32)


def mb(a, b, dims):
    return lax.dot_general(a, b, dims, preferred_element_type=F32)


def split(x):
    high = x.astype(BF)
    return high, (x - high.astype(F32)).astype(BF)


def block(i):
    return pl.ds(pl.multiple_of(i * BS, BS), BS)


def apply_small(m, x):
    rows = m.shape[0]
    m_high, m_low = split(m)
    left = cat([cat([m_high, m_high], axis=1), cat([m_low, jnp.zeros_like(m_low)], axis=1)], axis=0)
    out = mb(left, cat(split(x), axis=0), NN)
    return out[:rows] + out[rows:]


def factor_of(gram):
    n = gram.shape[0]
    rows = lax.broadcasted_iota(jnp.int32, (n, n), 0)
    cols = lax.broadcasted_iota(jnp.int32, (n, n), 1)
    low = jnp.zeros((n, n), F32)
    inverse = (rows == cols).astype(F32)
    left = gram
    for j in range(n):
        scale = 1.0 / jnp.sqrt(left[j : j + 1, j : j + 1])
        column = jnp.where(rows >= j, left[:, j : j + 1] * scale, 0.0)
        low = jnp.where(cols == j, column, low)
        line = inverse[j : j + 1, :] * scale
        below = jnp.where(rows > j, column, 0.0)
        left = left - below * (left[j : j + 1, :] * scale)
        inverse = jnp.where(rows == j, line, inverse - below * line)
    return low, inverse


def fold(q, w):
    n = q.shape[0]
    g = cat([q, w], axis=0)
    g = mm(g, g, NT)
    parts = (g[:n, :n], g[:n, n:], g[n:, n:])
    pieces = [p[h : h + 8] for p in parts for h in (0, 8)]
    return cat(pieces + [jnp.zeros((8, BS - 6 * n), F32)], axis=1)


def step_matrices(tails, points):
    t = jnp.sum(tails, axis=0) * (1.0 / points)
    s, a, b = (cat([t[:, 32 * k : 32 * k + 16], t[:, 32 * k + 16 : 32 * k + 32]], axis=0) for k in range(3))
    g = b - mm(a, a, TN) - mm(a, a, TN) + mm(a, mm(s, a, NN), TN)
    low, inverse = factor_of(g)
    return a, low, inverse, mm(inverse, a, NT)


def tile_stack(tile):
    return cat(split(tile), axis=0)


def pair_terms(stack, first, second):
    f_high, f_low = first
    s_high, s_low = second
    rows = f_high.shape[0]
    a = mb(cat([s_high, s_low], axis=0), stack, NT)
    to_first = a[:rows, :BS] + a[rows:, :BS] + a[:rows, BS:]
    left = cat([cat([f_high, f_high], axis=1), cat([f_low, jnp.zeros_like(f_low)], axis=1)], axis=0)
    b = mb(left, stack, NN)
    return to_first, b[:rows] + b[rows:]


def start_kernel(wide, cap, own_blocks, pairs, points, q_in, unit, out, raw, q, vec, meta, sems, sem):
    vec_rows = q.shape[0]
    slot_rows = BS + vec_rows
    size = raw.shape[0] // CHUNKS
    loads = [
        pltpu.make_async_copy(
            points.at[pl.ds(k * size, size), :], raw.at[pl.ds(k * size, size), :], sems.at[k]
        )
        for k in range(CHUNKS)
    ]
    loads.append(pltpu.make_async_copy(q_in, q, sems.at[CHUNKS]))
    for load in (loads[-1], *loads[:-1]):
        load.start()
    loads[-1].wait()
    gram = mm(q[...], q[...], NT)
    pieces = []
    for _ in range(3):
        pieces.append(gram.astype(BF).astype(F32))
        gram = gram - pieces[-1]
    sums = cat(pieces + [jnp.zeros((vec_rows, BS - 3 * vec_rows), F32)], axis=1)
    lanes = lax.broadcasted_iota(jnp.int32, sums.shape, 1)
    for b in range(own_blocks):
        vec[b] = cat(split(q[:, b * BS : (b + 1) * BS]), axis=1)

    def label(p, carry):
        ids = [lax.rem(pairs[1, p * cap + c], own_blocks).astype(F32) for c in range(cap)]
        left = jnp.where(lanes < BS // 2, sums, ids[0])
        meta[p] = cat([left, jnp.full(sums.shape, ids[1])], axis=1).astype(BF)
        return carry

    lax.fori_loop(0, wide, label, 0, unroll=4)
    for k in range(CHUNKS):
        loads[k].wait()
        for b in range(own_blocks // CHUNKS):
            rows = pl.ds(k * size + b * BS, BS)
            x = raw[rows, :].astype(F32)
            x = x * lax.rsqrt(jnp.sum(x * x, axis=-1, keepdims=True) + EPSILON)
            unit[rows, :] = x.astype(BF)

    def send(p, carry):
        for c in range(cap):
            i = lax.rem(pairs[0, p * cap + c], own_blocks)
            pltpu.make_async_copy(
                unit.at[block(i), :], out.at[p, pl.ds(c * slot_rows, BS), :], sem
            ).start()
            pltpu.make_async_copy(
                vec.at[i], out.at[p, pl.ds(c * slot_rows + BS, vec_rows), :], sem
            ).start()
        pltpu.make_async_copy(
            meta.at[p], out.at[p, pl.ds(cap * slot_rows, vec_rows), :], sem
        ).start()
        return carry

    lax.fori_loop(0, wide, send, 0)
    pltpu.make_async_copy(out, out, sem).wait()


def put_terms(terms, ids, cap, rows, back, total):
    for s, (to_first, to_second) in enumerate(terms):
        back[s // cap, (s % cap) * rows : (s % cap + 1) * rows, :] = to_first
        total[:, block(ids[s])] += to_second


def tiles_kernel(peers, cap, ids, got, unit, q, tiles, back, total, gram):
    step = pl.program_id(0)
    vec_rows = q.shape[0]
    slot_rows = BS + vec_rows
    slots = range(peers * cap)

    @pl.when(step == 0)
    def _():
        total[...] = jnp.zeros_like(total)
        gram[...] = jnp.zeros_like(gram)

    for p in range(peers):
        gram[...] += got[p, cap * slot_rows : cap * slot_rows + vec_rows, :BS].astype(F32)
    held = [ids[step * peers * cap + s] for s in slots]
    stacks = []
    for s in slots:
        at = (s % cap) * slot_rows
        inner = mb(got[s // cap, at : at + BS, :], unit[block(held[s]), :], NT)
        tile = jnp.exp(KERNEL_FACTOR * (inner - 1.0))
        tiles[s] = tile
        stacks.append(tile_stack(tile))
    terms = []
    for s in slots:
        rows = slice((s % cap) * slot_rows + BS, (s % cap + 1) * slot_rows)
        first = (got[s // cap, rows, :BS], got[s // cap, rows, BS:])
        terms.append(pair_terms(stacks[s], first, split(q[:, block(held[s])])))
    put_terms(terms, held, cap, vec_rows, back, total)


def terms_kernel(peers, cap, ids, got, tiles, w0, back, total):
    step = pl.program_id(0)
    vec_rows = w0.shape[0]

    @pl.when(step == 0)
    def _():
        total[...] = jnp.zeros_like(total)

    slots = range(peers * cap)
    held = [ids[step * peers * cap + s] for s in slots]
    terms = []
    for s in slots:
        first = got[step * peers + s // cap, pl.ds((s % cap) * vec_rows, vec_rows), :]
        second = w0[:, block(held[s])]
        terms.append(pair_terms(tile_stack(tiles[s]), split(first), split(second)))
    put_terms(terms, held, cap, vec_rows, back, total)


def sum_kernel(cap, own_blocks, pairs, got, total, out):
    vec_rows = total.shape[0]
    out[...] = total[...]

    def add(p, carry):
        for c in range(cap):
            i = lax.rem(pairs[0, p * cap + c], own_blocks)
            out[:, block(i)] += got[p, c * vec_rows : (c + 1) * vec_rows, :]
        return carry

    lax.fori_loop(0, got.shape[0], add, 0, unroll=4)


def first_factor_kernel(points, gram, matrix):
    g = gram[...]
    n = g.shape[0]
    _, inverse = factor_of((g[:, :n] + g[:, n : 2 * n] + g[:, 2 * n : 3 * n]) * (1.0 / points))
    none = jnp.zeros_like(inverse)
    matrix[...] = cat([cat([inverse, none], axis=1), cat([none, inverse], axis=1)], axis=0)


def factor_kernel(points, cap, last, got, matrix, along, low_out):
    n = along.shape[0]
    a, low, inverse, turned = step_matrices(got[:, cap * n :, :], points)
    along[...] = a
    low_out[...] = low
    none = jnp.zeros_like(low)
    across = mm(-low, (lax.broadcasted_iota(jnp.int32, (n, n), 0) == lax.broadcasted_iota(jnp.int32, (n, n), 1)).astype(F32), TN)
    lines = [cat([inverse, -turned, none, none], axis=1)]
    if not last:
        lines.append(cat([none, none, inverse, -turned], axis=1))
    lines.append(cat([none, across, inverse, -turned], axis=1))
    matrix[...] = cat(lines, axis=0)


def update_kernel(cap, own_blocks, old, pairs, t0, t1, t2, t3, *refs):
    given, matrix, outs, out = refs[:old], refs[old], refs[old + 1 : -1], refs[-1]
    image = (t0[...] + t2[...]) + (t1[...] + t3[...])
    rows = [r[...] for r in given]
    rows.insert(2 if old > 1 else 1, image)
    new = apply_small(matrix[...], cat(rows, axis=0))
    n = image.shape[0]
    for k, ref in enumerate(outs):
        ref[...] = new[k * n : (k + 1) * n]
    q, w0 = outs[0], outs[-1]
    tail = fold(new[:n], new[-n:])
    if not cap:
        out[...] = jnp.broadcast_to(tail[None], out.shape)
        return

    def put(p, carry):
        for c in range(cap):
            i = lax.rem(pairs[0, p * cap + c], own_blocks)
            out[p, c * n : (c + 1) * n, :] = w0[:, block(i)]
        out[p, cap * n :, :] = tail
        return carry

    lax.fori_loop(0, out.shape[0], put, 0, unroll=4)


def finish_kernel(points, got, w0, q, a0, l0, a1, l1, basis, coeffs):
    a, low, inverse, turned = step_matrices(got[...], points)
    basis[...] = apply_small(cat([inverse, -turned], axis=1), cat([w0[...], q[...]], axis=0))
    for k, m in enumerate((a0[...], l0[...], a1[...], l1[...], a, low)):
        coeffs[k // 2, k % 2] = m


def call(kernel, outs, n_ids=0, **more):
    params = pltpu.CompilerParams(vmem_limit_bytes=VMEM_LIMIT)
    shapes = tuple(jax.ShapeDtypeStruct(s, d) for s, d in outs)
    if "grid" in more:
        return pl.pallas_call(
            kernel,
            out_shape=shapes,
            grid_spec=pltpu.PrefetchScalarGridSpec(num_scalar_prefetch=n_ids, **more),
            compiler_params=params,
        )

    def run(*args):
        given = dict(more)
        vmem = pl.BlockSpec(memory_space=pltpu.VMEM)
        places = [pl.BlockSpec(memory_space=pltpu.SMEM)] * n_ids + [vmem] * (len(args) - n_ids)
        given.setdefault("in_specs", places)
        given.setdefault("out_specs", (vmem,) * len(outs))
        return pl.pallas_call(kernel, out_shape=shapes, compiler_params=params, **given)(*args)

    return run


def per_device(points, q_init, pairs):
    wide = lax.axis_size("wide")
    narrow = lax.axis_size("narrow")
    own_points, width = points.shape
    own_blocks = own_points // BS
    vec_rows = q_init.shape[0]
    pair_count = pairs.shape[1]
    cap = pair_count // wide
    total_points = own_points * wide
    slot_rows = BS + vec_rows
    start_rows = cap * slot_rows + vec_rows
    peers = min(8, wide)
    vectors = ((vec_rows, own_points), F32)
    small = ((vec_rows, vec_rows), F32)
    payload = ((wide, cap * vec_rows + TAIL, BS), F32)
    reply = ((wide, cap * vec_rows, BS), F32)
    tail = ((wide, TAIL, BS), F32)

    def exchange(x):
        return lax.all_to_all(x, "wide", split_axis=0, concat_axis=0, tiled=True)

    anywhere = pl.BlockSpec(memory_space=pl.ANY)
    unit, sent = call(
        functools.partial(start_kernel, wide, cap, own_blocks),
        [((own_points, width), BF), ((wide, start_rows, width), BF)],
        1,
        in_specs=[pl.BlockSpec(memory_space=pltpu.SMEM), anywhere, anywhere],
        out_specs=(pl.BlockSpec(memory_space=pltpu.VMEM), anywhere),
        scratch_shapes=[
            pltpu.VMEM((own_points, width), BF),
            pltpu.VMEM((vec_rows, own_points), F32),
            pltpu.VMEM((own_blocks, vec_rows, 2 * BS), BF),
            pltpu.VMEM((wide, vec_rows, width), BF),
            pltpu.SemaphoreType.DMA((CHUNKS + 1,)),
            pltpu.SemaphoreType.DMA,
        ],
    )(pairs, points, q_init)
    got = exchange(sent)
    labels = got[:, cap * slot_rows, BS // 2 : BS // 2 * (cap + 1) : BS // 2]
    ids = labels.astype(jnp.int32).reshape(pair_count)

    def whole(shape):
        return pl.BlockSpec(shape, lambda i, *_: (0,) * len(shape))

    def part(shape):
        return pl.BlockSpec(shape, lambda i, *_: (i,) + (0,) * (len(shape) - 1))

    tile_part = part((peers * cap, BS, BS))
    back_part = part((peers, cap * vec_rows, BS))
    tiles, back, total, gram = call(
        functools.partial(tiles_kernel, peers, cap),
        [((pair_count, BS, BS), F32), reply, vectors, ((vec_rows, BS), F32)],
        1,
        grid=(wide // peers,),
        in_specs=[part((peers, start_rows, width)), whole(unit.shape), whole(q_init.shape)],
        out_specs=(tile_part, back_part, whole(q_init.shape), whole((vec_rows, BS))),
    )(ids, got, unit, q_init)

    def narrow_terms(back, total):
        (total,) = call(functools.partial(sum_kernel, cap, own_blocks), [vectors], 1)(
            pairs, exchange(back), total
        )
        return (total,) + tuple(
            lax.ppermute(total, "narrow", [(i, (i + s) % narrow) for i in range(narrow)])
            for s in range(1, narrow)
        )

    sums = narrow_terms(back, total)
    (matrix,) = call(
        functools.partial(first_factor_kernel, total_points), [((2 * vec_rows, 2 * vec_rows), F32)]
    )(gram)
    q, w0, out = call(
        functools.partial(update_kernel, cap, own_blocks, 1), [vectors, vectors, payload], 1
    )(pairs, *sums, q_init, matrix)
    y = w0
    records = []
    for step in range(1, STEPS):
        last = step == STEPS - 1
        got = exchange(out)
        back, total = call(
            functools.partial(terms_kernel, peers, cap),
            [reply, vectors],
            1,
            grid=(wide // peers,),
            in_specs=[whole(payload[0]), tile_part, whole(q_init.shape)],
            out_specs=(back_part, whole(q_init.shape)),
        )(ids, got, tiles, w0)
        sums = narrow_terms(back, total)
        count = 2 if last else 3
        matrix, along, low = call(
            functools.partial(factor_kernel, total_points, cap, last),
            [((count * vec_rows, 4 * vec_rows), F32), small, small],
        )(got)
        *new, out = call(
            functools.partial(update_kernel, 0 if last else cap, own_blocks, 3),
            [vectors] * count + [tail if last else payload],
            1,
        )(pairs, *sums, w0, q, y, matrix)
        q, y, w0 = new[0], new[1], new[-1]
        records += [along, low]
    return call(
        functools.partial(finish_kernel, total_points),
        [vectors, ((STEPS, 2, vec_rows, vec_rows), F32)],
    )(exchange(out), w0, q, *records)


def solution(mesh):
    placed = (P("wide", None), P(None, "wide"), P(None, ("wide", "narrow")))
    return jax.shard_map(
        per_device, mesh=mesh, in_specs=placed, out_specs=(P(None, "wide"), P()), check_vma=False
    )
```

time: 283 us -> 248 us (0.88)
  Pallas kernels: 58 us -> 36.8 us
  blocking collectives: 174 us -> 159 us
  local copies, waits for them, and re-layouts: 3.7 us -> 6.79 us
    all_to_all x8 -> x7, blocking collectives: 174 us -> 159 us  [exchange(): return lax.all_to_all(x, 'wide', split_axis=0, concat_axis=0, tiled=True)]
    pallas_call x1, Pallas kernels: 16.6 us -> 4.05 us  [per_device(): call(functools.partial(tiles_kernel, peers, cap), [((pair_count, BS, BS),...]
    pallas_call x14 -> x13, Pallas kernels: 41.4 us -> 32.8 us  [the longest x11 27.1 us: run(): pl.pallas_call(kernel, out_shape=shapes, compiler_params=params, **given)]
    unnamed x6 -> x12, local copies, waits for them, and re-layouts: 2.54 us -> 5.63 us
where the time goes in v2:
time: 248 us; the launch traced here: 247 us
  blocking collectives  159 us (64%)
  waiting for transfers between devices  37.1 us (15%)
  Pallas kernels  36.8 us (15%)
  starting transfers between devices  6.97 us (3%)
  local copies, waits for them, and re-layouts  6.79 us (3%)
    all_to_all x7, blocking collectives, exchange(): return lax.all_to_all(x, 'wide', split_axis=0, concat_axis=0, tiled=True)  159 us
    ppermute x9, waiting for transfers between devices, narrow_terms(): lax.ppermute(total, 'narrow', [(i, (i + s) % narrow) for i in range(narro...  37.1 us
    pallas_call x11, Pallas kernels, run(): pl.pallas_call(kernel, out_shape=shapes, compiler_params=params, **given)  27.1 us
    ppermute x9, starting transfers between devices, narrow_terms(): lax.ppermute(total, 'narrow', [(i, (i + s) % narrow) for i in range(narro...  6.97 us
    pallas_call x2, Pallas kernels, per_device(): call(functools.partial(terms_kernel, peers, cap), [reply, vectors], 1, gr...  5.66 us
    unnamed x12, local copies, waits for them, and re-layouts  5.63 us
  transfers between devices with their start and end apart: 9, of which 8 were waited for; matrix products, arithmetic and copies ran while one was open for 0% of the time, Pallas kernels for 2%

profile of v2, /device:TPU:1, one launch (start us, length us, event | category | flops | bytes accessed | tf_op | source)
XLA Modules:
  0.0 247.0 jit_solution(13637027127521180896)
XLA Ops:
  0.6 0.0 copy-start.1
  0.6 0.9 copy-done.1
  1.6 0.0 copy-start.3
  1.6 1.6 copy-done.3
  3.2 0.0 copy-start.4
  3.2 0.7 copy-done.4
  3.9 10.0 %shard_map.50 = (bf16[4096,256]{1,0:T(8,128)(2,1)S(1)}, bf16[32,304,256]{2,1,0:T(8,128)(2,1)S(1)}) custom-call(s32[2,64]{1,0:T(2,128)S(1)} %copy-done.4, bf16[4096,256]{1,0:T(8,128)(2,1)S(1)} %copy-done.3, f32[16,4096]{1,0:T(8,128)S(1)} %copy-done.1), custom_call_target="tpu_custom_call" | custom-call | tf_op jit(solution)/shard_map/pallas_call | solution.py:295
  13.8 0.0 copy-start.2
  13.8 68.6 %all_to_all.35.got = bf16[32,304,256]{2,1,0:T(8,128)(2,1)} all-to-all(bf16[32,304,256]{2,1,0:T(8,128)(2,1)S(1)} %get-tuple-element.28), channel_id=1, replica_groups=mesh['wide'=32,'narrow'=4] {'wide'}, dimensions={0} | all-to-all | bytes 9961472 | tf_op jit(solution)/shard_map/all_to_all | solution.py:319
  82.5 1.1 slice.3
  83.5 0.1 convert_reduce_fusion
  83.6 0.1 reshape.8.ids
  83.7 0.0 copy-done.2
  83.7 0.0 copy-start
  83.7 2.4 copy-done
  86.1 0.0 copy-start.5
  86.1 4.0 %shard_map.51 = (f32[64,128,128]{2,1,0:T(8,128)S(1)}, f32[32,32,128]{2,1,0:T(8,128)S(1)}, f32[16,4096]{1,0:T(8,128)S(1)}, f32[16,128]{1,0:T(8,128)S(1)}) custom-call(s32[64]{0:T(128)S(1)} %reshape.8.ids, bf16[32,304,256]{2,1,0:T(8,128)(2,1)S(1)} %copy-done, bf16[4096,256]{1,0:T(8,128)(2,1)S(1)} %get-tuple-element.29.unit, f32[16,4096]{1,0:T(8,128)S(1)} %copy-done.2), custom_call_target="tpu_custom_call" | custom-call | tf_op jit(solution)/shard_map/pallas_call | solution.py:349
  90.2 15.3 %all_to_all.36.got = f32[32,32,128]{2,1,0:T(8,128)S(1)} all-to-all(f32[32,32,128]{2,1,0:T(8,128)S(1)} %get-tuple-element.30), channel_id=1, replica_groups=mesh['wide'=32,'narrow'=4] {'wide'}, dimensions={0} | all-to-all | bytes 1048576 | tf_op jit(solution)/shard_map/all_to_all | solution.py:319
  105.4 0.0 copy-done.5
  105.4 0.9 shard_map.52.t0
  106.3 2.8 %collective-permute-start.2 = (f32[16,4096]{1,0:T(8,128)S(1)}, f32[16,4096]{1,0:T(8,128)S(1)}, u32[]{:S(2)}, u32[]{:S(2)}) collective-permute-start(f32[16,4096]{1,0:T(8,128)S(1)} %shard_map.52.t0), channel_id=1, source_target_pairs={{0,3},{1,0},{2,1},{3,2},{4,7},{5,4},{6,5},{7,6},{8,11},{9,8},{10,9... | collective-permute-start | bytes 786440 | tf_op jit(solution)/shard_map/ppermute | solution.py:363
  109.1 0.4 collective-permute-start.1
  109.5 0.7 collective-permute-start
  110.2 1.6 shard_map.53.refs_1_
  111.7 8.7 %collective-permute-done.2.t3 = f32[16,4096]{1,0:T(8,128)S(1)} collective-permute-done((f32[16,4096]{1,0:T(8,128)S(1)}, f32[16,4096]{1,0:T(8,128)S(1)}, u32[]{:S(2)}, u32[]{:S(2)}) %collective-permute-start.2) | collective-permute-done | bytes 262176 | tf_op jit(solution)/shard_map/ppermute | solution.py:363
  120.5 0.0 collective-permute-done.1.t2
  120.5 4.0 %collective-permute-done.t1 = f32[16,4096]{1,0:T(8,128)S(1)} collective-permute-done((f32[16,4096]{1,0:T(8,128)S(1)}, f32[16,4096]{1,0:T(8,128)S(1)}, u32[]{:S(2)}, u32[]{:S(2)}) %collective-permute-start) | collective-permute-done | bytes 262176 | tf_op jit(solution)/shard_map/ppermute | solution.py:363
  124.5 1.8 shard_map.54
  126.3 16.6 %all_to_all.37.got = f32[32,40,128]{2,1,0:T(8,128)S(1)} all-to-all(f32[32,40,128]{2,1,0:T(8,128)S(1)} %get-tuple-element.33), channel_id=1, replica_groups=mesh['wide'=32,'narrow'=4] {'wide'}, dimensions={0} | all-to-all | bytes 1310720 | tf_op jit(solution)/shard_map/all_to_all | solution.py:319
  142.9 2.8 %shard_map.55 = (f32[32,32,128]{2,1,0:T(8,128)S(1)}, f32[16,4096]{1,0:T(8,128)S(1)}) custom-call(s32[64]{0:T(128)S(1)} %reshape.8.ids, f32[32,40,128]{2,1,0:T(8,128)S(1)} %all_to_all.37.got, f32[64,128,128]{2,1,0:T(8,128)S(1)} %get-tuple-element.34.tiles, f32[16,4096]{1,0:T(8,128)S(1)} %get-tuple-element.35.w0.refs_0_.refs_2_), custom_call_target="tpu_custom_call" | custom-call | tf_op jit(solution)/shard_map/pallas_call | solution.py:379
  145.7 15.1 %all_to_all.38.got = f32[32,32,128]{2,1,0:T(8,128)S(1)} all-to-all(f32[32,32,128]{2,1,0:T(8,128)S(1)} %get-tuple-element.36), channel_id=1, replica_groups=mesh['wide'=32,'narrow'=4] {'wide'}, dimensions={0} | all-to-all | bytes 1048576 | tf_op jit(solution)/shard_map/all_to_all | solution.py:319
  160.8 0.9 shard_map.56.t0
  161.7 0.4 collective-permute-start.5
  162.1 0.4 collective-permute-start.4
  162.5 0.8 collective-permute-start.3
  163.3 2.2 shard_map.57
  165.5 4.4 %collective-permute-done.5.t3 = f32[16,4096]{1,0:T(8,128)S(1)} collective-permute-done((f32[16,4096]{1,0:T(8,128)S(1)}, f32[16,4096]{1,0:T(8,128)S(1)}, u32[]{:S(2)}, u32[]{:S(2)}) %collective-permute-start.5) | collective-permute-done | bytes 262176 | tf_op jit(solution)/shard_map/ppermute | solution.py:363
  169.9 1.7 collective-permute-done.4.t2
  171.6 6.0 %collective-permute-done.3.t1 = f32[16,4096]{1,0:T(8,128)S(1)} collective-permute-done((f32[16,4096]{1,0:T(8,128)S(1)}, f32[16,4096]{1,0:T(8,128)S(1)}, u32[]{:S(2)}, u32[]{:S(2)}) %collective-permute-start.3) | collective-permute-done | bytes 262176 | tf_op jit(solution)/shard_map/ppermute | solution.py:363
  177.6 1.9 shard_map.58
  179.4 16.5 %all_to_all.39.got = f32[32,40,128]{2,1,0:T(8,128)S(1)} all-to-all(f32[32,40,128]{2,1,0:T(8,128)S(1)} %get-tuple-element.40), channel_id=1, replica_groups=mesh['wide'=32,'narrow'=4] {'wide'}, dimensions={0} | all-to-all | bytes 1310720 | tf_op jit(solution)/shard_map/all_to_all | solution.py:319
  196.0 2.8 %shard_map.59 = (f32[32,32,128]{2,1,0:T(8,128)S(1)}, f32[16,4096]{1,0:T(8,128)S(1)}) custom-call(s32[64]{0:T(128)S(1)} %reshape.8.ids, f32[32,40,128]{2,1,0:T(8,128)S(1)} %all_to_all.39.got, f32[64,128,128]{2,1,0:T(8,128)S(1)} %get-tuple-element.34.tiles, f32[16,4096]{1,0:T(8,128)S(1)} %get-tuple-element.41.w0.refs_0_), custom_call_target="tpu_custom_call" | custom-call | tf_op jit(solution)/shard_map/pallas_call | solution.py:379
  198.8 15.1 %all_to_all.40.got = f32[32,32,128]{2,1,0:T(8,128)S(1)} all-to-all(f32[32,32,128]{2,1,0:T(8,128)S(1)} %get-tuple-element.42), channel_id=1, replica_groups=mesh['wide'=32,'narrow'=4] {'wide'}, dimensions={0} | all-to-all | bytes 1048576 | tf_op jit(solution)/shard_map/all_to_all | solution.py:319
  214.0 0.9 shard_map.60.t0
  214.8 0.6 collective-permute-start.8
  215.5 0.1 collective-permute-start.7
  215.6 0.8 collective-permute-start.6
  216.4 2.2 shard_map.61
  218.6 4.4 %collective-permute-done.8.t3 = f32[16,4096]{1,0:T(8,128)S(1)} collective-permute-done((f32[16,4096]{1,0:T(8,128)S(1)}, f32[16,4096]{1,0:T(8,128)S(1)}, u32[]{:S(2)}, u32[]{:S(2)}) %collective-permute-start.8) | collective-permute-done | bytes 262176 | tf_op jit(solution)/shard_map/ppermute | solution.py:363
  223.0 1.9 collective-permute-done.7.t2
  224.9 6.0 %collective-permute-done.6.t1 = f32[16,4096]{1,0:T(8,128)S(1)} collective-permute-done((f32[16,4096]{1,0:T(8,128)S(1)}, f32[16,4096]{1,0:T(8,128)S(1)}, u32[]{:S(2)}, u32[]{:S(2)}) %collective-permute-start.6) | collective-permute-done | bytes 262176 | tf_op jit(solution)/shard_map/ppermute | solution.py:363
  230.9 1.6 shard_map.62
  232.5 11.3 %all_to_all.41.got = f32[32,8,128]{2,1,0:T(8,128)S(1)} all-to-all(f32[32,8,128]{2,1,0:T(8,128)S(1)} %get-tuple-element.47), channel_id=1, replica_groups=mesh['wide'=32,'narrow'=4] {'wide'}, dimensions={0} | all-to-all | bytes 262144 | tf_op jit(solution)/shard_map/all_to_all | solution.py:319
  243.8 3.2 %shard_map.63 = (f32[16,4096]{1,0:T(8,128)}, f32[3,2,16,16]{3,2,1,0:T(8,128)}) custom-call(f32[32,8,128]{2,1,0:T(8,128)S(1)} %all_to_all.41.got, f32[16,4096]{1,0:T(8,128)S(1)} %get-tuple-element.48.w0, f32[16,4096]{1,0:T(8,128)S(1)} %get-tuple-element.49.q, f32[16,16]{1,0:T(8,128)S(1)} %get-tuple-element.50.a0, f32[16,16]{1,0:T(8,128)S(1)} %get-tuple-element.51.l0, ...), custom_call_target="tpu_custom_call" | custom-call | tf_op jit(solution)/shard_map/pallas_call | solution.py:295
Async XLA Ops:
  0.6 1.0 copy-start.1
  1.6 1.6 copy-start.3
  3.2 0.7 copy-start.4
  13.8 69.9 %copy-start.2 = (f32[16,4096]{1,0:T(8,128)S(1)}, f32[16,4096]{1,0:T(8,128)}, u32[]{:S(2)}) copy-start(f32[16,4096]{1,0:T(8,128)} %refs_0_.1) | copy-start | bytes 786436
  83.7 2.4 copy-start
  86.1 19.3 %copy-start.5 = (s32[2,64]{1,0:T(2,128)S(1)}, s32[2,64]{1,0:T(2,128)}, u32[]{:S(2)}) copy-start(s32[2,64]{1,0:T(2,128)} %pairs.13) | copy-start | bytes 1540
  106.3 14.1 %collective-permute-start.2 = (f32[16,4096]{1,0:T(8,128)S(1)}, f32[16,4096]{1,0:T(8,128)S(1)}, u32[]{:S(2)}, u32[]{:S(2)}) collective-permute-start(f32[16,4096]{1,0:T(8,128)S(1)} %shard_map.52.t0), channel_id=1, source_target_pairs={{0,3},{1,0},{2,1},{3,2},{4,7},{5,4},{6,5},{7,6},{8,11},{9,8},{10,9... | collective-permute-start | bytes 786440 | tf_op jit(solution)/shard_map/ppermute | solution.py:363
  109.1 11.3 %collective-permute-start.1 = (f32[16,4096]{1,0:T(8,128)S(1)}, f32[16,4096]{1,0:T(8,128)S(1)}, u32[]{:S(2)}, u32[]{:S(2)}) collective-permute-start(f32[16,4096]{1,0:T(8,128)S(1)} %shard_map.52.t0), channel_id=1, source_target_pairs={{0,2},{1,3},{2,0},{3,1},{4,6},{5,7},{6,4},{7,5},{8,10},{9,11},{10,... | collective-permute-start | bytes 786440 | tf_op jit(solution)/shard_map/ppermute | solution.py:363
  109.5 15.0 %collective-permute-start = (f32[16,4096]{1,0:T(8,128)S(1)}, f32[16,4096]{1,0:T(8,128)S(1)}, u32[]{:S(2)}, u32[]{:S(2)}) collective-permute-start(f32[16,4096]{1,0:T(8,128)S(1)} %shard_map.52.t0), channel_id=1, source_target_pairs={{0,1},{1,2},{2,3},{3,0},{4,5},{5,6},{6,7},{7,4},{8,9},{9,10},{10,1... | collective-permute-start | bytes 786440 | tf_op jit(solution)/shard_map/ppermute | solution.py:363
  161.7 8.1 %collective-permute-start.5 = (f32[16,4096]{1,0:T(8,128)S(1)}, f32[16,4096]{1,0:T(8,128)S(1)}, u32[]{:S(2)}, u32[]{:S(2)}) collective-permute-start(f32[16,4096]{1,0:T(8,128)S(1)} %shard_map.56.t0), channel_id=1, source_target_pairs={{0,3},{1,0},{2,1},{3,2},{4,7},{5,4},{6,5},{7,6},{8,11},{9,8},{10,9... | collective-permute-start | bytes 786440 | tf_op jit(solution)/shard_map/ppermute | solution.py:363
  162.1 9.4 %collective-permute-start.4 = (f32[16,4096]{1,0:T(8,128)S(1)}, f32[16,4096]{1,0:T(8,128)S(1)}, u32[]{:S(2)}, u32[]{:S(2)}) collective-permute-start(f32[16,4096]{1,0:T(8,128)S(1)} %shard_map.56.t0), channel_id=1, source_target_pairs={{0,2},{1,3},{2,0},{3,1},{4,6},{5,7},{6,4},{7,5},{8,10},{9,11},{10,... | collective-permute-start | bytes 786440 | tf_op jit(solution)/shard_map/ppermute | solution.py:363
  162.5 15.1 %collective-permute-start.3 = (f32[16,4096]{1,0:T(8,128)S(1)}, f32[16,4096]{1,0:T(8,128)S(1)}, u32[]{:S(2)}, u32[]{:S(2)}) collective-permute-start(f32[16,4096]{1,0:T(8,128)S(1)} %shard_map.56.t0), channel_id=1, source_target_pairs={{0,1},{1,2},{2,3},{3,0},{4,5},{5,6},{6,7},{7,4},{8,9},{9,10},{10,1... | collective-permute-start | bytes 786440 | tf_op jit(solution)/shard_map/ppermute | solution.py:363
  214.8 8.1 %collective-permute-start.8 = (f32[16,4096]{1,0:T(8,128)S(1)}, f32[16,4096]{1,0:T(8,128)S(1)}, u32[]{:S(2)}, u32[]{:S(2)}) collective-permute-start(f32[16,4096]{1,0:T(8,128)S(1)} %shard_map.60.t0), channel_id=1, source_target_pairs={{0,3},{1,0},{2,1},{3,2},{4,7},{5,4},{6,5},{7,6},{8,11},{9,8},{10,9... | collective-permute-start | bytes 786440 | tf_op jit(solution)/shard_map/ppermute | solution.py:363
  215.5 9.4 %collective-permute-start.7 = (f32[16,4096]{1,0:T(8,128)S(1)}, f32[16,4096]{1,0:T(8,128)S(1)}, u32[]{:S(2)}, u32[]{:S(2)}) collective-permute-start(f32[16,4096]{1,0:T(8,128)S(1)} %shard_map.60.t0), channel_id=1, source_target_pairs={{0,2},{1,3},{2,0},{3,1},{4,6},{5,7},{6,4},{7,5},{8,10},{9,11},{10,... | collective-permute-start | bytes 786440 | tf_op jit(solution)/shard_map/ppermute | solution.py:363
  215.6 15.3 %collective-permute-start.6 = (f32[16,4096]{1,0:T(8,128)S(1)}, f32[16,4096]{1,0:T(8,128)S(1)}, u32[]{:S(2)}, u32[]{:S(2)}) collective-permute-start(f32[16,4096]{1,0:T(8,128)S(1)} %shard_map.60.t0), channel_id=1, source_target_pairs={{0,1},{1,2},{2,3},{3,0},{4,5},{5,6},{6,7},{7,4},{8,9},{9,10},{10,1... | collective-permute-start | bytes 786440 | tf_op jit(solution)/shard_map/ppermute | solution.py:363

commit v3 on v2

--- a/solution.py
+++ b/solution.py
@@ -12,7 +12,8 @@
 KERNEL_FACTOR = 3.0
 EPSILON = 1e-06
 HIGH = lax.Precision.HIGHEST
-VMEM_LIMIT = 40 * 2**20
+VMEM_LIMIT = 16 * 2**20
+VMEM_START = 60 * 2**20
 TAIL = 8
 CHUNKS = 8
 BF = jnp.bfloat16
@@ -109,26 +110,9 @@
         for k in range(CHUNKS)
     ]
     loads.append(pltpu.make_async_copy(q_in, q, sems.at[CHUNKS]))
-    for load in (loads[-1], *loads[:-1]):
+    for load in loads:
         load.start()
-    loads[-1].wait()
-    gram = mm(q[...], q[...], NT)
-    pieces = []
-    for _ in range(3):
-        pieces.append(gram.astype(BF).astype(F32))
-        gram = gram - pieces[-1]
-    sums = cat(pieces + [jnp.zeros((vec_rows, BS - 3 * vec_rows), F32)], axis=1)
-    lanes = lax.broadcasted_iota(jnp.int32, sums.shape, 1)
-    for b in range(own_blocks):
-        vec[b] = cat(split(q[:, b * BS : (b + 1) * BS]), axis=1)
-
-    def label(p, carry):
-        ids = [lax.rem(pairs[1, p * cap + c], own_blocks).astype(F32) for c in range(cap)]
-        left = jnp.where(lanes < BS // 2, sums, ids[0])
-        meta[p] = cat([left, jnp.full(sums.shape, ids[1])], axis=1).astype(BF)
-        return carry
-
-    lax.fori_loop(0, wide, label, 0, unroll=4)
+
     for k in range(CHUNKS):
         loads[k].wait()
         for b in range(own_blocks // CHUNKS):
@@ -143,6 +127,30 @@
             pltpu.make_async_copy(
                 unit.at[block(i), :], out.at[p, pl.ds(c * slot_rows, BS), :], sem
             ).start()
+        return carry
+
+    lax.fori_loop(0, wide, send, 0, unroll=4)
+    loads[-1].wait()
+    high, low = split(q[...])
+    for b in range(own_blocks):
+        cols = slice(b * BS, (b + 1) * BS)
+        vec[b] = cat([high[:, cols], low[:, cols]], axis=1)
+    both = cat([high, low], axis=0)
+    gram = mb(both, both, NT)
+    gram = gram[:vec_rows, :vec_rows] + (gram[:vec_rows, vec_rows:] + gram[vec_rows:, :vec_rows])
+    pieces = []
+    for _ in range(3):
+        pieces.append(gram.astype(BF).astype(F32))
+        gram = gram - pieces[-1]
+    sums = cat(pieces + [jnp.zeros((vec_rows, BS - 3 * vec_rows), F32)], axis=1)
+    lanes = lax.broadcasted_iota(jnp.int32, sums.shape, 1)
+
+    def label(p, carry):
+        ids = [lax.rem(pairs[1, p * cap + c], own_blocks).astype(F32) for c in range(cap)]
+        left = jnp.where(lanes < BS // 2, sums, ids[0])
+        meta[p] = cat([left, jnp.full(sums.shape, ids[1])], axis=1).astype(BF)
+        for c in range(cap):
+            i = lax.rem(pairs[0, p * cap + c], own_blocks)
             pltpu.make_async_copy(
                 vec.at[i], out.at[p, pl.ds(c * slot_rows + BS, vec_rows), :], sem
             ).start()
@@ -151,7 +159,7 @@
         ).start()
         return carry
 
-    lax.fori_loop(0, wide, send, 0)
+    lax.fori_loop(0, wide, label, 0, unroll=4)
     pltpu.make_async_copy(out, out, sem).wait()
 
 
@@ -275,8 +283,8 @@
         coeffs[k // 2, k % 2] = m
 
 
-def call(kernel, outs, n_ids=0, **more):
-    params = pltpu.CompilerParams(vmem_limit_bytes=VMEM_LIMIT)
+def call(kernel, outs, n_ids=0, limit=VMEM_LIMIT, **more):
+    params = pltpu.CompilerParams(vmem_limit_bytes=limit)
     shapes = tuple(jax.ShapeDtypeStruct(s, d) for s, d in outs)
     if "grid" in more:
         return pl.pallas_call(
@@ -323,6 +331,7 @@
         functools.partial(start_kernel, wide, cap, own_blocks),
         [((own_points, width), BF), ((wide, start_rows, width), BF)],
         1,
+        VMEM_START,
         in_specs=[pl.BlockSpec(memory_space=pltpu.SMEM), anywhere, anywhere],
         out_specs=(pl.BlockSpec(memory_space=pltpu.VMEM), anywhere),
         scratch_shapes=[

time: 248 us -> 241 us (0.972)
  Pallas kernels: 36.8 us -> 33.4 us
  local copies, waits for them, and re-layouts: 6.79 us -> 3.58 us
    pallas_call x11, Pallas kernels: 27.1 us -> 23.7 us  [run(): pl.pallas_call(kernel, out_shape=shapes, compiler_params=params, **given)]
    unnamed x12 -> x8, local copies, waits for them, and re-layouts: 5.63 us -> 2.42 us
where the time goes in v3:
time: 241 us
  blocking collectives  159 us (66%)
  waiting for transfers between devices  37.1 us (15%)
  Pallas kernels  33.4 us (14%)
  starting transfers between devices  6.97 us (3%)
  local copies, waits for them, and re-layouts  3.58 us (1%)
    all_to_all x7, blocking collectives, exchange(): return lax.all_to_all(x, 'wide', split_axis=0, concat_axis=0, tiled=True)  159 us
    ppermute x9, waiting for transfers between devices, narrow_terms(): lax.ppermute(total, 'narrow', [(i, (i + s) % narrow) for i in range(narro...  37.1 us
    pallas_call x11, Pallas kernels, run(): pl.pallas_call(kernel, out_shape=shapes, compiler_params=params, **given)  23.7 us
    ppermute x9, starting transfers between devices, narrow_terms(): lax.ppermute(total, 'narrow', [(i, (i + s) % narrow) for i in range(narro...  6.97 us
    pallas_call x2, Pallas kernels, per_device(): call(functools.partial(terms_kernel, peers, cap), [reply, vectors], 1, gr...  5.66 us
  transfers between devices with their start and end apart: 9, of which 8 were waited for; matrix products, arithmetic and copies ran while one was open for 0% of the time, Pallas kernels for 2%

profile of v3, /device:TPU:1, one launch (start us, length us, event | category | flops | bytes accessed | tf_op | source)
XLA Modules:
  0.0 240.6 jit_solution(773014054307622484)
XLA Ops:
  0.6 6.5 %shard_map.50 = (bf16[4096,256]{1,0:T(8,128)(2,1)}, bf16[32,304,256]{2,1,0:T(8,128)(2,1)}) custom-call(s32[2,64]{1,0:T(2,128)} %pairs.13, bf16[4096,256]{1,0:T(8,128)(2,1)} %points.1, f32[16,4096]{1,0:T(8,128)} %refs_0_.1), custom_call_target="tpu_custom_call" | custom-call | tf_op jit(solution)/shard_map/pallas_call | solution.py:303
  7.2 0.0 copy-start.1
  7.2 0.0 copy-start.2
  7.2 68.8 %all_to_all.35.got = bf16[32,304,256]{2,1,0:T(8,128)(2,1)} all-to-all(bf16[32,304,256]{2,1,0:T(8,128)(2,1)} %get-tuple-element.28), channel_id=1, replica_groups=mesh['wide'=32,'narrow'=4] {'wide'}, dimensions={0} | all-to-all | bytes 9961472 | tf_op jit(solution)/shard_map/all_to_all | solution.py:327
  76.0 1.1 slice.3
  77.1 0.1 convert_reduce_fusion
  77.2 0.1 reshape.8.ids
  77.3 0.0 copy-done.1
  77.3 0.0 copy-done.2
  77.3 0.0 copy-start
  77.3 2.4 copy-done
  79.7 0.0 copy-start.3
  79.7 4.0 %shard_map.51 = (f32[64,128,128]{2,1,0:T(8,128)S(1)}, f32[32,32,128]{2,1,0:T(8,128)S(1)}, f32[16,4096]{1,0:T(8,128)S(1)}, f32[16,128]{1,0:T(8,128)S(1)}) custom-call(s32[64]{0:T(128)S(1)} %reshape.8.ids, bf16[32,304,256]{2,1,0:T(8,128)(2,1)S(1)} %copy-done, bf16[4096,256]{1,0:T(8,128)(2,1)S(1)} %copy-done.2, f32[16,4096]{1,0:T(8,128)S(1)} %copy-done.1), custom_call_target="tpu_custom_call" | custom-call | tf_op jit(solution)/shard_map/pallas_call | solution.py:358
  83.8 15.3 %all_to_all.36.got = f32[32,32,128]{2,1,0:T(8,128)S(1)} all-to-all(f32[32,32,128]{2,1,0:T(8,128)S(1)} %get-tuple-element.30), channel_id=1, replica_groups=mesh['wide'=32,'narrow'=4] {'wide'}, dimensions={0} | all-to-all | bytes 1048576 | tf_op jit(solution)/shard_map/all_to_all | solution.py:327
  99.0 0.0 copy-done.3
  99.0 0.9 shard_map.52.t0
  99.9 2.8 %collective-permute-start.2 = (f32[16,4096]{1,0:T(8,128)S(1)}, f32[16,4096]{1,0:T(8,128)S(1)}, u32[]{:S(2)}, u32[]{:S(2)}) collective-permute-start(f32[16,4096]{1,0:T(8,128)S(1)} %shard_map.52.t0), channel_id=1, source_target_pairs={{0,3},{1,0},{2,1},{3,2},{4,7},{5,4},{6,5},{7,6},{8,11},{9,8},{10,9... | collective-permute-start | bytes 786440 | tf_op jit(solution)/shard_map/ppermute | solution.py:372
  102.7 0.4 collective-permute-start.1
  103.1 0.7 collective-permute-start
  103.8 1.6 shard_map.53.refs_1_
  105.3 8.7 %collective-permute-done.2.t3 = f32[16,4096]{1,0:T(8,128)S(1)} collective-permute-done((f32[16,4096]{1,0:T(8,128)S(1)}, f32[16,4096]{1,0:T(8,128)S(1)}, u32[]{:S(2)}, u32[]{:S(2)}) %collective-permute-start.2) | collective-permute-done | bytes 262176 | tf_op jit(solution)/shard_map/ppermute | solution.py:372
  114.0 0.0 collective-permute-done.1.t2
  114.0 4.0 %collective-permute-done.t1 = f32[16,4096]{1,0:T(8,128)S(1)} collective-permute-done((f32[16,4096]{1,0:T(8,128)S(1)}, f32[16,4096]{1,0:T(8,128)S(1)}, u32[]{:S(2)}, u32[]{:S(2)}) %collective-permute-start) | collective-permute-done | bytes 262176 | tf_op jit(solution)/shard_map/ppermute | solution.py:372
  118.1 1.8 shard_map.54
  119.9 16.6 %all_to_all.37.got = f32[32,40,128]{2,1,0:T(8,128)S(1)} all-to-all(f32[32,40,128]{2,1,0:T(8,128)S(1)} %get-tuple-element.33), channel_id=1, replica_groups=mesh['wide'=32,'narrow'=4] {'wide'}, dimensions={0} | all-to-all | bytes 1310720 | tf_op jit(solution)/shard_map/all_to_all | solution.py:327
  136.5 2.8 %shard_map.55 = (f32[32,32,128]{2,1,0:T(8,128)S(1)}, f32[16,4096]{1,0:T(8,128)S(1)}) custom-call(s32[64]{0:T(128)S(1)} %reshape.8.ids, f32[32,40,128]{2,1,0:T(8,128)S(1)} %all_to_all.37.got, f32[64,128,128]{2,1,0:T(8,128)S(1)} %get-tuple-element.34.tiles, f32[16,4096]{1,0:T(8,128)S(1)} %get-tuple-element.35.w0.refs_0_.refs_2_), custom_call_target="tpu_custom_call" | custom-call | tf_op jit(solution)/shard_map/pallas_call | solution.py:388
  139.3 15.1 %all_to_all.38.got = f32[32,32,128]{2,1,0:T(8,128)S(1)} all-to-all(f32[32,32,128]{2,1,0:T(8,128)S(1)} %get-tuple-element.36), channel_id=1, replica_groups=mesh['wide'=32,'narrow'=4] {'wide'}, dimensions={0} | all-to-all | bytes 1048576 | tf_op jit(solution)/shard_map/all_to_all | solution.py:327
  154.4 0.9 shard_map.56.t0
  155.3 0.4 collective-permute-start.5
  155.7 0.4 collective-permute-start.4
  156.1 0.8 collective-permute-start.3
  156.9 2.2 shard_map.57
  159.1 4.4 %collective-permute-done.5.t3 = f32[16,4096]{1,0:T(8,128)S(1)} collective-permute-done((f32[16,4096]{1,0:T(8,128)S(1)}, f32[16,4096]{1,0:T(8,128)S(1)}, u32[]{:S(2)}, u32[]{:S(2)}) %collective-permute-start.5) | collective-permute-done | bytes 262176 | tf_op jit(solution)/shard_map/ppermute | solution.py:372
  163.5 1.7 collective-permute-done.4.t2
  165.1 6.0 %collective-permute-done.3.t1 = f32[16,4096]{1,0:T(8,128)S(1)} collective-permute-done((f32[16,4096]{1,0:T(8,128)S(1)}, f32[16,4096]{1,0:T(8,128)S(1)}, u32[]{:S(2)}, u32[]{:S(2)}) %collective-permute-start.3) | collective-permute-done | bytes 262176 | tf_op jit(solution)/shard_map/ppermute | solution.py:372
  171.1 1.9 shard_map.58
  173.0 16.5 %all_to_all.39.got = f32[32,40,128]{2,1,0:T(8,128)S(1)} all-to-all(f32[32,40,128]{2,1,0:T(8,128)S(1)} %get-tuple-element.40), channel_id=1, replica_groups=mesh['wide'=32,'narrow'=4] {'wide'}, dimensions={0} | all-to-all | bytes 1310720 | tf_op jit(solution)/shard_map/all_to_all | solution.py:327
  189.6 2.8 %shard_map.59 = (f32[32,32,128]{2,1,0:T(8,128)S(1)}, f32[16,4096]{1,0:T(8,128)S(1)}) custom-call(s32[64]{0:T(128)S(1)} %reshape.8.ids, f32[32,40,128]{2,1,0:T(8,128)S(1)} %all_to_all.39.got, f32[64,128,128]{2,1,0:T(8,128)S(1)} %get-tuple-element.34.tiles, f32[16,4096]{1,0:T(8,128)S(1)} %get-tuple-element.41.w0.refs_0_), custom_call_target="tpu_custom_call" | custom-call | tf_op jit(solution)/shard_map/pallas_call | solution.py:388
  192.4 15.1 %all_to_all.40.got = f32[32,32,128]{2,1,0:T(8,128)S(1)} all-to-all(f32[32,32,128]{2,1,0:T(8,128)S(1)} %get-tuple-element.42), channel_id=1, replica_groups=mesh['wide'=32,'narrow'=4] {'wide'}, dimensions={0} | all-to-all | bytes 1048576 | tf_op jit(solution)/shard_map/all_to_all | solution.py:327
  207.5 0.9 shard_map.60.t0
  208.4 0.6 collective-permute-start.8
  209.1 0.1 collective-permute-start.7
  209.2 0.8 collective-permute-start.6
  210.0 2.2 shard_map.61
  212.2 4.4 %collective-permute-done.8.t3 = f32[16,4096]{1,0:T(8,128)S(1)} collective-permute-done((f32[16,4096]{1,0:T(8,128)S(1)}, f32[16,4096]{1,0:T(8,128)S(1)}, u32[]{:S(2)}, u32[]{:S(2)}) %collective-permute-start.8) | collective-permute-done | bytes 262176 | tf_op jit(solution)/shard_map/ppermute | solution.py:372
  216.6 1.9 collective-permute-done.7.t2
  218.5 6.0 %collective-permute-done.6.t1 = f32[16,4096]{1,0:T(8,128)S(1)} collective-permute-done((f32[16,4096]{1,0:T(8,128)S(1)}, f32[16,4096]{1,0:T(8,128)S(1)}, u32[]{:S(2)}, u32[]{:S(2)}) %collective-permute-start.6) | collective-permute-done | bytes 262176 | tf_op jit(solution)/shard_map/ppermute | solution.py:372
  224.5 1.6 shard_map.62
  226.1 11.3 %all_to_all.41.got = f32[32,8,128]{2,1,0:T(8,128)S(1)} all-to-all(f32[32,8,128]{2,1,0:T(8,128)S(1)} %get-tuple-element.47), channel_id=1, replica_groups=mesh['wide'=32,'narrow'=4] {'wide'}, dimensions={0} | all-to-all | bytes 262144 | tf_op jit(solution)/shard_map/all_to_all | solution.py:327
  237.4 3.2 %shard_map.63 = (f32[16,4096]{1,0:T(8,128)}, f32[3,2,16,16]{3,2,1,0:T(8,128)}) custom-call(f32[32,8,128]{2,1,0:T(8,128)S(1)} %all_to_all.41.got, f32[16,4096]{1,0:T(8,128)S(1)} %get-tuple-element.48.w0, f32[16,4096]{1,0:T(8,128)S(1)} %get-tuple-element.49.q, f32[16,16]{1,0:T(8,128)S(1)} %get-tuple-element.50.a0, f32[16,16]{1,0:T(8,128)S(1)} %get-tuple-element.51.l0, ...), custom_call_target="tpu_custom_call" | custom-call | tf_op jit(solution)/shard_map/pallas_call | solution.py:303
Async XLA Ops:
  7.2 70.1 %copy-start.1 = (f32[16,4096]{1,0:T(8,128)S(1)}, f32[16,4096]{1,0:T(8,128)}, u32[]{:S(2)}) copy-start(f32[16,4096]{1,0:T(8,128)} %refs_0_.1) | copy-start | bytes 786436
  7.2 70.1 %copy-start.2 = (bf16[4096,256]{1,0:T(8,128)(2,1)S(1)}, bf16[4096,256]{1,0:T(8,128)(2,1)}, u32[]{:S(2)}) copy-start(bf16[4096,256]{1,0:T(8,128)(2,1)} %get-tuple-element.29.unit) | copy-start | bytes 6291460
  77.3 2.4 %copy-start = (bf16[32,304,256]{2,1,0:T(8,128)(2,1)S(1)}, bf16[32,304,256]{2,1,0:T(8,128)(2,1)}, u32[]{:S(2)}) copy-start(bf16[32,304,256]{2,1,0:T(8,128)(2,1)} %all_to_all.35.got) | copy-start | bytes 14942212
  79.7 19.3 %copy-start.3 = (s32[2,64]{1,0:T(2,128)S(1)}, s32[2,64]{1,0:T(2,128)}, u32[]{:S(2)}) copy-start(s32[2,64]{1,0:T(2,128)} %pairs.13) | copy-start | bytes 1540
  99.9 14.1 %collective-permute-start.2 = (f32[16,4096]{1,0:T(8,128)S(1)}, f32[16,4096]{1,0:T(8,128)S(1)}, u32[]{:S(2)}, u32[]{:S(2)}) collective-permute-start(f32[16,4096]{1,0:T(8,128)S(1)} %shard_map.52.t0), channel_id=1, source_target_pairs={{0,3},{1,0},{2,1},{3,2},{4,7},{5,4},{6,5},{7,6},{8,11},{9,8},{10,9... | collective-permute-start | bytes 786440 | tf_op jit(solution)/shard_map/ppermute | solution.py:372
  102.7 11.3 %collective-permute-start.1 = (f32[16,4096]{1,0:T(8,128)S(1)}, f32[16,4096]{1,0:T(8,128)S(1)}, u32[]{:S(2)}, u32[]{:S(2)}) collective-permute-start(f32[16,4096]{1,0:T(8,128)S(1)} %shard_map.52.t0), channel_id=1, source_target_pairs={{0,2},{1,3},{2,0},{3,1},{4,6},{5,7},{6,4},{7,5},{8,10},{9,11},{10,... | collective-permute-start | bytes 786440 | tf_op jit(solution)/shard_map/ppermute | solution.py:372
  103.1 15.0 %collective-permute-start = (f32[16,4096]{1,0:T(8,128)S(1)}, f32[16,4096]{1,0:T(8,128)S(1)}, u32[]{:S(2)}, u32[]{:S(2)}) collective-permute-start(f32[16,4096]{1,0:T(8,128)S(1)} %shard_map.52.t0), channel_id=1, source_target_pairs={{0,1},{1,2},{2,3},{3,0},{4,5},{5,6},{6,7},{7,4},{8,9},{9,10},{10,1... | collective-permute-start | bytes 786440 | tf_op jit(solution)/shard_map/ppermute | solution.py:372
  155.3 8.1 %collective-permute-start.5 = (f32[16,4096]{1,0:T(8,128)S(1)}, f32[16,4096]{1,0:T(8,128)S(1)}, u32[]{:S(2)}, u32[]{:S(2)}) collective-permute-start(f32[16,4096]{1,0:T(8,128)S(1)} %shard_map.56.t0), channel_id=1, source_target_pairs={{0,3},{1,0},{2,1},{3,2},{4,7},{5,4},{6,5},{7,6},{8,11},{9,8},{10,9... | collective-permute-start | bytes 786440 | tf_op jit(solution)/shard_map/ppermute | solution.py:372
  155.7 9.4 %collective-permute-start.4 = (f32[16,4096]{1,0:T(8,128)S(1)}, f32[16,4096]{1,0:T(8,128)S(1)}, u32[]{:S(2)}, u32[]{:S(2)}) collective-permute-start(f32[16,4096]{1,0:T(8,128)S(1)} %shard_map.56.t0), channel_id=1, source_target_pairs={{0,2},{1,3},{2,0},{3,1},{4,6},{5,7},{6,4},{7,5},{8,10},{9,11},{10,... | collective-permute-start | bytes 786440 | tf_op jit(solution)/shard_map/ppermute | solution.py:372
  156.1 15.0 %collective-permute-start.3 = (f32[16,4096]{1,0:T(8,128)S(1)}, f32[16,4096]{1,0:T(8,128)S(1)}, u32[]{:S(2)}, u32[]{:S(2)}) collective-permute-start(f32[16,4096]{1,0:T(8,128)S(1)} %shard_map.56.t0), channel_id=1, source_target_pairs={{0,1},{1,2},{2,3},{3,0},{4,5},{5,6},{6,7},{7,4},{8,9},{9,10},{10,1... | collective-permute-start | bytes 786440 | tf_op jit(solution)/shard_map/ppermute | solution.py:372
  208.4 8.1 %collective-permute-start.8 = (f32[16,4096]{1,0:T(8,128)S(1)}, f32[16,4096]{1,0:T(8,128)S(1)}, u32[]{:S(2)}, u32[]{:S(2)}) collective-permute-start(f32[16,4096]{1,0:T(8,128)S(1)} %shard_map.60.t0), channel_id=1, source_target_pairs={{0,3},{1,0},{2,1},{3,2},{4,7},{5,4},{6,5},{7,6},{8,11},{9,8},{10,9... | collective-permute-start | bytes 786440 | tf_op jit(solution)/shard_map/ppermute | solution.py:372
  209.1 9.4 %collective-permute-start.7 = (f32[16,4096]{1,0:T(8,128)S(1)}, f32[16,4096]{1,0:T(8,128)S(1)}, u32[]{:S(2)}, u32[]{:S(2)}) collective-permute-start(f32[16,4096]{1,0:T(8,128)S(1)} %shard_map.60.t0), channel_id=1, source_target_pairs={{0,2},{1,3},{2,0},{3,1},{4,6},{5,7},{6,4},{7,5},{8,10},{9,11},{10,... | collective-permute-start | bytes 786440 | tf_op jit(solution)/shard_map/ppermute | solution.py:372
  209.2 15.3 %collective-permute-start.6 = (f32[16,4096]{1,0:T(8,128)S(1)}, f32[16,4096]{1,0:T(8,128)S(1)}, u32[]{:S(2)}, u32[]{:S(2)}) collective-permute-start(f32[16,4096]{1,0:T(8,128)S(1)} %shard_map.60.t0), channel_id=1, source_target_pairs={{0,1},{1,2},{2,3},{3,0},{4,5},{5,6},{6,7},{7,4},{8,9},{9,10},{10,1... | collective-permute-start | bytes 786440 | tf_op jit(solution)/shard_map/ppermute | solution.py:372

commit v4 on v3

--- a/solution.py
+++ b/solution.py
@@ -14,6 +14,7 @@
 HIGH = lax.Precision.HIGHEST
 VMEM_LIMIT = 16 * 2**20
 VMEM_START = 60 * 2**20
+VMEM_TILES = 30 * 2**20
 TAIL = 8
 CHUNKS = 8
 BF = jnp.bfloat16
@@ -53,24 +54,25 @@
     n = gram.shape[0]
     rows = lax.broadcasted_iota(jnp.int32, (n, n), 0)
     cols = lax.broadcasted_iota(jnp.int32, (n, n), 1)
-    low = jnp.zeros((n, n), F32)
-    inverse = (rows == cols).astype(F32)
-    left = gram
+    same = (rows == cols).astype(F32)
+    low, inverse, left = same, same, gram
+    across, down = jnp.ones((1, n), F32), jnp.ones((n, 1), F32)
     for j in range(n):
-        scale = 1.0 / jnp.sqrt(left[j : j + 1, j : j + 1])
-        column = jnp.where(rows >= j, left[:, j : j + 1] * scale, 0.0)
-        low = jnp.where(cols == j, column, low)
-        line = inverse[j : j + 1, :] * scale
-        below = jnp.where(rows > j, column, 0.0)
-        left = left - below * (left[j : j + 1, :] * scale)
-        inverse = jnp.where(rows == j, line, inverse - below * line)
-    return low, inverse
+        pivot = left[j : j + 1, j : j + 1]
+        column = jnp.where(rows > j, left[:, j : j + 1] * (1.0 / pivot), 0.0)
+        left = left - column * left[j : j + 1, :]
+        inverse = inverse - column * inverse[j : j + 1, :]
+        low = jnp.where(cols == j, low + column, low)
+        across = jnp.where(cols[:1] == j, pivot, across)
+        down = jnp.where(rows[:, :1] == j, pivot, down)
+    return low * jnp.sqrt(across), inverse * (1.0 / jnp.sqrt(down))
 
 
 def fold(q, w):
     n = q.shape[0]
-    g = cat([q, w], axis=0)
-    g = mm(g, g, NT)
+    both = cat(split(cat([q, w], axis=0)), axis=0)
+    g = mb(both, both, NT)
+    g = g[: 2 * n, : 2 * n] + (g[: 2 * n, 2 * n :] + g[2 * n :, : 2 * n])
     parts = (g[:n, :n], g[:n, n:], g[n:, n:])
     pieces = [p[h : h + 8] for p in parts for h in (0, 8)]
     return cat(pieces + [jnp.zeros((8, BS - 6 * n), F32)], axis=1)
@@ -79,7 +81,7 @@
 def step_matrices(tails, points):
     t = jnp.sum(tails, axis=0) * (1.0 / points)
     s, a, b = (cat([t[:, 32 * k : 32 * k + 16], t[:, 32 * k + 16 : 32 * k + 32]], axis=0) for k in range(3))
-    g = b - mm(a, a, TN) - mm(a, a, TN) + mm(a, mm(s, a, NN), TN)
+    g = b - mm(a, 2.0 * a - mm(s, a, NN), TN)
     low, inverse = factor_of(g)
     return a, low, inverse, mm(inverse, a, NT)
 
@@ -163,57 +165,72 @@
     pltpu.make_async_copy(out, out, sem).wait()
 
 
-def put_terms(terms, ids, cap, rows, back, total):
+def put_terms(terms, ids, first_slot, cap, rows, back, total):
     for s, (to_first, to_second) in enumerate(terms):
-        back[s // cap, (s % cap) * rows : (s % cap + 1) * rows, :] = to_first
+        back[(first_slot + s) // cap, (s % cap) * rows : (s % cap + 1) * rows, :] = to_first
         total[:, block(ids[s])] += to_second
 
 
-def tiles_kernel(peers, cap, ids, got, unit, q, tiles, back, total, gram):
-    step = pl.program_id(0)
+def tiles_kernel(peers, cap, sent, unit, q, tiles, back, total, gram, ids, got, sems):
+    wide = got.shape[0]
     vec_rows = q.shape[0]
     slot_rows = BS + vec_rows
     slots = range(peers * cap)
 
-    @pl.when(step == 0)
-    def _():
-        total[...] = jnp.zeros_like(total)
-        gram[...] = jnp.zeros_like(gram)
-
-    for p in range(peers):
-        gram[...] += got[p, cap * slot_rows : cap * slot_rows + vec_rows, :BS].astype(F32)
-    held = [ids[step * peers * cap + s] for s in slots]
-    stacks = []
-    for s in slots:
-        at = (s % cap) * slot_rows
-        inner = mb(got[s // cap, at : at + BS, :], unit[block(held[s]), :], NT)
-        tile = jnp.exp(KERNEL_FACTOR * (inner - 1.0))
-        tiles[s] = tile
-        stacks.append(tile_stack(tile))
-    terms = []
-    for s in slots:
-        rows = slice((s % cap) * slot_rows + BS, (s % cap + 1) * slot_rows)
-        first = (got[s // cap, rows, :BS], got[s // cap, rows, BS:])
-        terms.append(pair_terms(stacks[s], first, split(q[:, block(held[s])])))
-    put_terms(terms, held, cap, vec_rows, back, total)
+    def load(k):
+        part = pl.ds(k * peers, peers)
+        return pltpu.make_async_copy(sent.at[part], got.at[part], sems.at[k])
+
+    for k in range(wide // peers):
+        load(k).start()
+    total[...] = jnp.zeros_like(total)
+    gram[...] = jnp.zeros_like(gram)
+
+    def chunk(k, carry):
+        load(k).wait()
+        peer = k * peers
+        held = []
+        for p in range(peers):
+            label = got[peer + p, pl.ds(cap * slot_rows, vec_rows), :].astype(F32)
+            gram[...] += label[:, :BS]
+            for c in range(cap):
+                j = label[0, (c + 1) * (BS // 2)].astype(jnp.int32)
+                ids[(peer + p) * cap + c] = j
+                held.append(j)
+        stacks = []
+        for s in slots:
+            rows = pl.ds((s % cap) * slot_rows, BS)
+            inner = mb(got[peer + s // cap, rows, :], unit[block(held[s]), :], NT)
+            stacks.append(tile_stack(jnp.exp(KERNEL_FACTOR * (inner - 1.0))))
+            tiles[peer * cap + s] = stacks[s]
+        terms = []
+        for s in slots:
+            rows = pl.ds((s % cap) * slot_rows + BS, vec_rows)
+            first = (got[peer + s // cap, rows, :BS], got[peer + s // cap, rows, BS:])
+            terms.append(pair_terms(stacks[s], first, split(q[:, block(held[s])])))
+        put_terms(terms, held, peer * cap, cap, vec_rows, back, total)
+        return carry
+
+    lax.fori_loop(0, wide // peers, chunk, 0)
 
 
 def terms_kernel(peers, cap, ids, got, tiles, w0, back, total):
-    step = pl.program_id(0)
     vec_rows = w0.shape[0]
-
-    @pl.when(step == 0)
-    def _():
-        total[...] = jnp.zeros_like(total)
-
     slots = range(peers * cap)
-    held = [ids[step * peers * cap + s] for s in slots]
-    terms = []
-    for s in slots:
-        first = got[step * peers + s // cap, pl.ds((s % cap) * vec_rows, vec_rows), :]
-        second = w0[:, block(held[s])]
-        terms.append(pair_terms(tile_stack(tiles[s]), split(first), split(second)))
-    put_terms(terms, held, cap, vec_rows, back, total)
+    total[...] = jnp.zeros_like(total)
+
+    def chunk(k, carry):
+        peer = k * peers
+        held = [ids[peer * cap + s] for s in slots]
+        terms = []
+        for s in slots:
+            first = got[peer + s // cap, pl.ds((s % cap) * vec_rows, vec_rows), :]
+            second = w0[:, block(held[s])]
+            terms.append(pair_terms(tiles[peer * cap + s], split(first), split(second)))
+        put_terms(terms, held, peer * cap, cap, vec_rows, back, total)
+        return carry
+
+    lax.fori_loop(0, got.shape[0] // peers, chunk, 0)
 
 
 def sum_kernel(cap, own_blocks, pairs, got, total, out):
@@ -286,14 +303,6 @@
 def call(kernel, outs, n_ids=0, limit=VMEM_LIMIT, **more):
     params = pltpu.CompilerParams(vmem_limit_bytes=limit)
     shapes = tuple(jax.ShapeDtypeStruct(s, d) for s, d in outs)
-    if "grid" in more:
-        return pl.pallas_call(
-            kernel,
-            out_shape=shapes,
-            grid_spec=pltpu.PrefetchScalarGridSpec(num_scalar_prefetch=n_ids, **more),
-            compiler_params=params,
-        )
-
     def run(*args):
         given = dict(more)
         vmem = pl.BlockSpec(memory_space=pltpu.VMEM)
@@ -343,26 +352,25 @@
             pltpu.SemaphoreType.DMA,
         ],
     )(pairs, points, q_init)
-    got = exchange(sent)
-    labels = got[:, cap * slot_rows, BS // 2 : BS // 2 * (cap + 1) : BS // 2]
-    ids = labels.astype(jnp.int32).reshape(pair_count)
-
-    def whole(shape):
-        return pl.BlockSpec(shape, lambda i, *_: (0,) * len(shape))
-
-    def part(shape):
-        return pl.BlockSpec(shape, lambda i, *_: (i,) + (0,) * (len(shape) - 1))
-
-    tile_part = part((peers * cap, BS, BS))
-    back_part = part((peers, cap * vec_rows, BS))
-    tiles, back, total, gram = call(
+    vmem = pl.BlockSpec(memory_space=pltpu.VMEM)
+    tiles, back, total, gram, ids = call(
         functools.partial(tiles_kernel, peers, cap),
-        [((pair_count, BS, BS), F32), reply, vectors, ((vec_rows, BS), F32)],
-        1,
-        grid=(wide // peers,),
-        in_specs=[part((peers, start_rows, width)), whole(unit.shape), whole(q_init.shape)],
-        out_specs=(tile_part, back_part, whole(q_init.shape), whole((vec_rows, BS))),
-    )(ids, got, unit, q_init)
+        [
+            ((pair_count, 2 * BS, BS), BF),
+            reply,
+            vectors,
+            ((vec_rows, BS), F32),
+            ((pair_count,), jnp.int32),
+        ],
+        0,
+        VMEM_TILES,
+        in_specs=[anywhere, vmem, vmem],
+        out_specs=(vmem, vmem, vmem, vmem, pl.BlockSpec(memory_space=pltpu.SMEM)),
+        scratch_shapes=[
+            pltpu.VMEM((wide, start_rows, width), BF),
+            pltpu.SemaphoreType.DMA((wide // peers,)),
+        ],
+    )(exchange(sent), unit, q_init)
 
     def narrow_terms(back, total):
         (total,) = call(functools.partial(sum_kernel, cap, own_blocks), [vectors], 1)(
@@ -386,12 +394,7 @@
         last = step == STEPS - 1
         got = exchange(out)
         back, total = call(
-            functools.partial(terms_kernel, peers, cap),
-            [reply, vectors],
-            1,
-            grid=(wide // peers,),
-            in_specs=[whole(payload[0]), tile_part, whole(q_init.shape)],
-            out_specs=(back_part, whole(q_init.shape)),
+            functools.partial(terms_kernel, 2 * peers, cap), [reply, vectors], 1
         )(ids, got, tiles, w0)
         sums = narrow_terms(back, total)
         count = 2 if last else 3

time: 241 us -> 238 us (0.988)
  local copies, waits for them, and re-layouts: 3.58 us -> 0.01 us
    pallas_call x11 -> x14, Pallas kernels: 23.7 us -> 33.8 us  [run(): pl.pallas_call(kernel, out_shape=shapes, compiler_params=params, **given)]
    pallas_call x3 -> x0, Pallas kernels: 9.71 us -> none  [the longest x2 5.66 us: per_device(): call(functools.partial(terms_kernel, peers, cap), [reply, vectors], 1, gr...]
where the time goes in v4:
time: 238 us; the launch traced here: 237 us
  blocking collectives  159 us (67%)
  waiting for transfers between devices  37.1 us (16%)
  Pallas kernels  33.8 us (14%)
  starting transfers between devices  6.98 us (3%)
    all_to_all x7, blocking collectives, exchange(): return lax.all_to_all(x, 'wide', split_axis=0, concat_axis=0, tiled=True)  159 us
    ppermute x9, waiting for transfers between devices, narrow_terms(): lax.ppermute(total, 'narrow', [(i, (i + s) % narrow) for i in range(narro...  37.1 us
    pallas_call x14, Pallas kernels, run(): pl.pallas_call(kernel, out_shape=shapes, compiler_params=params, **given)  33.8 us
    ppermute x9, starting transfers between devices, narrow_terms(): lax.ppermute(total, 'narrow', [(i, (i + s) % narrow) for i in range(narro...  6.98 us
  transfers between devices with their start and end apart: 9, of which 8 were waited for; matrix products, arithmetic and copies ran while one was open for 0% of the time, Pallas kernels for 2%

profile of v4, /device:TPU:1, one launch (start us, length us, event | category | flops | bytes accessed | tf_op | source)
XLA Modules:
  0.0 237.3 jit_solution(8102015673422486750)
XLA Ops:
  0.6 6.6 %shard_map.50 = (bf16[4096,256]{1,0:T(8,128)(2,1)}, bf16[32,304,256]{2,1,0:T(8,128)(2,1)}) custom-call(s32[2,64]{1,0:T(2,128)} %pairs.13, bf16[4096,256]{1,0:T(8,128)(2,1)} %points.1, f32[16,4096]{1,0:T(8,128)} %refs_0_.1), custom_call_target="tpu_custom_call" | custom-call | tf_op jit(solution)/shard_map/pallas_call | solution.py:312
  7.2 0.0 copy-start
  7.2 0.0 copy-start.1
  7.2 68.7 %all_to_all.35.sent = bf16[32,304,256]{2,1,0:T(8,128)(2,1)S(1)} all-to-all(bf16[32,304,256]{2,1,0:T(8,128)(2,1)} %get-tuple-element.29), channel_id=1, replica_groups=mesh['wide'=32,'narrow'=4] {'wide'}, dimensions={0} | all-to-all | bytes 9961472 | tf_op jit(solution)/shard_map/all_to_all | solution.py:336
  76.0 0.0 copy-done
  76.0 0.0 copy-done.1
  76.0 0.0 copy-start.2
  76.0 5.8 %shard_map.51 = (bf16[64,256,128]{2,1,0:T(8,128)(2,1)S(1)}, f32[32,32,128]{2,1,0:T(8,128)S(1)}, f32[16,4096]{1,0:T(8,128)S(1)}, f32[16,128]{1,0:T(8,128)S(1)}, s32[64]{0:T(128)S(1)}) custom-call(bf16[32,304,256]{2,1,0:T(8,128)(2,1)S(1)} %all_to_all.35.sent, bf16[4096,256]{1,0:T(8,128)(2,1)S(1)} %copy-done.1, f32[16,4096]{1,0:T(8,128)S(1)} %copy-done), custom_call_target="tpu_custom_call" | custom-call | tf_op jit(solution)/shard_map/pallas_call | solution.py:312
  81.7 15.3 %all_to_all.36.got = f32[32,32,128]{2,1,0:T(8,128)S(1)} all-to-all(f32[32,32,128]{2,1,0:T(8,128)S(1)} %get-tuple-element.32), channel_id=1, replica_groups=mesh['wide'=32,'narrow'=4] {'wide'}, dimensions={0} | all-to-all | bytes 1048576 | tf_op jit(solution)/shard_map/all_to_all | solution.py:336
  97.0 0.0 copy-done.2
  97.0 0.9 shard_map.52.t0
  97.9 2.8 %collective-permute-start.2 = (f32[16,4096]{1,0:T(8,128)S(1)}, f32[16,4096]{1,0:T(8,128)S(1)}, u32[]{:S(2)}, u32[]{:S(2)}) collective-permute-start(f32[16,4096]{1,0:T(8,128)S(1)} %shard_map.52.t0), channel_id=1, source_target_pairs={{0,3},{1,0},{2,1},{3,2},{4,7},{5,4},{6,5},{7,6},{8,11},{9,8},{10,9... | collective-permute-start | bytes 786440 | tf_op jit(solution)/shard_map/ppermute | solution.py:380
  100.7 0.4 collective-permute-start.1
  101.1 0.7 collective-permute-start
  101.8 1.4 shard_map.53.refs_1_
  103.2 8.9 %collective-permute-done.2.t3 = f32[16,4096]{1,0:T(8,128)S(1)} collective-permute-done((f32[16,4096]{1,0:T(8,128)S(1)}, f32[16,4096]{1,0:T(8,128)S(1)}, u32[]{:S(2)}, u32[]{:S(2)}) %collective-permute-start.2) | collective-permute-done | bytes 262176 | tf_op jit(solution)/shard_map/ppermute | solution.py:380
  112.0 0.0 collective-permute-done.1.t2
  112.0 4.0 %collective-permute-done.t1 = f32[16,4096]{1,0:T(8,128)S(1)} collective-permute-done((f32[16,4096]{1,0:T(8,128)S(1)}, f32[16,4096]{1,0:T(8,128)S(1)}, u32[]{:S(2)}, u32[]{:S(2)}) %collective-permute-start) | collective-permute-done | bytes 262176 | tf_op jit(solution)/shard_map/ppermute | solution.py:380
  116.1 1.6 shard_map.54
  117.7 16.6 %all_to_all.37.got = f32[32,40,128]{2,1,0:T(8,128)S(1)} all-to-all(f32[32,40,128]{2,1,0:T(8,128)S(1)} %get-tuple-element.35), channel_id=1, replica_groups=mesh['wide'=32,'narrow'=4] {'wide'}, dimensions={0} | all-to-all | bytes 1310720 | tf_op jit(solution)/shard_map/all_to_all | solution.py:336
  134.2 2.5 %shard_map.55 = (f32[32,32,128]{2,1,0:T(8,128)S(1)}, f32[16,4096]{1,0:T(8,128)S(1)}) custom-call(s32[64]{0:T(128)S(1)} %get-tuple-element.31.ids, f32[32,40,128]{2,1,0:T(8,128)S(1)} %all_to_all.37.got, bf16[64,256,128]{2,1,0:T(8,128)(2,1)S(1)} %get-tuple-element.36.tiles, f32[16,4096]{1,0:T(8,128)S(1)} %get-tuple-element.37.w0.refs_0_.refs_2_), custom_call_target="tpu_custom_call" | custom-call | tf_op jit(solution)/shard_map/pallas_call | solution.py:312
  136.8 15.1 %all_to_all.38.got = f32[32,32,128]{2,1,0:T(8,128)S(1)} all-to-all(f32[32,32,128]{2,1,0:T(8,128)S(1)} %get-tuple-element.38), channel_id=1, replica_groups=mesh['wide'=32,'narrow'=4] {'wide'}, dimensions={0} | all-to-all | bytes 1048576 | tf_op jit(solution)/shard_map/all_to_all | solution.py:336
  151.9 0.9 shard_map.56.t0
  152.8 0.4 collective-permute-start.5
  153.2 0.4 collective-permute-start.4
  153.6 0.8 collective-permute-start.3
  154.4 2.2 shard_map.57
  156.6 4.3 %collective-permute-done.5.t3 = f32[16,4096]{1,0:T(8,128)S(1)} collective-permute-done((f32[16,4096]{1,0:T(8,128)S(1)}, f32[16,4096]{1,0:T(8,128)S(1)}, u32[]{:S(2)}, u32[]{:S(2)}) %collective-permute-start.5) | collective-permute-done | bytes 262176 | tf_op jit(solution)/shard_map/ppermute | solution.py:380
  160.9 1.7 collective-permute-done.4.t2
  162.6 6.0 %collective-permute-done.3.t1 = f32[16,4096]{1,0:T(8,128)S(1)} collective-permute-done((f32[16,4096]{1,0:T(8,128)S(1)}, f32[16,4096]{1,0:T(8,128)S(1)}, u32[]{:S(2)}, u32[]{:S(2)}) %collective-permute-start.3) | collective-permute-done | bytes 262176 | tf_op jit(solution)/shard_map/ppermute | solution.py:380
  168.6 1.7 shard_map.58
  170.3 16.5 %all_to_all.39.got = f32[32,40,128]{2,1,0:T(8,128)S(1)} all-to-all(f32[32,40,128]{2,1,0:T(8,128)S(1)} %get-tuple-element.42), channel_id=1, replica_groups=mesh['wide'=32,'narrow'=4] {'wide'}, dimensions={0} | all-to-all | bytes 1310720 | tf_op jit(solution)/shard_map/all_to_all | solution.py:336
  186.8 2.5 %shard_map.59 = (f32[32,32,128]{2,1,0:T(8,128)S(1)}, f32[16,4096]{1,0:T(8,128)S(1)}) custom-call(s32[64]{0:T(128)S(1)} %get-tuple-element.31.ids, f32[32,40,128]{2,1,0:T(8,128)S(1)} %all_to_all.39.got, bf16[64,256,128]{2,1,0:T(8,128)(2,1)S(1)} %get-tuple-element.36.tiles, f32[16,4096]{1,0:T(8,128)S(1)} %get-tuple-element.43.w0.refs_0_), custom_call_target="tpu_custom_call" | custom-call | tf_op jit(solution)/shard_map/pallas_call | solution.py:312
  189.4 15.1 %all_to_all.40.got = f32[32,32,128]{2,1,0:T(8,128)S(1)} all-to-all(f32[32,32,128]{2,1,0:T(8,128)S(1)} %get-tuple-element.44), channel_id=1, replica_groups=mesh['wide'=32,'narrow'=4] {'wide'}, dimensions={0} | all-to-all | bytes 1048576 | tf_op jit(solution)/shard_map/all_to_all | solution.py:336
  204.5 0.9 shard_map.60.t0
  205.4 0.6 collective-permute-start.8
  206.0 0.1 collective-permute-start.7
  206.2 0.8 collective-permute-start.6
  207.0 2.2 shard_map.61
  209.2 4.3 %collective-permute-done.8.t3 = f32[16,4096]{1,0:T(8,128)S(1)} collective-permute-done((f32[16,4096]{1,0:T(8,128)S(1)}, f32[16,4096]{1,0:T(8,128)S(1)}, u32[]{:S(2)}, u32[]{:S(2)}) %collective-permute-start.8) | collective-permute-done | bytes 262176 | tf_op jit(solution)/shard_map/ppermute | solution.py:380
  213.5 1.9 collective-permute-done.7.t2
  215.5 6.0 %collective-permute-done.6.t1 = f32[16,4096]{1,0:T(8,128)S(1)} collective-permute-done((f32[16,4096]{1,0:T(8,128)S(1)}, f32[16,4096]{1,0:T(8,128)S(1)}, u32[]{:S(2)}, u32[]{:S(2)}) %collective-permute-start.6) | collective-permute-done | bytes 262176 | tf_op jit(solution)/shard_map/ppermute | solution.py:380
  221.4 1.4 shard_map.62
  222.8 11.3 %all_to_all.41.got = f32[32,8,128]{2,1,0:T(8,128)S(1)} all-to-all(f32[32,8,128]{2,1,0:T(8,128)S(1)} %get-tuple-element.49), channel_id=1, replica_groups=mesh['wide'=32,'narrow'=4] {'wide'}, dimensions={0} | all-to-all | bytes 262144 | tf_op jit(solution)/shard_map/all_to_all | solution.py:336
  234.1 3.2 %shard_map.63 = (f32[16,4096]{1,0:T(8,128)}, f32[3,2,16,16]{3,2,1,0:T(8,128)}) custom-call(f32[32,8,128]{2,1,0:T(8,128)S(1)} %all_to_all.41.got, f32[16,4096]{1,0:T(8,128)S(1)} %get-tuple-element.50.w0, f32[16,4096]{1,0:T(8,128)S(1)} %get-tuple-element.51.q, f32[16,16]{1,0:T(8,128)S(1)} %get-tuple-element.52.a0, f32[16,16]{1,0:T(8,128)S(1)} %get-tuple-element.53.l0, ...), custom_call_target="tpu_custom_call" | custom-call | tf_op jit(solution)/shard_map/pallas_call | solution.py:312
Async XLA Ops:
  7.2 68.8 %copy-start = (f32[16,4096]{1,0:T(8,128)S(1)}, f32[16,4096]{1,0:T(8,128)}, u32[]{:S(2)}) copy-start(f32[16,4096]{1,0:T(8,128)} %refs_0_.1) | copy-start | bytes 786436
  7.2 68.8 %copy-start.1 = (bf16[4096,256]{1,0:T(8,128)(2,1)S(1)}, bf16[4096,256]{1,0:T(8,128)(2,1)}, u32[]{:S(2)}) copy-start(bf16[4096,256]{1,0:T(8,128)(2,1)} %get-tuple-element.30.unit) | copy-start | bytes 6291460
  76.0 21.0 %copy-start.2 = (s32[2,64]{1,0:T(2,128)S(1)}, s32[2,64]{1,0:T(2,128)}, u32[]{:S(2)}) copy-start(s32[2,64]{1,0:T(2,128)} %pairs.13) | copy-start | bytes 1540
  97.9 14.1 %collective-permute-start.2 = (f32[16,4096]{1,0:T(8,128)S(1)}, f32[16,4096]{1,0:T(8,128)S(1)}, u32[]{:S(2)}, u32[]{:S(2)}) collective-permute-start(f32[16,4096]{1,0:T(8,128)S(1)} %shard_map.52.t0), channel_id=1, source_target_pairs={{0,3},{1,0},{2,1},{3,2},{4,7},{5,4},{6,5},{7,6},{8,11},{9,8},{10,9... | collective-permute-start | bytes 786440 | tf_op jit(solution)/shard_map/ppermute | solution.py:380
  100.7 11.3 %collective-permute-start.1 = (f32[16,4096]{1,0:T(8,128)S(1)}, f32[16,4096]{1,0:T(8,128)S(1)}, u32[]{:S(2)}, u32[]{:S(2)}) collective-permute-start(f32[16,4096]{1,0:T(8,128)S(1)} %shard_map.52.t0), channel_id=1, source_target_pairs={{0,2},{1,3},{2,0},{3,1},{4,6},{5,7},{6,4},{7,5},{8,10},{9,11},{10,... | collective-permute-start | bytes 786440 | tf_op jit(solution)/shard_map/ppermute | solution.py:380
  101.1 15.0 %collective-permute-start = (f32[16,4096]{1,0:T(8,128)S(1)}, f32[16,4096]{1,0:T(8,128)S(1)}, u32[]{:S(2)}, u32[]{:S(2)}) collective-permute-start(f32[16,4096]{1,0:T(8,128)S(1)} %shard_map.52.t0), channel_id=1, source_target_pairs={{0,1},{1,2},{2,3},{3,0},{4,5},{5,6},{6,7},{7,4},{8,9},{9,10},{10,1... | collective-permute-start | bytes 786440 | tf_op jit(solution)/shard_map/ppermute | solution.py:380
  152.8 8.1 %collective-permute-start.5 = (f32[16,4096]{1,0:T(8,128)S(1)}, f32[16,4096]{1,0:T(8,128)S(1)}, u32[]{:S(2)}, u32[]{:S(2)}) collective-permute-start(f32[16,4096]{1,0:T(8,128)S(1)} %shard_map.56.t0), channel_id=1, source_target_pairs={{0,3},{1,0},{2,1},{3,2},{4,7},{5,4},{6,5},{7,6},{8,11},{9,8},{10,9... | collective-permute-start | bytes 786440 | tf_op jit(solution)/shard_map/ppermute | solution.py:380
  153.2 9.4 %collective-permute-start.4 = (f32[16,4096]{1,0:T(8,128)S(1)}, f32[16,4096]{1,0:T(8,128)S(1)}, u32[]{:S(2)}, u32[]{:S(2)}) collective-permute-start(f32[16,4096]{1,0:T(8,128)S(1)} %shard_map.56.t0), channel_id=1, source_target_pairs={{0,2},{1,3},{2,0},{3,1},{4,6},{5,7},{6,4},{7,5},{8,10},{9,11},{10,... | collective-permute-start | bytes 786440 | tf_op jit(solution)/shard_map/ppermute | solution.py:380
  153.6 15.0 %collective-permute-start.3 = (f32[16,4096]{1,0:T(8,128)S(1)}, f32[16,4096]{1,0:T(8,128)S(1)}, u32[]{:S(2)}, u32[]{:S(2)}) collective-permute-start(f32[16,4096]{1,0:T(8,128)S(1)} %shard_map.56.t0), channel_id=1, source_target_pairs={{0,1},{1,2},{2,3},{3,0},{4,5},{5,6},{6,7},{7,4},{8,9},{9,10},{10,1... | collective-permute-start | bytes 786440 | tf_op jit(solution)/shard_map/ppermute | solution.py:380
  205.4 8.1 %collective-permute-start.8 = (f32[16,4096]{1,0:T(8,128)S(1)}, f32[16,4096]{1,0:T(8,128)S(1)}, u32[]{:S(2)}, u32[]{:S(2)}) collective-permute-start(f32[16,4096]{1,0:T(8,128)S(1)} %shard_map.60.t0), channel_id=1, source_target_pairs={{0,3},{1,0},{2,1},{3,2},{4,7},{5,4},{6,5},{7,6},{8,11},{9,8},{10,9... | collective-permute-start | bytes 786440 | tf_op jit(solution)/shard_map/ppermute | solution.py:380
  206.0 9.4 %collective-permute-start.7 = (f32[16,4096]{1,0:T(8,128)S(1)}, f32[16,4096]{1,0:T(8,128)S(1)}, u32[]{:S(2)}, u32[]{:S(2)}) collective-permute-start(f32[16,4096]{1,0:T(8,128)S(1)} %shard_map.60.t0), channel_id=1, source_target_pairs={{0,2},{1,3},{2,0},{3,1},{4,6},{5,7},{6,4},{7,5},{8,10},{9,11},{10,... | collective-permute-start | bytes 786440 | tf_op jit(solution)/shard_map/ppermute | solution.py:380
  206.2 15.3 %collective-permute-start.6 = (f32[16,4096]{1,0:T(8,128)S(1)}, f32[16,4096]{1,0:T(8,128)S(1)}, u32[]{:S(2)}, u32[]{:S(2)}) collective-permute-start(f32[16,4096]{1,0:T(8,128)S(1)} %shard_map.60.t0), channel_id=1, source_target_pairs={{0,1},{1,2},{2,3},{3,0},{4,5},{5,6},{6,7},{7,4},{8,9},{9,10},{10,1... | collective-permute-start | bytes 786440 | tf_op jit(solution)/shard_map/ppermute | solution.py:380

commit v5 on v4

--- a/solution.py
+++ b/solution.py
@@ -101,7 +101,7 @@
     return to_first, b[:rows] + b[rows:]
 
 
-def start_kernel(wide, cap, own_blocks, pairs, points, q_in, unit, out, raw, q, vec, meta, sems, sem):
+def start_kernel(wide, cap, own_blocks, pairs, points, q_in, unit_out, out, unit, raw, q, meta, sems, sem):
     vec_rows = q.shape[0]
     slot_rows = BS + vec_rows
     size = raw.shape[0] // CHUNKS
@@ -112,31 +112,39 @@
         for k in range(CHUNKS)
     ]
     loads.append(pltpu.make_async_copy(q_in, q, sems.at[CHUNKS]))
-    for load in loads:
+    for load in (loads[-1], *loads[:-1]):
         load.start()
-
-    for k in range(CHUNKS):
-        loads[k].wait()
-        for b in range(own_blocks // CHUNKS):
-            rows = pl.ds(k * size + b * BS, BS)
-            x = raw[rows, :].astype(F32)
-            x = x * lax.rsqrt(jnp.sum(x * x, axis=-1, keepdims=True) + EPSILON)
-            unit[rows, :] = x.astype(BF)
-
-    def send(p, carry):
-        for c in range(cap):
-            i = lax.rem(pairs[0, p * cap + c], own_blocks)
-            pltpu.make_async_copy(
-                unit.at[block(i), :], out.at[p, pl.ds(c * slot_rows, BS), :], sem
-            ).start()
-        return carry
-
-    lax.fori_loop(0, wide, send, 0, unroll=4)
     loads[-1].wait()
     high, low = split(q[...])
     for b in range(own_blocks):
         cols = slice(b * BS, (b + 1) * BS)
-        vec[b] = cat([high[:, cols], low[:, cols]], axis=1)
+        unit[b, BS:, :] = cat([high[:, cols], low[:, cols]], axis=1)
+    half = own_blocks // 2
+    for k in range(CHUNKS):
+        loads[k].wait()
+        for b in range(own_blocks // CHUNKS):
+            x = raw[pl.ds(k * size + b * BS, BS), :].astype(F32)
+            x = x * lax.rsqrt(jnp.sum(x * x, axis=-1, keepdims=True) + EPSILON)
+            unit[k * (own_blocks // CHUNKS) + b, :BS, :] = x.astype(BF)
+        if k % (CHUNKS // 2) != CHUNKS // 2 - 1:
+            continue
+        late = k == CHUNKS - 1
+
+        def send(p, carry, late=late):
+            for c in range(cap):
+                i = lax.rem(pairs[0, p * cap + c], own_blocks)
+
+                @pl.when((i >= half) == late)
+                def _(i=i, c=c):
+                    pltpu.make_async_copy(
+                        unit.at[i], out.at[p, pl.ds(c * slot_rows, slot_rows), :], sem
+                    ).start()
+
+            return carry
+
+        lax.fori_loop(0, wide, send, 0, unroll=8)
+    keep = pltpu.make_async_copy(unit, unit_out, sems.at[CHUNKS + 1])
+    keep.start()
     both = cat([high, low], axis=0)
     gram = mb(both, both, NT)
     gram = gram[:vec_rows, :vec_rows] + (gram[:vec_rows, vec_rows:] + gram[vec_rows:, :vec_rows])
@@ -151,18 +159,12 @@
         ids = [lax.rem(pairs[1, p * cap + c], own_blocks).astype(F32) for c in range(cap)]
         left = jnp.where(lanes < BS // 2, sums, ids[0])
         meta[p] = cat([left, jnp.full(sums.shape, ids[1])], axis=1).astype(BF)
-        for c in range(cap):
-            i = lax.rem(pairs[0, p * cap + c], own_blocks)
-            pltpu.make_async_copy(
-                vec.at[i], out.at[p, pl.ds(c * slot_rows + BS, vec_rows), :], sem
-            ).start()
-        pltpu.make_async_copy(
-            meta.at[p], out.at[p, pl.ds(cap * slot_rows, vec_rows), :], sem
-        ).start()
         return carry
 
-    lax.fori_loop(0, wide, label, 0, unroll=4)
+    lax.fori_loop(0, wide, label, 0, unroll=8)
+    pltpu.make_async_copy(meta, out.at[:, pl.ds(cap * slot_rows, vec_rows), :], sem).start()
     pltpu.make_async_copy(out, out, sem).wait()
+    keep.wait()
 
 
 def put_terms(terms, ids, first_slot, cap, rows, back, total):
@@ -171,36 +173,40 @@
         total[:, block(ids[s])] += to_second
 
 
-def tiles_kernel(peers, cap, sent, unit, q, tiles, back, total, gram, ids, got, sems):
+def tiles_kernel(peers, cap, sent, unit, q, tiles, back, total, gram, ids, got, labels, sems):
     wide = got.shape[0]
     vec_rows = q.shape[0]
     slot_rows = BS + vec_rows
     slots = range(peers * cap)
+    steps = wide // peers
 
     def load(k):
         part = pl.ds(k * peers, peers)
-        return pltpu.make_async_copy(sent.at[part], got.at[part], sems.at[k])
-
-    for k in range(wide // peers):
+        here = pl.ds(0, cap * slot_rows)
+        return pltpu.make_async_copy(sent.at[part, here], got.at[part], sems.at[k])
+
+    first = pltpu.make_async_copy(
+        sent.at[:, pl.ds(cap * slot_rows, vec_rows)], labels, sems.at[steps]
+    )
+    first.start()
+    for k in range(steps):
         load(k).start()
     total[...] = jnp.zeros_like(total)
-    gram[...] = jnp.zeros_like(gram)
+    first.wait()
+    gram[...] = jnp.sum(labels[:, :, :BS].astype(F32), axis=0)
+    for p in range(wide):
+        label = labels[p].astype(F32)
+        for c in range(cap):
+            ids[p * cap + c] = label[0, (c + 1) * (BS // 2)].astype(jnp.int32)
 
     def chunk(k, carry):
         load(k).wait()
         peer = k * peers
-        held = []
-        for p in range(peers):
-            label = got[peer + p, pl.ds(cap * slot_rows, vec_rows), :].astype(F32)
-            gram[...] += label[:, :BS]
-            for c in range(cap):
-                j = label[0, (c + 1) * (BS // 2)].astype(jnp.int32)
-                ids[(peer + p) * cap + c] = j
-                held.append(j)
+        held = [ids[peer * cap + s] for s in slots]
         stacks = []
         for s in slots:
             rows = pl.ds((s % cap) * slot_rows, BS)
-            inner = mb(got[peer + s // cap, rows, :], unit[block(held[s]), :], NT)
+            inner = mb(got[peer + s // cap, rows, :], unit[held[s], :BS, :], NT)
             stacks.append(tile_stack(jnp.exp(KERNEL_FACTOR * (inner - 1.0))))
             tiles[peer * cap + s] = stacks[s]
         terms = []
@@ -211,7 +217,7 @@
         put_terms(terms, held, peer * cap, cap, vec_rows, back, total)
         return carry
 
-    lax.fori_loop(0, wide // peers, chunk, 0)
+    lax.fori_loop(0, steps, chunk, 0)
 
 
 def terms_kernel(peers, cap, ids, got, tiles, w0, back, total):
@@ -243,7 +249,7 @@
             out[:, block(i)] += got[p, c * vec_rows : (c + 1) * vec_rows, :]
         return carry
 
-    lax.fori_loop(0, got.shape[0], add, 0, unroll=4)
+    lax.fori_loop(0, got.shape[0], add, 0, unroll=8)
 
 
 def first_factor_kernel(points, gram, matrix):
@@ -290,7 +296,7 @@
         out[p, cap * n :, :] = tail
         return carry
 
-    lax.fori_loop(0, out.shape[0], put, 0, unroll=4)
+    lax.fori_loop(0, out.shape[0], put, 0, unroll=8)
 
 
 def finish_kernel(points, got, w0, q, a0, l0, a1, l1, basis, coeffs):
@@ -338,23 +344,23 @@
     anywhere = pl.BlockSpec(memory_space=pl.ANY)
     unit, sent = call(
         functools.partial(start_kernel, wide, cap, own_blocks),
-        [((own_points, width), BF), ((wide, start_rows, width), BF)],
+        [((own_blocks, slot_rows, width), BF), ((wide, start_rows, width), BF)],
         1,
         VMEM_START,
         in_specs=[pl.BlockSpec(memory_space=pltpu.SMEM), anywhere, anywhere],
-        out_specs=(pl.BlockSpec(memory_space=pltpu.VMEM), anywhere),
+        out_specs=(anywhere, anywhere),
         scratch_shapes=[
+            pltpu.VMEM((own_blocks, slot_rows, width), BF),
             pltpu.VMEM((own_points, width), BF),
             pltpu.VMEM((vec_rows, own_points), F32),
-            pltpu.VMEM((own_blocks, vec_rows, 2 * BS), BF),
             pltpu.VMEM((wide, vec_rows, width), BF),
-            pltpu.SemaphoreType.DMA((CHUNKS + 1,)),
+            pltpu.SemaphoreType.DMA((CHUNKS + 2,)),
             pltpu.SemaphoreType.DMA,
         ],
     )(pairs, points, q_init)
     vmem = pl.BlockSpec(memory_space=pltpu.VMEM)
     tiles, back, total, gram, ids = call(
-        functools.partial(tiles_kernel, peers, cap),
+        functools.partial(tiles_kernel, peers * 2, cap),
         [
             ((pair_count, 2 * BS, BS), BF),
             reply,
@@ -367,8 +373,9 @@
         in_specs=[anywhere, vmem, vmem],
         out_specs=(vmem, vmem, vmem, vmem, pl.BlockSpec(memory_space=pltpu.SMEM)),
         scratch_shapes=[
-            pltpu.VMEM((wide, start_rows, width), BF),
-            pltpu.SemaphoreType.DMA((wide // peers,)),
+            pltpu.VMEM((wide, cap * slot_rows, width), BF),
+            pltpu.VMEM((wide, vec_rows, width), BF),
+            pltpu.SemaphoreType.DMA((wide // peers + 1,)),
         ],
     )(exchange(sent), unit, q_init)
 
@@ -394,7 +401,7 @@
         last = step == STEPS - 1
         got = exchange(out)
         back, total = call(
-            functools.partial(terms_kernel, 2 * peers, cap), [reply, vectors], 1
+            functools.partial(terms_kernel, 4 * peers, cap), [reply, vectors], 1
         )(ids, got, tiles, w0)
         sums = narrow_terms(back, total)
         count = 2 if last else 3

time: 238 us -> 235 us (0.987)
  Pallas kernels: 33.8 us -> 30.9 us
    pallas_call x14, Pallas kernels: 33.8 us -> 30.9 us  [run(): pl.pallas_call(kernel, out_shape=shapes, compiler_params=params, **given)]
  transfers between devices with their start and end apart: 9 -> 9, of which waited for: 8 -> 8; matrix products, arithmetic and copies ran while one was open for 0% -> 0% of each run, Pallas kernels for 2% -> 3%
where the time goes in v5:
time: 235 us; the launch traced here: 234 us
  blocking collectives  159 us (68%)
  waiting for transfers between devices  37.1 us (16%)
  Pallas kernels  30.9 us (13%)
  starting transfers between devices  6.82 us (3%)
    all_to_all x7, blocking collectives, exchange(): return lax.all_to_all(x, 'wide', split_axis=0, concat_axis=0, tiled=True)  159 us
    ppermute x9, waiting for transfers between devices, narrow_terms(): lax.ppermute(total, 'narrow', [(i, (i + s) % narrow) for i in range(narro...  37.1 us
    pallas_call x14, Pallas kernels, run(): pl.pallas_call(kernel, out_shape=shapes, compiler_params=params, **given)  30.9 us
    ppermute x9, starting transfers between devices, narrow_terms(): lax.ppermute(total, 'narrow', [(i, (i + s) % narrow) for i in range(narro...  6.82 us
  transfers between devices with their start and end apart: 9, of which 8 were waited for; matrix products, arithmetic and copies ran while one was open for 0% of the time, Pallas kernels for 3%

profile of v5, /device:TPU:1, one launch (start us, length us, event | category | flops | bytes accessed | tf_op | source)
XLA Modules:
  0.0 234.5 jit_solution(793965117602552799)
XLA Ops:
  0.6 5.4 %shard_map.50 = (bf16[32,144,256]{2,1,0:T(8,128)(2,1)}, bf16[32,304,256]{2,1,0:T(8,128)(2,1)}) custom-call(s32[2,64]{1,0:T(2,128)} %pairs.13, bf16[4096,256]{1,0:T(8,128)(2,1)} %points.1, f32[16,4096]{1,0:T(8,128)} %refs_0_.1), custom_call_target="tpu_custom_call" | custom-call | tf_op jit(solution)/shard_map/pallas_call | solution.py:318
  6.1 0.0 copy-start
  6.1 0.0 copy-start.1
  6.1 68.9 %all_to_all.35.sent = bf16[32,304,256]{2,1,0:T(8,128)(2,1)S(1)} all-to-all(bf16[32,304,256]{2,1,0:T(8,128)(2,1)} %get-tuple-element.29), channel_id=1, replica_groups=mesh['wide'=32,'narrow'=4] {'wide'}, dimensions={0} | all-to-all | bytes 9961472 | tf_op jit(solution)/shard_map/all_to_all | solution.py:342
  75.0 0.0 copy-done
  75.0 0.0 copy-done.1
  75.0 0.0 copy-start.2
  75.0 4.3 %shard_map.51 = (bf16[64,256,128]{2,1,0:T(8,128)(2,1)S(1)}, f32[32,32,128]{2,1,0:T(8,128)S(1)}, f32[16,4096]{1,0:T(8,128)S(1)}, f32[16,128]{1,0:T(8,128)S(1)}, s32[64]{0:T(128)S(1)}) custom-call(bf16[32,304,256]{2,1,0:T(8,128)(2,1)S(1)} %all_to_all.35.sent, bf16[32,144,256]{2,1,0:T(8,128)(2,1)S(1)} %copy-done, f32[16,4096]{1,0:T(8,128)S(1)} %copy-done.1), custom_call_target="tpu_custom_call" | custom-call | tf_op jit(solution)/shard_map/pallas_call | solution.py:318
  79.3 15.3 %all_to_all.36.got = f32[32,32,128]{2,1,0:T(8,128)S(1)} all-to-all(f32[32,32,128]{2,1,0:T(8,128)S(1)} %get-tuple-element.32), channel_id=1, replica_groups=mesh['wide'=32,'narrow'=4] {'wide'}, dimensions={0} | all-to-all | bytes 1048576 | tf_op jit(solution)/shard_map/all_to_all | solution.py:342
  94.6 0.0 copy-done.2
  94.6 0.9 shard_map.52.t0
  95.5 2.7 %collective-permute-start.2 = (f32[16,4096]{1,0:T(8,128)S(1)}, f32[16,4096]{1,0:T(8,128)S(1)}, u32[]{:S(2)}, u32[]{:S(2)}) collective-permute-start(f32[16,4096]{1,0:T(8,128)S(1)} %shard_map.52.t0), channel_id=1, source_target_pairs={{0,3},{1,0},{2,1},{3,2},{4,7},{5,4},{6,5},{7,6},{8,11},{9,8},{10,9... | collective-permute-start | bytes 786440 | tf_op jit(solution)/shard_map/ppermute | solution.py:387
  98.1 0.4 collective-permute-start.1
  98.5 0.7 collective-permute-start
  99.2 1.4 shard_map.53.refs_1_
  100.6 8.8 %collective-permute-done.2.t3 = f32[16,4096]{1,0:T(8,128)S(1)} collective-permute-done((f32[16,4096]{1,0:T(8,128)S(1)}, f32[16,4096]{1,0:T(8,128)S(1)}, u32[]{:S(2)}, u32[]{:S(2)}) %collective-permute-start.2) | collective-permute-done | bytes 262176 | tf_op jit(solution)/shard_map/ppermute | solution.py:387
  109.5 0.0 collective-permute-done.1.t2
  109.5 4.0 %collective-permute-done.t1 = f32[16,4096]{1,0:T(8,128)S(1)} collective-permute-done((f32[16,4096]{1,0:T(8,128)S(1)}, f32[16,4096]{1,0:T(8,128)S(1)}, u32[]{:S(2)}, u32[]{:S(2)}) %collective-permute-start) | collective-permute-done | bytes 262176 | tf_op jit(solution)/shard_map/ppermute | solution.py:387
  113.5 1.6 shard_map.54
  115.1 16.6 %all_to_all.37.got = f32[32,40,128]{2,1,0:T(8,128)S(1)} all-to-all(f32[32,40,128]{2,1,0:T(8,128)S(1)} %get-tuple-element.35), channel_id=1, replica_groups=mesh['wide'=32,'narrow'=4] {'wide'}, dimensions={0} | all-to-all | bytes 1310720 | tf_op jit(solution)/shard_map/all_to_all | solution.py:342
  131.7 2.4 %shard_map.55 = (f32[32,32,128]{2,1,0:T(8,128)S(1)}, f32[16,4096]{1,0:T(8,128)S(1)}) custom-call(s32[64]{0:T(128)S(1)} %get-tuple-element.31.ids, f32[32,40,128]{2,1,0:T(8,128)S(1)} %all_to_all.37.got, bf16[64,256,128]{2,1,0:T(8,128)(2,1)S(1)} %get-tuple-element.36.tiles, f32[16,4096]{1,0:T(8,128)S(1)} %get-tuple-element.37.w0.refs_0_.refs_2_), custom_call_target="tpu_custom_call" | custom-call | tf_op jit(solution)/shard_map/pallas_call | solution.py:318
  134.0 15.1 %all_to_all.38.got = f32[32,32,128]{2,1,0:T(8,128)S(1)} all-to-all(f32[32,32,128]{2,1,0:T(8,128)S(1)} %get-tuple-element.38), channel_id=1, replica_groups=mesh['wide'=32,'narrow'=4] {'wide'}, dimensions={0} | all-to-all | bytes 1048576 | tf_op jit(solution)/shard_map/all_to_all | solution.py:342
  149.2 0.9 shard_map.56.t0
  150.1 0.4 collective-permute-start.5
  150.5 0.4 collective-permute-start.4
  150.9 0.7 collective-permute-start.3
  151.6 2.2 shard_map.57
  153.9 4.3 %collective-permute-done.5.t3 = f32[16,4096]{1,0:T(8,128)S(1)} collective-permute-done((f32[16,4096]{1,0:T(8,128)S(1)}, f32[16,4096]{1,0:T(8,128)S(1)}, u32[]{:S(2)}, u32[]{:S(2)}) %collective-permute-start.5) | collective-permute-done | bytes 262176 | tf_op jit(solution)/shard_map/ppermute | solution.py:387
  158.2 1.7 collective-permute-done.4.t2
  159.9 6.0 %collective-permute-done.3.t1 = f32[16,4096]{1,0:T(8,128)S(1)} collective-permute-done((f32[16,4096]{1,0:T(8,128)S(1)}, f32[16,4096]{1,0:T(8,128)S(1)}, u32[]{:S(2)}, u32[]{:S(2)}) %collective-permute-start.3) | collective-permute-done | bytes 262176 | tf_op jit(solution)/shard_map/ppermute | solution.py:387
  165.9 1.7 shard_map.58
  167.6 16.5 %all_to_all.39.got = f32[32,40,128]{2,1,0:T(8,128)S(1)} all-to-all(f32[32,40,128]{2,1,0:T(8,128)S(1)} %get-tuple-element.42), channel_id=1, replica_groups=mesh['wide'=32,'narrow'=4] {'wide'}, dimensions={0} | all-to-all | bytes 1310720 | tf_op jit(solution)/shard_map/all_to_all | solution.py:342
  184.1 2.4 %shard_map.59 = (f32[32,32,128]{2,1,0:T(8,128)S(1)}, f32[16,4096]{1,0:T(8,128)S(1)}) custom-call(s32[64]{0:T(128)S(1)} %get-tuple-element.31.ids, f32[32,40,128]{2,1,0:T(8,128)S(1)} %all_to_all.39.got, bf16[64,256,128]{2,1,0:T(8,128)(2,1)S(1)} %get-tuple-element.36.tiles, f32[16,4096]{1,0:T(8,128)S(1)} %get-tuple-element.43.w0.refs_0_), custom_call_target="tpu_custom_call" | custom-call | tf_op jit(solution)/shard_map/pallas_call | solution.py:318
  186.5 15.1 %all_to_all.40.got = f32[32,32,128]{2,1,0:T(8,128)S(1)} all-to-all(f32[32,32,128]{2,1,0:T(8,128)S(1)} %get-tuple-element.44), channel_id=1, replica_groups=mesh['wide'=32,'narrow'=4] {'wide'}, dimensions={0} | all-to-all | bytes 1048576 | tf_op jit(solution)/shard_map/all_to_all | solution.py:342
  201.6 0.9 shard_map.60.t0
  202.5 0.6 collective-permute-start.8
  203.2 0.2 collective-permute-start.7
  203.3 0.7 collective-permute-start.6
  204.1 2.2 shard_map.61
  206.3 4.3 %collective-permute-done.8.t3 = f32[16,4096]{1,0:T(8,128)S(1)} collective-permute-done((f32[16,4096]{1,0:T(8,128)S(1)}, f32[16,4096]{1,0:T(8,128)S(1)}, u32[]{:S(2)}, u32[]{:S(2)}) %collective-permute-start.8) | collective-permute-done | bytes 262176 | tf_op jit(solution)/shard_map/ppermute | solution.py:387
  210.7 1.9 collective-permute-done.7.t2
  212.6 6.0 %collective-permute-done.6.t1 = f32[16,4096]{1,0:T(8,128)S(1)} collective-permute-done((f32[16,4096]{1,0:T(8,128)S(1)}, f32[16,4096]{1,0:T(8,128)S(1)}, u32[]{:S(2)}, u32[]{:S(2)}) %collective-permute-start.6) | collective-permute-done | bytes 262176 | tf_op jit(solution)/shard_map/ppermute | solution.py:387
  218.6 1.4 shard_map.62
  220.0 11.3 %all_to_all.41.got = f32[32,8,128]{2,1,0:T(8,128)S(1)} all-to-all(f32[32,8,128]{2,1,0:T(8,128)S(1)} %get-tuple-element.49), channel_id=1, replica_groups=mesh['wide'=32,'narrow'=4] {'wide'}, dimensions={0} | all-to-all | bytes 262144 | tf_op jit(solution)/shard_map/all_to_all | solution.py:342
  231.3 3.2 %shard_map.63 = (f32[16,4096]{1,0:T(8,128)}, f32[3,2,16,16]{3,2,1,0:T(8,128)}) custom-call(f32[32,8,128]{2,1,0:T(8,128)S(1)} %all_to_all.41.got, f32[16,4096]{1,0:T(8,128)S(1)} %get-tuple-element.50.w0, f32[16,4096]{1,0:T(8,128)S(1)} %get-tuple-element.51.q, f32[16,16]{1,0:T(8,128)S(1)} %get-tuple-element.52.a0, f32[16,16]{1,0:T(8,128)S(1)} %get-tuple-element.53.l0, ...), custom_call_target="tpu_custom_call" | custom-call | tf_op jit(solution)/shard_map/pallas_call | solution.py:318
Async XLA Ops:
  6.1 69.0 %copy-start = (bf16[32,144,256]{2,1,0:T(8,128)(2,1)S(1)}, bf16[32,144,256]{2,1,0:T(8,128)(2,1)}, u32[]{:S(2)}) copy-start(bf16[32,144,256]{2,1,0:T(8,128)(2,1)} %get-tuple-element.30.unit) | copy-start | bytes 7077892
  6.1 69.0 %copy-start.1 = (f32[16,4096]{1,0:T(8,128)S(1)}, f32[16,4096]{1,0:T(8,128)}, u32[]{:S(2)}) copy-start(f32[16,4096]{1,0:T(8,128)} %refs_0_.1) | copy-start | bytes 786436
  75.0 19.5 %copy-start.2 = (s32[2,64]{1,0:T(2,128)S(1)}, s32[2,64]{1,0:T(2,128)}, u32[]{:S(2)}) copy-start(s32[2,64]{1,0:T(2,128)} %pairs.13) | copy-start | bytes 1540
  95.5 14.0 %collective-permute-start.2 = (f32[16,4096]{1,0:T(8,128)S(1)}, f32[16,4096]{1,0:T(8,128)S(1)}, u32[]{:S(2)}, u32[]{:S(2)}) collective-permute-start(f32[16,4096]{1,0:T(8,128)S(1)} %shard_map.52.t0), channel_id=1, source_target_pairs={{0,3},{1,0},{2,1},{3,2},{4,7},{5,4},{6,5},{7,6},{8,11},{9,8},{10,9... | collective-permute-start | bytes 786440 | tf_op jit(solution)/shard_map/ppermute | solution.py:387
  98.1 11.3 %collective-permute-start.1 = (f32[16,4096]{1,0:T(8,128)S(1)}, f32[16,4096]{1,0:T(8,128)S(1)}, u32[]{:S(2)}, u32[]{:S(2)}) collective-permute-start(f32[16,4096]{1,0:T(8,128)S(1)} %shard_map.52.t0), channel_id=1, source_target_pairs={{0,2},{1,3},{2,0},{3,1},{4,6},{5,7},{6,4},{7,5},{8,10},{9,11},{10,... | collective-permute-start | bytes 786440 | tf_op jit(solution)/shard_map/ppermute | solution.py:387
  98.5 15.0 %collective-permute-start = (f32[16,4096]{1,0:T(8,128)S(1)}, f32[16,4096]{1,0:T(8,128)S(1)}, u32[]{:S(2)}, u32[]{:S(2)}) collective-permute-start(f32[16,4096]{1,0:T(8,128)S(1)} %shard_map.52.t0), channel_id=1, source_target_pairs={{0,1},{1,2},{2,3},{3,0},{4,5},{5,6},{6,7},{7,4},{8,9},{9,10},{10,1... | collective-permute-start | bytes 786440 | tf_op jit(solution)/shard_map/ppermute | solution.py:387
  150.1 8.1 %collective-permute-start.5 = (f32[16,4096]{1,0:T(8,128)S(1)}, f32[16,4096]{1,0:T(8,128)S(1)}, u32[]{:S(2)}, u32[]{:S(2)}) collective-permute-start(f32[16,4096]{1,0:T(8,128)S(1)} %shard_map.56.t0), channel_id=1, source_target_pairs={{0,3},{1,0},{2,1},{3,2},{4,7},{5,4},{6,5},{7,6},{8,11},{9,8},{10,9... | collective-permute-start | bytes 786440 | tf_op jit(solution)/shard_map/ppermute | solution.py:387
  150.5 9.4 %collective-permute-start.4 = (f32[16,4096]{1,0:T(8,128)S(1)}, f32[16,4096]{1,0:T(8,128)S(1)}, u32[]{:S(2)}, u32[]{:S(2)}) collective-permute-start(f32[16,4096]{1,0:T(8,128)S(1)} %shard_map.56.t0), channel_id=1, source_target_pairs={{0,2},{1,3},{2,0},{3,1},{4,6},{5,7},{6,4},{7,5},{8,10},{9,11},{10,... | collective-permute-start | bytes 786440 | tf_op jit(solution)/shard_map/ppermute | solution.py:387
  150.9 15.0 %collective-permute-start.3 = (f32[16,4096]{1,0:T(8,128)S(1)}, f32[16,4096]{1,0:T(8,128)S(1)}, u32[]{:S(2)}, u32[]{:S(2)}) collective-permute-start(f32[16,4096]{1,0:T(8,128)S(1)} %shard_map.56.t0), channel_id=1, source_target_pairs={{0,1},{1,2},{2,3},{3,0},{4,5},{5,6},{6,7},{7,4},{8,9},{9,10},{10,1... | collective-permute-start | bytes 786440 | tf_op jit(solution)/shard_map/ppermute | solution.py:387
  202.5 8.1 %collective-permute-start.8 = (f32[16,4096]{1,0:T(8,128)S(1)}, f32[16,4096]{1,0:T(8,128)S(1)}, u32[]{:S(2)}, u32[]{:S(2)}) collective-permute-start(f32[16,4096]{1,0:T(8,128)S(1)} %shard_map.60.t0), channel_id=1, source_target_pairs={{0,3},{1,0},{2,1},{3,2},{4,7},{5,4},{6,5},{7,6},{8,11},{9,8},{10,9... | collective-permute-start | bytes 786440 | tf_op jit(solution)/shard_map/ppermute | solution.py:387
  203.2 9.4 %collective-permute-start.7 = (f32[16,4096]{1,0:T(8,128)S(1)}, f32[16,4096]{1,0:T(8,128)S(1)}, u32[]{:S(2)}, u32[]{:S(2)}) collective-permute-start(f32[16,4096]{1,0:T(8,128)S(1)} %shard_map.60.t0), channel_id=1, source_target_pairs={{0,2},{1,3},{2,0},{3,1},{4,6},{5,7},{6,4},{7,5},{8,10},{9,11},{10,... | collective-permute-start | bytes 786440 | tf_op jit(solution)/shard_map/ppermute | solution.py:387
  203.3 15.3 %collective-permute-start.6 = (f32[16,4096]{1,0:T(8,128)S(1)}, f32[16,4096]{1,0:T(8,128)S(1)}, u32[]{:S(2)}, u32[]{:S(2)}) collective-permute-start(f32[16,4096]{1,0:T(8,128)S(1)} %shard_map.60.t0), channel_id=1, source_target_pairs={{0,1},{1,2},{2,3},{3,0},{4,5},{5,6},{6,7},{7,4},{8,9},{9,10},{10,1... | collective-permute-start | bytes 786440 | tf_op jit(solution)/shard_map/ppermute | solution.py:387

commit v6 on v5

--- a/solution.py
+++ b/solution.py
@@ -239,14 +239,17 @@
     lax.fori_loop(0, got.shape[0] // peers, chunk, 0)
 
 
-def sum_kernel(cap, own_blocks, pairs, got, total, out):
+def sum_kernel(cap, own_blocks, pairs, got, total, top, low):
     vec_rows = total.shape[0]
-    out[...] = total[...]
+    half = vec_rows // 2
+    top[...] = total[:half]
+    low[...] = total[half:]
 
     def add(p, carry):
         for c in range(cap):
             i = lax.rem(pairs[0, p * cap + c], own_blocks)
-            out[:, block(i)] += got[p, c * vec_rows : (c + 1) * vec_rows, :]
+            top[:, block(i)] += got[p, c * vec_rows : c * vec_rows + half, :]
+            low[:, block(i)] += got[p, c * vec_rows + half : (c + 1) * vec_rows, :]
         return carry
 
     lax.fori_loop(0, got.shape[0], add, 0, unroll=8)
@@ -274,9 +277,9 @@
     matrix[...] = cat(lines, axis=0)
 
 
-def update_kernel(cap, own_blocks, old, pairs, t0, t1, t2, t3, *refs):
+def update_kernel(cap, own_blocks, old, pairs, t0, t1, b0, b1, *refs):
     given, matrix, outs, out = refs[:old], refs[old], refs[old + 1 : -1], refs[-1]
-    image = (t0[...] + t2[...]) + (t1[...] + t3[...])
+    image = cat([t0[...] + t1[...], b0[...] + b1[...]], axis=0)
     rows = [r[...] for r in given]
     rows.insert(2 if old > 1 else 1, image)
     new = apply_small(matrix[...], cat(rows, axis=0))
@@ -379,14 +382,18 @@
         ],
     )(exchange(sent), unit, q_init)
 
+    def swap(x, mask):
+        return lax.ppermute(x, "narrow", [(i, i ^ mask) for i in range(narrow)])
+
+    half = ((vec_rows // 2, own_points), F32)
+
     def narrow_terms(back, total):
-        (total,) = call(functools.partial(sum_kernel, cap, own_blocks), [vectors], 1)(
+        top, low = call(functools.partial(sum_kernel, cap, own_blocks), [half, half], 1)(
             pairs, exchange(back), total
         )
-        return (total,) + tuple(
-            lax.ppermute(total, "narrow", [(i, (i + s) % narrow) for i in range(narrow)])
-            for s in range(1, narrow)
-        )
+        top_from, low_from = swap(top, 1), swap(low, 3)
+        top, low = top + top_from, low + low_from
+        return top, swap(top, 3), low, swap(low, 1)
 
     sums = narrow_terms(back, total)
     (matrix,) = call(

time: 235 us -> 223 us (0.949)
  waiting for transfers between devices: 37.1 us -> 16.2 us
  starting transfers between devices: 6.82 us -> 12.3 us
  blocking collectives: 159 us -> 163 us
    ppermute x9 -> x12, waiting for transfers between devices: 37.1 us -> 16.2 us  [swap(): return lax.ppermute(x, 'narrow', [(i, i ^ mask) for i in range(narrow)])]
    ppermute x9 -> x12, starting transfers between devices: 6.82 us -> 12.3 us  [swap(): return lax.ppermute(x, 'narrow', [(i, i ^ mask) for i in range(narrow)])]
    all_to_all x7, blocking collectives: 159 us -> 163 us  [exchange(): return lax.all_to_all(x, 'wide', split_axis=0, concat_axis=0, tiled=True)]
  transfers between devices with their start and end apart: 9 -> 12, of which waited for: 8 -> 8; matrix products, arithmetic and copies ran while one was open for 0% -> 0% of each run, Pallas kernels for 3% -> 3%
where the time goes in v6:
time: 223 us
  blocking collectives  163 us (73%)
  Pallas kernels  30.9 us (14%)
  waiting for transfers between devices  16.2 us (7%)
  starting transfers between devices  12.3 us (6%)
    all_to_all x7, blocking collectives, exchange(): return lax.all_to_all(x, 'wide', split_axis=0, concat_axis=0, tiled=True)  163 us
    pallas_call x14, Pallas kernels, run(): pl.pallas_call(kernel, out_shape=shapes, compiler_params=params, **given)  30.9 us
    ppermute x12, waiting for transfers between devices, swap(): return lax.ppermute(x, 'narrow', [(i, i ^ mask) for i in range(narrow)])  16.2 us
    ppermute x12, starting transfers between devices, swap(): return lax.ppermute(x, 'narrow', [(i, i ^ mask) for i in range(narrow)])  12.3 us
  transfers between devices with their start and end apart: 12, of which 8 were waited for; matrix products, arithmetic and copies ran while one was open for 0% of the time, Pallas kernels for 3%

profile of v6, /device:TPU:1, one launch (start us, length us, event | category | flops | bytes accessed | tf_op | source)
XLA Modules:
  0.0 223.0 jit_solution(16589997802147752035)
XLA Ops:
  0.6 5.5 %shard_map.50 = (bf16[32,144,256]{2,1,0:T(8,128)(2,1)}, bf16[32,304,256]{2,1,0:T(8,128)(2,1)}) custom-call(s32[2,64]{1,0:T(2,128)} %pairs.13, bf16[4096,256]{1,0:T(8,128)(2,1)} %points.1, f32[16,4096]{1,0:T(8,128)} %refs_0_.1), custom_call_target="tpu_custom_call" | custom-call | tf_op jit(solution)/shard_map/pallas_call | solution.py:321
  6.1 0.0 copy-start
  6.1 0.0 copy-start.1
  6.2 68.8 %all_to_all.35.sent = bf16[32,304,256]{2,1,0:T(8,128)(2,1)S(1)} all-to-all(bf16[32,304,256]{2,1,0:T(8,128)(2,1)} %get-tuple-element.35), channel_id=1, replica_groups=mesh['wide'=32,'narrow'=4] {'wide'}, dimensions={0} | all-to-all | bytes 9961472 | tf_op jit(solution)/shard_map/all_to_all | solution.py:345
  75.0 0.0 copy-done
  75.0 0.0 copy-done.1
  75.0 0.0 copy-start.2
  75.0 4.3 %shard_map.51 = (bf16[64,256,128]{2,1,0:T(8,128)(2,1)S(1)}, f32[32,32,128]{2,1,0:T(8,128)S(1)}, f32[16,4096]{1,0:T(8,128)S(1)}, f32[16,128]{1,0:T(8,128)S(1)}, s32[64]{0:T(128)S(1)}) custom-call(bf16[32,304,256]{2,1,0:T(8,128)(2,1)S(1)} %all_to_all.35.sent, bf16[32,144,256]{2,1,0:T(8,128)(2,1)S(1)} %copy-done, f32[16,4096]{1,0:T(8,128)S(1)} %copy-done.1), custom_call_target="tpu_custom_call" | custom-call | tf_op jit(solution)/shard_map/pallas_call | solution.py:321
  79.3 15.3 %all_to_all.36.got = f32[32,32,128]{2,1,0:T(8,128)S(1)} all-to-all(f32[32,32,128]{2,1,0:T(8,128)S(1)} %get-tuple-element.38), channel_id=1, replica_groups=mesh['wide'=32,'narrow'=4] {'wide'}, dimensions={0} | all-to-all | bytes 1048576 | tf_op jit(solution)/shard_map/all_to_all | solution.py:345
  94.5 0.0 copy-done.2
  94.5 0.9 shard_map.52
  95.4 1.3 collective-permute-start
  96.7 2.0 collective-permute-start.2
  98.7 2.1 collective-permute-done
  100.8 2.9 %collective-permute-start.1 = (f32[8,4096]{1,0:T(8,128)S(1)}, f32[8,4096]{1,0:T(8,128)S(1)}, u32[]{:S(2)}, u32[]{:S(2)}) collective-permute-start(f32[8,4096]{1,0:T(8,128)S(1)} %add.18.t0), channel_id=1, source_target_pairs={{0,3},{1,2},{2,1},{3,0},{4,7},{5,6},{6,5},{7,4},{8,11},{9,10},{10,... | collective-permute-start | bytes 393224 | tf_op jit(solution)/shard_map/ppermute | solution.py:386
  103.7 0.0 collective-permute-done.2
  103.7 0.1 collective-permute-start.3
  103.8 1.4 shard_map.53.refs_1_
  105.2 1.6 collective-permute-done.1.t1
  106.8 0.9 collective-permute-done.3.b1
  107.7 1.6 shard_map.54
  109.3 18.1 %all_to_all.37.got = f32[32,40,128]{2,1,0:T(8,128)S(1)} all-to-all(f32[32,40,128]{2,1,0:T(8,128)S(1)} %get-tuple-element.43), channel_id=1, replica_groups=mesh['wide'=32,'narrow'=4] {'wide'}, dimensions={0} | all-to-all | bytes 1310720 | tf_op jit(solution)/shard_map/all_to_all | solution.py:345
  127.4 2.4 %shard_map.55 = (f32[32,32,128]{2,1,0:T(8,128)S(1)}, f32[16,4096]{1,0:T(8,128)S(1)}) custom-call(s32[64]{0:T(128)S(1)} %get-tuple-element.37.ids, f32[32,40,128]{2,1,0:T(8,128)S(1)} %all_to_all.37.got, bf16[64,256,128]{2,1,0:T(8,128)(2,1)S(1)} %get-tuple-element.44.tiles, f32[16,4096]{1,0:T(8,128)S(1)} %get-tuple-element.45.w0.refs_0_.refs_2_), custom_call_target="tpu_custom_call" | custom-call | tf_op jit(solution)/shard_map/pallas_call | solution.py:321
  129.8 15.1 %all_to_all.38.got = f32[32,32,128]{2,1,0:T(8,128)S(1)} all-to-all(f32[32,32,128]{2,1,0:T(8,128)S(1)} %get-tuple-element.46), channel_id=1, replica_groups=mesh['wide'=32,'narrow'=4] {'wide'}, dimensions={0} | all-to-all | bytes 1048576 | tf_op jit(solution)/shard_map/all_to_all | solution.py:345
  144.9 0.9 shard_map.56
  145.8 0.1 collective-permute-start.4
  145.9 1.2 collective-permute-start.6
  147.1 4.0 %collective-permute-done.4 = f32[8,4096]{1,0:T(8,128)S(1)} collective-permute-done((f32[8,4096]{1,0:T(8,128)S(1)}, f32[8,4096]{1,0:T(8,128)S(1)}, u32[]{:S(2)}, u32[]{:S(2)}) %collective-permute-start.4) | collective-permute-done | bytes 131104 | tf_op jit(solution)/shard_map/ppermute | solution.py:386
  151.2 1.2 collective-permute-start.5
  152.4 0.0 collective-permute-done.6
  152.4 0.1 collective-permute-start.7
  152.5 2.2 %shard_map.57 = (f32[48,64]{1,0:T(8,128)S(1)}, f32[16,16]{1,0:T(8,128)S(1)}, f32[16,16]{1,0:T(8,128)S(1)}) custom-call(f32[32,40,128]{2,1,0:T(8,128)S(1)} %all_to_all.37.got), custom_call_target="tpu_custom_call" | custom-call | tf_op jit(solution)/shard_map/pallas_call | solution.py:321
  154.8 2.0 collective-permute-done.5.t1
  156.8 0.0 collective-permute-done.7.b1
  156.8 1.7 shard_map.58
  158.5 17.6 %all_to_all.39.got = f32[32,40,128]{2,1,0:T(8,128)S(1)} all-to-all(f32[32,40,128]{2,1,0:T(8,128)S(1)} %get-tuple-element.52), channel_id=1, replica_groups=mesh['wide'=32,'narrow'=4] {'wide'}, dimensions={0} | all-to-all | bytes 1310720 | tf_op jit(solution)/shard_map/all_to_all | solution.py:345
  176.2 2.4 %shard_map.59 = (f32[32,32,128]{2,1,0:T(8,128)S(1)}, f32[16,4096]{1,0:T(8,128)S(1)}) custom-call(s32[64]{0:T(128)S(1)} %get-tuple-element.37.ids, f32[32,40,128]{2,1,0:T(8,128)S(1)} %all_to_all.39.got, bf16[64,256,128]{2,1,0:T(8,128)(2,1)S(1)} %get-tuple-element.44.tiles, f32[16,4096]{1,0:T(8,128)S(1)} %get-tuple-element.53.w0.refs_0_), custom_call_target="tpu_custom_call" | custom-call | tf_op jit(solution)/shard_map/pallas_call | solution.py:321
  178.5 15.1 %all_to_all.40.got = f32[32,32,128]{2,1,0:T(8,128)S(1)} all-to-all(f32[32,32,128]{2,1,0:T(8,128)S(1)} %get-tuple-element.54), channel_id=1, replica_groups=mesh['wide'=32,'narrow'=4] {'wide'}, dimensions={0} | all-to-all | bytes 1048576 | tf_op jit(solution)/shard_map/all_to_all | solution.py:345
  193.7 0.9 shard_map.60
  194.6 0.1 collective-permute-start.8
  194.7 1.6 collective-permute-start.10
  196.3 3.6 %collective-permute-done.8 = f32[8,4096]{1,0:T(8,128)S(1)} collective-permute-done((f32[8,4096]{1,0:T(8,128)S(1)}, f32[8,4096]{1,0:T(8,128)S(1)}, u32[]{:S(2)}, u32[]{:S(2)}) %collective-permute-start.8) | collective-permute-done | bytes 131104 | tf_op jit(solution)/shard_map/ppermute | solution.py:386
  199.9 1.6 collective-permute-start.9
  201.6 0.0 collective-permute-done.10
  201.6 0.1 collective-permute-start.11
  201.7 2.2 %shard_map.61 = (f32[32,64]{1,0:T(8,128)S(1)}, f32[16,16]{1,0:T(8,128)S(1)}, f32[16,16]{1,0:T(8,128)S(1)}) custom-call(f32[32,40,128]{2,1,0:T(8,128)S(1)} %all_to_all.39.got), custom_call_target="tpu_custom_call" | custom-call | tf_op jit(solution)/shard_map/pallas_call | solution.py:321
  203.9 1.7 collective-permute-done.9.t1
  205.6 0.2 collective-permute-done.11.b1
  205.8 1.4 shard_map.62
  207.1 12.7 %all_to_all.41.got = f32[32,8,128]{2,1,0:T(8,128)S(1)} all-to-all(f32[32,8,128]{2,1,0:T(8,128)S(1)} %get-tuple-element.61), channel_id=1, replica_groups=mesh['wide'=32,'narrow'=4] {'wide'}, dimensions={0} | all-to-all | bytes 262144 | tf_op jit(solution)/shard_map/all_to_all | solution.py:345
  219.8 3.2 %shard_map.63 = (f32[16,4096]{1,0:T(8,128)}, f32[3,2,16,16]{3,2,1,0:T(8,128)}) custom-call(f32[32,8,128]{2,1,0:T(8,128)S(1)} %all_to_all.41.got, f32[16,4096]{1,0:T(8,128)S(1)} %get-tuple-element.62.w0, f32[16,4096]{1,0:T(8,128)S(1)} %get-tuple-element.63.q, f32[16,16]{1,0:T(8,128)S(1)} %get-tuple-element.64.a0, f32[16,16]{1,0:T(8,128)S(1)} %get-tuple-element.65.l0, ...), custom_call_target="tpu_custom_call" | custom-call | tf_op jit(solution)/shard_map/pallas_call | solution.py:321
  (6 shorter events, 0.1 us)
Async XLA Ops:
  6.1 68.8 %copy-start = (bf16[32,144,256]{2,1,0:T(8,128)(2,1)S(1)}, bf16[32,144,256]{2,1,0:T(8,128)(2,1)}, u32[]{:S(2)}) copy-start(bf16[32,144,256]{2,1,0:T(8,128)(2,1)} %get-tuple-element.36.unit) | copy-start | bytes 7077892
  6.1 68.8 %copy-start.1 = (f32[16,4096]{1,0:T(8,128)S(1)}, f32[16,4096]{1,0:T(8,128)}, u32[]{:S(2)}) copy-start(f32[16,4096]{1,0:T(8,128)} %refs_0_.1) | copy-start | bytes 786436
  75.0 19.5 %copy-start.2 = (s32[2,64]{1,0:T(2,128)S(1)}, s32[2,64]{1,0:T(2,128)}, u32[]{:S(2)}) copy-start(s32[2,64]{1,0:T(2,128)} %pairs.13) | copy-start | bytes 1540
  95.4 5.3 %collective-permute-start = (f32[8,4096]{1,0:T(8,128)S(1)}, f32[8,4096]{1,0:T(8,128)S(1)}, u32[]{:S(2)}, u32[]{:S(2)}) collective-permute-start(f32[8,4096]{1,0:T(8,128)S(1)} %get-tuple-element.40), channel_id=1, source_target_pairs={{0,1},{1,0},{2,3},{3,2},{4,5},{5,4},{6,7},{7,6},{8,9},{9,8},{10,11... | collective-permute-start | bytes 393224 | tf_op jit(solution)/shard_map/ppermute | solution.py:386
  96.7 7.0 %collective-permute-start.2 = (f32[8,4096]{1,0:T(8,128)S(1)}, f32[8,4096]{1,0:T(8,128)S(1)}, u32[]{:S(2)}, u32[]{:S(2)}) collective-permute-start(f32[8,4096]{1,0:T(8,128)S(1)} %get-tuple-element.41), channel_id=1, source_target_pairs={{0,3},{1,2},{2,1},{3,0},{4,7},{5,6},{6,5},{7,4},{8,11},{9,10},{10,... | collective-permute-start | bytes 393224 | tf_op jit(solution)/shard_map/ppermute | solution.py:386
  100.8 6.1 %collective-permute-start.1 = (f32[8,4096]{1,0:T(8,128)S(1)}, f32[8,4096]{1,0:T(8,128)S(1)}, u32[]{:S(2)}, u32[]{:S(2)}) collective-permute-start(f32[8,4096]{1,0:T(8,128)S(1)} %add.18.t0), channel_id=1, source_target_pairs={{0,3},{1,2},{2,1},{3,0},{4,7},{5,6},{6,5},{7,4},{8,11},{9,10},{10,... | collective-permute-start | bytes 393224 | tf_op jit(solution)/shard_map/ppermute | solution.py:386
  103.7 4.0 %collective-permute-start.3 = (f32[8,4096]{1,0:T(8,128)S(1)}, f32[8,4096]{1,0:T(8,128)S(1)}, u32[]{:S(2)}, u32[]{:S(2)}) collective-permute-start(f32[8,4096]{1,0:T(8,128)S(1)} %add.19.b0), channel_id=1, source_target_pairs={{0,1},{1,0},{2,3},{3,2},{4,5},{5,4},{6,7},{7,6},{8,9},{9,8},{10,11... | collective-permute-start | bytes 393224 | tf_op jit(solution)/shard_map/ppermute | solution.py:386
  145.8 5.3 %collective-permute-start.4 = (f32[8,4096]{1,0:T(8,128)S(1)}, f32[8,4096]{1,0:T(8,128)S(1)}, u32[]{:S(2)}, u32[]{:S(2)}) collective-permute-start(f32[8,4096]{1,0:T(8,128)S(1)} %get-tuple-element.48), channel_id=1, source_target_pairs={{0,1},{1,0},{2,3},{3,2},{4,5},{5,4},{6,7},{7,6},{8,9},{9,8},{10,11... | collective-permute-start | bytes 393224 | tf_op jit(solution)/shard_map/ppermute | solution.py:386
  145.9 6.5 %collective-permute-start.6 = (f32[8,4096]{1,0:T(8,128)S(1)}, f32[8,4096]{1,0:T(8,128)S(1)}, u32[]{:S(2)}, u32[]{:S(2)}) collective-permute-start(f32[8,4096]{1,0:T(8,128)S(1)} %get-tuple-element.49), channel_id=1, source_target_pairs={{0,3},{1,2},{2,1},{3,0},{4,7},{5,6},{6,5},{7,4},{8,11},{9,10},{10,... | collective-permute-start | bytes 393224 | tf_op jit(solution)/shard_map/ppermute | solution.py:386
  151.2 5.7 %collective-permute-start.5 = (f32[8,4096]{1,0:T(8,128)S(1)}, f32[8,4096]{1,0:T(8,128)S(1)}, u32[]{:S(2)}, u32[]{:S(2)}) collective-permute-start(f32[8,4096]{1,0:T(8,128)S(1)} %add.20.t0), channel_id=1, source_target_pairs={{0,3},{1,2},{2,1},{3,0},{4,7},{5,6},{6,5},{7,4},{8,11},{9,10},{10,... | collective-permute-start | bytes 393224 | tf_op jit(solution)/shard_map/ppermute | solution.py:386
  152.4 4.4 %collective-permute-start.7 = (f32[8,4096]{1,0:T(8,128)S(1)}, f32[8,4096]{1,0:T(8,128)S(1)}, u32[]{:S(2)}, u32[]{:S(2)}) collective-permute-start(f32[8,4096]{1,0:T(8,128)S(1)} %add.21.b0), channel_id=1, source_target_pairs={{0,1},{1,0},{2,3},{3,2},{4,5},{5,4},{6,7},{7,6},{8,9},{9,8},{10,11... | collective-permute-start | bytes 393224 | tf_op jit(solution)/shard_map/ppermute | solution.py:386
  194.6 5.3 %collective-permute-start.8 = (f32[8,4096]{1,0:T(8,128)S(1)}, f32[8,4096]{1,0:T(8,128)S(1)}, u32[]{:S(2)}, u32[]{:S(2)}) collective-permute-start(f32[8,4096]{1,0:T(8,128)S(1)} %get-tuple-element.56), channel_id=1, source_target_pairs={{0,1},{1,0},{2,3},{3,2},{4,5},{5,4},{6,7},{7,6},{8,9},{9,8},{10,11... | collective-permute-start | bytes 393224 | tf_op jit(solution)/shard_map/ppermute | solution.py:386
  194.7 6.9 %collective-permute-start.10 = (f32[8,4096]{1,0:T(8,128)S(1)}, f32[8,4096]{1,0:T(8,128)S(1)}, u32[]{:S(2)}, u32[]{:S(2)}) collective-permute-start(f32[8,4096]{1,0:T(8,128)S(1)} %get-tuple-element.57), channel_id=1, source_target_pairs={{0,3},{1,2},{2,1},{3,0},{4,7},{5,6},{6,5},{7,4},{8,11},{9,10},{10,... | collective-permute-start | bytes 393224 | tf_op jit(solution)/shard_map/ppermute | solution.py:386
  199.9 5.7 %collective-permute-start.9 = (f32[8,4096]{1,0:T(8,128)S(1)}, f32[8,4096]{1,0:T(8,128)S(1)}, u32[]{:S(2)}, u32[]{:S(2)}) collective-permute-start(f32[8,4096]{1,0:T(8,128)S(1)} %add.22.t0), channel_id=1, source_target_pairs={{0,3},{1,2},{2,1},{3,0},{4,7},{5,6},{6,5},{7,4},{8,11},{9,10},{10,... | collective-permute-start | bytes 393224 | tf_op jit(solution)/shard_map/ppermute | solution.py:386
  201.6 4.2 %collective-permute-start.11 = (f32[8,4096]{1,0:T(8,128)S(1)}, f32[8,4096]{1,0:T(8,128)S(1)}, u32[]{:S(2)}, u32[]{:S(2)}) collective-permute-start(f32[8,4096]{1,0:T(8,128)S(1)} %add.23.b0), channel_id=1, source_target_pairs={{0,1},{1,0},{2,3},{3,2},{4,5},{5,4},{6,7},{7,6},{8,9},{9,8},{10,11... | collective-permute-start | bytes 393224 | tf_op jit(solution)/shard_map/ppermute | solution.py:386

commit v7 on v6

v7 whole, which is shorter than its diff:
```python
import functools

import jax
import jax.numpy as jnp
from jax import lax
from jax.experimental import pallas as pl
from jax.experimental.pallas import tpu as pltpu
from jax.sharding import PartitionSpec as P

BS = 128
STEPS = 3
KERNEL_FACTOR = 3.0
EPSILON = 1e-06
HIGH = lax.Precision.HIGHEST
VMEM_LIMIT = 16 * 2**20
VMEM_START = 60 * 2**20
VMEM_TILES = 30 * 2**20
TAIL = 8
CHUNKS = 8
BF = jnp.bfloat16
F32 = jnp.float32
NT = (((1,), (1,)), ((), ()))
TN = (((0,), (0,)), ((), ()))
NN = (((1,), (0,)), ((), ()))
cat = jnp.concatenate


def mm(a, b, dims):
    return lax.dot_general(a, b, dims, precision=HIGH, preferred_element_type=F32)


def mb(a, b, dims):
    return lax.dot_general(a, b, dims, preferred_element_type=F32)


def split(x):
    high = x.astype(BF)
    return high, (x - high.astype(F32)).astype(BF)


def block(i):
    return pl.ds(pl.multiple_of(i * BS, BS), BS)


def apply_small(m, x):
    rows = m.shape[0]
    m_high, m_low = split(m)
    left = cat([cat([m_high, m_high], axis=1), cat([m_low, jnp.zeros_like(m_low)], axis=1)], axis=0)
    out = mb(left, cat(split(x), axis=0), NN)
    return out[:rows] + out[rows:]


def factor_of(gram):
    n = gram.shape[0]
    rows = lax.broadcasted_iota(jnp.int32, (n, n), 0)
    cols = lax.broadcasted_iota(jnp.int32, (n, n), 1)
    same = (rows == cols).astype(F32)
    low, inverse, left = same, same, gram
    across, down = jnp.ones((1, n), F32), jnp.ones((n, 1), F32)
    for j in range(n):
        pivot = left[j : j + 1, j : j + 1]
        column = jnp.where(rows > j, left[:, j : j + 1] * (1.0 / pivot), 0.0)
        left = left - column * left[j : j + 1, :]
        inverse = inverse - column * inverse[j : j + 1, :]
        low = jnp.where(cols == j, low + column, low)
        across = jnp.where(cols[:1] == j, pivot, across)
        down = jnp.where(rows[:, :1] == j, pivot, down)
    return low * jnp.sqrt(across), inverse * (1.0 / jnp.sqrt(down))


def fold(q, w):
    n = q.shape[0]
    both = cat(split(cat([q, w], axis=0)), axis=0)
    g = mb(both, both, NT)
    g = g[: 2 * n, : 2 * n] + (g[: 2 * n, 2 * n :] + g[2 * n :, : 2 * n])
    parts = (g[:n, :n], g[:n, n:], g[n:, n:])
    pieces = [p[h : h + 8] for p in parts for h in (0, 8)]
    return cat(pieces + [jnp.zeros((8, BS - 6 * n), F32)], axis=1)


def sums_of(tails, points):
    t = jnp.sum(tails, axis=0) * (1.0 / points)
    return (cat([t[:, k : k + 16], t[:, k + 16 : k + 32]], axis=0) for k in (0, 32, 64))


def rest_gram(s, a, b):
    return b - mm(a, 2.0 * a - mm(s, a, NN), TN)


def step_matrices(tails, points):
    s, a, b = sums_of(tails, points)
    low, inverse = factor_of(rest_gram(s, a, b))
    return a, low, inverse, mm(inverse, a, NT)


def tile_stack(tile):
    return cat(split(tile), axis=0)


def first_term(stack, second):
    high, low = second
    rows = high.shape[0]
    a = mb(cat([high, low], axis=0), stack, NT)
    return a[:rows, :BS] + a[rows:, :BS] + a[:rows, BS:]


def second_term(stack, first):
    high, low = first
    rows = high.shape[0]
    left = cat([cat([high, high], axis=1), cat([low, jnp.zeros_like(low)], axis=1)], axis=0)
    b = mb(left, stack, NN)
    return b[:rows] + b[rows:]


def own_block(i, own_blocks):
    return lax.rem(i, own_blocks) if own_blocks & (own_blocks - 1) else i & (own_blocks - 1)


def start_kernel(wide, cap, own_blocks, pairs, points, q_in, unit_out, out, unit, raw, q, meta, sems, sem):
    vec_rows = q.shape[0]
    panels = raw.shape[1] // BS
    slot_rows = panels * BS + 2 * vec_rows
    size = raw.shape[0] // CHUNKS
    loads = [
        pltpu.make_async_copy(
            points.at[pl.ds(k * size, size), :], raw.at[pl.ds(k * size, size), :], sems.at[k]
        )
        for k in range(CHUNKS)
    ]
    loads.append(pltpu.make_async_copy(q_in, q, sems.at[CHUNKS]))
    for load in (loads[-1], *loads[:-1]):
        load.start()
    loads[-1].wait()
    high, low = split(q[...])
    for b in range(own_blocks):
        cols = slice(b * BS, (b + 1) * BS)
        unit[b, panels * BS :, :] = cat([high[:, cols], low[:, cols]], axis=0)
    half = own_blocks // 2
    for k in range(CHUNKS):
        loads[k].wait()
        for b in range(own_blocks // CHUNKS):
            x = raw[pl.ds(k * size + b * BS, BS), :].astype(F32)
            x = x * lax.rsqrt(jnp.sum(x * x, axis=-1, keepdims=True) + EPSILON)
            x = x.astype(BF)
            for h in range(panels):
                at = slice(h * BS, (h + 1) * BS)
                unit[k * (own_blocks // CHUNKS) + b, at, :] = x[:, at]
        if k % (CHUNKS // 2) != CHUNKS // 2 - 1:
            continue
        late = k == CHUNKS - 1

        def send(p, carry, late=late):
            for c in range(cap):
                i = own_block(pairs[0, p * cap + c], own_blocks)

                @pl.when((i >= half) == late)
                def _(i=i, c=c):
                    pltpu.make_async_copy(
                        unit.at[i], out.at[p, pl.ds(c * slot_rows, slot_rows), :], sem
                    ).start()

            return carry

        lax.fori_loop(0, wide, send, 0, unroll=8)
    keep = pltpu.make_async_copy(unit, unit_out, sems.at[CHUNKS + 1])
    keep.start()
    both = cat([high, low], axis=0)
    gram = mb(both, both, NT)
    gram = gram[:vec_rows, :vec_rows] + (gram[:vec_rows, vec_rows:] + gram[vec_rows:, :vec_rows])
    pieces = []
    for _ in range(3):
        pieces.append(gram.astype(BF).astype(F32))
        gram = gram - pieces[-1]
    sums = cat(pieces + [jnp.zeros((vec_rows, BS - 3 * vec_rows), F32)], axis=1)
    lanes = lax.broadcasted_iota(jnp.int32, sums.shape, 1)

    def label(p, carry):
        ids = [own_block(pairs[1, p * cap + c], own_blocks).astype(F32) for c in range(cap)]
        right = jnp.where(lanes < BS // 2 + BS // 4, ids[0], ids[1])
        meta[p] = jnp.where(lanes < BS // 2, sums, right).astype(BF)
        return carry

    lax.fori_loop(0, wide, label, 0, unroll=8)
    pltpu.make_async_copy(meta, out.at[:, pl.ds(cap * slot_rows, vec_rows), :], sem).start()
    pltpu.make_async_copy(out, out, sem).wait()
    keep.wait()


def put_terms(terms, ids, first_slot, cap, rows, back, total):
    for s, (to_first, to_second) in enumerate(terms):
        back[(first_slot + s) // cap, (s % cap) * rows : (s % cap + 1) * rows, :] = to_first
        total[:, block(ids[s])] += to_second


def tiles_kernel(peers, cap, sent, unit, q, tiles, back, total, gram, ids, got, labels, sems):
    wide = got.shape[0]
    vec_rows = q.shape[0]
    slot_rows = unit.shape[1]
    panels = (slot_rows - 2 * vec_rows) // BS
    slots = range(peers * cap)
    steps = wide // peers

    def load(k):
        part = pl.ds(k * peers, peers)
        here = pl.ds(0, cap * slot_rows)
        return pltpu.make_async_copy(sent.at[part, here], got.at[part], sems.at[k])

    first = pltpu.make_async_copy(
        sent.at[:, pl.ds(cap * slot_rows, vec_rows)], labels, sems.at[steps]
    )
    first.start()
    for k in range(steps):
        load(k).start()
    total[...] = jnp.zeros_like(total)
    first.wait()
    gram[...] = jnp.sum(labels[...].astype(F32), axis=0)
    for p in range(wide):
        label = labels[p].astype(F32)
        for c in range(cap):
            ids[p * cap + c] = label[0, BS // 2 + c * (BS // 4)].astype(jnp.int32)

    def chunk(k, carry):
        load(k).wait()
        peer = k * peers
        held = [ids[peer * cap + s] for s in slots]
        stacks = []
        for s in slots:
            at = (s % cap) * slot_rows
            here = [got[peer + s // cap, pl.ds(at + h * BS, BS), :] for h in range(panels)]
            own = [unit[held[s], h * BS : (h + 1) * BS, :] for h in range(panels)]
            inner = mb(cat(here, axis=1), cat(own, axis=1), NT)
            stacks.append(tile_stack(jnp.exp(KERNEL_FACTOR * (inner - 1.0))))
            tiles[peer * cap + s] = stacks[s]
        terms = []
        for s in slots:
            at = (s % cap) * slot_rows + panels * BS
            first = [got[peer + s // cap, pl.ds(at + h * vec_rows, vec_rows), :] for h in range(2)]
            second = split(q[:, block(held[s])])
            terms.append((first_term(stacks[s], second), second_term(stacks[s], first)))
        put_terms(terms, held, peer * cap, cap, vec_rows, back, total)
        return carry

    lax.fori_loop(0, steps, chunk, 0)


def gather_kernel(peers, cap, own_blocks, pairs, ids, got, tiles, top, low):
    half = top.shape[0]
    vec_rows = 2 * half
    slots = range(peers * cap)
    top[...] = jnp.zeros_like(top)
    low[...] = jnp.zeros_like(low)

    def put(at, term):
        top[:, at] += term[:half]
        low[:, at] += term[half:]

    def chunk(k, carry):
        peer = k * peers
        terms = []
        for s in slots:
            first = split(got[peer + s // cap, pl.ds((s % cap) * vec_rows, vec_rows), :])
            terms.append(second_term(tiles[peer * cap + s], first))
        for s in slots:
            put(block(ids[peer * cap + s]), terms[s])
            i = own_block(pairs[0, peer * cap + s], own_blocks)
            put(block(i), got[peer + s // cap, pl.ds((cap + s % cap) * vec_rows, vec_rows), :])
        return carry

    lax.fori_loop(0, got.shape[0] // peers, chunk, 0)


def sum_kernel(cap, own_blocks, pairs, got, total, top, low):
    vec_rows = total.shape[0]
    half = vec_rows // 2
    top[...] = total[:half]
    low[...] = total[half:]

    def add(p, carry):
        for c in range(cap):
            i = own_block(pairs[0, p * cap + c], own_blocks)
            top[:, block(i)] += got[p, c * vec_rows : c * vec_rows + half, :]
            low[:, block(i)] += got[p, c * vec_rows + half : (c + 1) * vec_rows, :]
        return carry

    lax.fori_loop(0, got.shape[0], add, 0, unroll=8)


def first_factor_kernel(points, gram, q_init, inverse, q):
    g = gram[...]
    n = q.shape[0]
    _, inv = factor_of((g[:, :n] + g[:, n : 2 * n] + g[:, 2 * n : 3 * n]) * (1.0 / points))
    inverse[...] = inv
    q[...] = apply_small(inv, q_init[...])


def factor_kernel(points, cap, got, w0, q, y, along, low_out, inverse, q_next, part, y_part):
    n = along.shape[0]
    a, low, inv, turned = step_matrices(got[:, 2 * cap * n :, :], points)
    along[...] = a
    low_out[...] = low
    inverse[...] = inv
    none = jnp.zeros_like(low)
    rows = lax.broadcasted_iota(jnp.int32, (n, n), 0)
    cols = lax.broadcasted_iota(jnp.int32, (n, n), 1)
    across = mm(-low, (rows == cols).astype(F32), TN)
    lines = [[inv, -turned, none], [none, none, -turned], [none, across, -turned]]
    matrix = cat([cat(line, axis=1) for line in lines], axis=0)
    new = apply_small(matrix, cat([w0[...], q[...], y[...]], axis=0))
    q_next[...] = new[:n]
    y_part[...] = new[n : 2 * n]
    part[...] = new[2 * n :]


def update_kernel(peers, cap, own_blocks, kept, pairs, ids, t0, t1, b0, b1, inverse, q, *refs):
    parts, rest = refs[:kept], refs[kept:]
    tiles, outs, out = (rest[0], rest[1:-1], rest[-1]) if cap else (None, rest[:-1], rest[-1])
    image = cat([t0[...] + t1[...], b0[...] + b1[...]], axis=0)
    n = image.shape[0]
    image = apply_small(inverse[...], image)
    w0 = outs[0]
    new = image + parts[0][...] if kept else image
    w0[...] = new
    if kept > 1:
        outs[1][...] = image + parts[1][...]
    tail = fold(q[...], new)
    if not cap:
        out[...] = jnp.broadcast_to(tail[None], out.shape)
        return

    def chunk(k, carry):
        peer = k * peers
        slots = range(peers * cap)
        terms = []
        for s in slots:
            second = split(w0[:, block(ids[peer * cap + s])])
            terms.append(first_term(tiles[peer * cap + s], second))
        for s in slots:
            p, c = peer + s // cap, s % cap
            i = own_block(pairs[0, peer * cap + s], own_blocks)
            out[p, c * n : (c + 1) * n, :] = w0[:, block(i)]
            out[p, (cap + c) * n : (cap + c + 1) * n, :] = terms[s]
        for p in range(peers):
            out[peer + p, 2 * cap * n :, :] = tail
        return carry

    lax.fori_loop(0, out.shape[0] // peers, chunk, 0)


def finish_kernel(points, got, w0, q, a0, l0, a1, l1, basis, coeffs):
    s, a, b = sums_of(got[...], points)
    n = a.shape[0]
    rows = lax.broadcasted_iota(jnp.int32, (n, n), 0)
    cols = lax.broadcasted_iota(jnp.int32, (n, n), 1)
    turned = mm(a, (rows == cols).astype(F32), TN)
    rest = w0[...] - apply_small(turned, q[...])
    low, inverse = factor_of(rest_gram(s, a, b))
    basis[...] = apply_small(inverse, rest)
    for k, m in enumerate((a0[...], l0[...], a1[...], l1[...], a, low)):
        coeffs[k // 2, k % 2] = m


def call(kernel, outs, n_ids=0, limit=VMEM_LIMIT, **more):
    params = pltpu.CompilerParams(vmem_limit_bytes=limit)
    shapes = tuple(jax.ShapeDtypeStruct(s, d) for s, d in outs)
    def run(*args):
        given = dict(more)
        vmem = pl.BlockSpec(memory_space=pltpu.VMEM)
        places = [pl.BlockSpec(memory_space=pltpu.SMEM)] * n_ids + [vmem] * (len(args) - n_ids)
        given.setdefault("in_specs", places)
        given.setdefault("out_specs", (vmem,) * len(outs))
        return pl.pallas_call(kernel, out_shape=shapes, compiler_params=params, **given)(*args)

    return run


def per_device(points, q_init, pairs):
    wide = lax.axis_size("wide")
    narrow = lax.axis_size("narrow")
    own_points, width = points.shape
    own_blocks = own_points // BS
    vec_rows = q_init.shape[0]
    pair_count = pairs.shape[1]
    cap = pair_count // wide
    total_points = own_points * wide
    slot_rows = width // BS * BS + 2 * vec_rows
    start_rows = cap * slot_rows + vec_rows
    peers = min(8, wide)
    vectors = ((vec_rows, own_points), F32)
    small = ((vec_rows, vec_rows), F32)
    payload = ((wide, 2 * cap * vec_rows + TAIL, BS), F32)
    reply = ((wide, cap * vec_rows, BS), F32)
    tail = ((wide, TAIL, BS), F32)

    def exchange(x):
        return lax.all_to_all(x, "wide", split_axis=0, concat_axis=0, tiled=True)

    anywhere = pl.BlockSpec(memory_space=pl.ANY)
    unit, sent = call(
        functools.partial(start_kernel, wide, cap, own_blocks),
        [((own_blocks, slot_rows, BS), BF), ((wide, start_rows, BS), BF)],
        1,
        VMEM_START,
        in_specs=[pl.BlockSpec(memory_space=pltpu.SMEM), anywhere, anywhere],
        out_specs=(anywhere, anywhere),
        scratch_shapes=[
            pltpu.VMEM((own_blocks, slot_rows, BS), BF),
            pltpu.VMEM((own_points, width), BF),
            pltpu.VMEM((vec_rows, own_points), F32),
            pltpu.VMEM((wide, vec_rows, BS), BF),
            pltpu.SemaphoreType.DMA((CHUNKS + 2,)),
            pltpu.SemaphoreType.DMA,
        ],
    )(pairs, points, q_init)
    vmem = pl.BlockSpec(memory_space=pltpu.VMEM)
    tiles, back, total, gram, ids = call(
        functools.partial(tiles_kernel, peers * 2, cap),
        [
            ((pair_count, 2 * BS, BS), BF),
            reply,
            vectors,
            ((vec_rows, BS), F32),
            ((pair_count,), jnp.int32),
        ],
        0,
        VMEM_TILES,
        in_specs=[anywhere, vmem, vmem],
        out_specs=(vmem, vmem, vmem, vmem, pl.BlockSpec(memory_space=pltpu.SMEM)),
        scratch_shapes=[
            pltpu.VMEM((wide, cap * slot_rows, BS), BF),
            pltpu.VMEM((wide, vec_rows, BS), BF),
            pltpu.SemaphoreType.DMA((wide // peers + 1,)),
        ],
    )(exchange(sent), unit, q_init)

    def swap(x, mask):
        return lax.ppermute(x, "narrow", [(i, i ^ mask) for i in range(narrow)])

    half = ((vec_rows // 2, own_points), F32)

    def narrow_sum(top, low):
        top_from, low_from = swap(top, 1), swap(low, 3)
        top, low = top + top_from, low + low_from
        return top, swap(top, 3), low, swap(low, 1)

    def update(kept, last, *args):
        count = max(kept, 1)
        return call(
            functools.partial(update_kernel, 4 * peers, 0 if last else cap, own_blocks, kept),
            [vectors] * count + [tail if last else payload],
            2,
        )(pairs, ids, *args, *([] if last else [tiles]))

    sums = narrow_sum(
        *call(functools.partial(sum_kernel, cap, own_blocks), [half, half], 1)(
            pairs, exchange(back), total
        )
    )
    inverse, q = call(
        functools.partial(first_factor_kernel, total_points), [small, vectors]
    )(gram, q_init)
    w0, out = update(0, False, *sums, inverse, q)
    y = w0
    records = []
    for step in range(1, STEPS):
        last = step == STEPS - 1
        got = exchange(out)
        sums = narrow_sum(
            *call(functools.partial(gather_kernel, 4 * peers, cap, own_blocks), [half, half], 2)(
                pairs, ids, got, tiles
            )
        )
        along, low, inverse, q, *parts = call(
            functools.partial(factor_kernel, total_points, cap),
            [small, small, small, vectors, vectors, vectors],
        )(got, w0, q, y)
        count = 1 if last else 2
        *new, out = update(count, last, *sums, inverse, q, *parts[:count])
        w0, y = new[0], new[-1]
        records += [along, low]
    return call(
        functools.partial(finish_kernel, total_points),
        [vectors, ((STEPS, 2, vec_rows, vec_rows), F32)],
    )(exchange(out), w0, q, *records)


def solution(mesh):
    placed = (P("wide", None), P(None, "wide"), P(None, ("wide", "narrow")))
    return jax.shard_map(
        per_device, mesh=mesh, in_specs=placed, out_specs=(P(None, "wide"), P()), check_vma=False
    )
```

time: 223 us -> 201 us (0.901)
  blocking collectives: 163 us -> 144 us
  waiting for transfers between devices: 16.2 us -> 12.1 us
    all_to_all x7 -> x5, blocking collectives: 163 us -> 144 us  [exchange(): return lax.all_to_all(x, 'wide', split_axis=0, concat_axis=0, tiled=True)]
    ppermute x12, waiting for transfers between devices: 16.2 us -> 12.1 us  [swap(): return lax.ppermute(x, 'narrow', [(i, i ^ mask) for i in range(narrow)])]
    pallas_call x14 -> x12, Pallas kernels: 30.9 us -> 30.1 us  [run(): pl.pallas_call(kernel, out_shape=shapes, compiler_params=params, **given)]
  transfers between devices with their start and end apart: 12 -> 12, of which waited for: 8 -> 9; matrix products, arithmetic and copies ran while one was open for 0% -> 0% of each run, Pallas kernels for 3% -> 4%
where the time goes in v7:
time: 201 us; the launch traced here: 200 us
  blocking collectives  144 us (72%)
  Pallas kernels  30.1 us (15%)
  starting transfers between devices  12.8 us (6%)
  waiting for transfers between devices  12.1 us (6%)
    all_to_all x5, blocking collectives, exchange(): return lax.all_to_all(x, 'wide', split_axis=0, concat_axis=0, tiled=True)  144 us
    pallas_call x12, Pallas kernels, run(): pl.pallas_call(kernel, out_shape=shapes, compiler_params=params, **given)  30.1 us
    ppermute x12, starting transfers between devices, swap(): return lax.ppermute(x, 'narrow', [(i, i ^ mask) for i in range(narrow)])  12.8 us
    ppermute x12, waiting for transfers between devices, swap(): return lax.ppermute(x, 'narrow', [(i, i ^ mask) for i in range(narrow)])  12.1 us
  transfers between devices with their start and end apart: 12, of which 9 were waited for; matrix products, arithmetic and copies ran while one was open for 0% of the time, Pallas kernels for 4%

profile of v7, /device:TPU:1, one launch (start us, length us, event | category | flops | bytes accessed | tf_op | source)
XLA Modules:
  0.0 200.2 jit_solution(12011195319380973736)
XLA Ops:
  0.6 5.4 %shard_map.50 = (bf16[32,288,128]{2,1,0:T(8,128)(2,1)}, bf16[32,592,128]{2,1,0:T(8,128)(2,1)}) custom-call(s32[2,64]{1,0:T(2,128)} %pairs.13, bf16[4096,256]{1,0:T(8,128)(2,1)} %points.1, f32[16,4096]{1,0:T(8,128)} %q_init.1), custom_call_target="tpu_custom_call" | custom-call | tf_op jit(solution)/shard_map/pallas_call | solution.py:371
  6.0 0.0 copy-start
  6.0 0.0 copy-start.1
  6.0 67.5 %all_to_all.25.sent = bf16[32,592,128]{2,1,0:T(8,128)(2,1)S(1)} all-to-all(bf16[32,592,128]{2,1,0:T(8,128)(2,1)} %get-tuple-element.35), channel_id=1, replica_groups=mesh['wide'=32,'narrow'=4] {'wide'}, dimensions={0} | all-to-all | bytes 9699328 | tf_op jit(solution)/shard_map/all_to_all | solution.py:395
  73.5 0.0 copy-done
  73.5 0.0 copy-done.1
  73.6 0.0 copy-start.2
  73.6 4.4 %shard_map.51 = (bf16[64,256,128]{2,1,0:T(8,128)(2,1)S(1)}, f32[32,32,128]{2,1,0:T(8,128)S(1)}, f32[16,4096]{1,0:T(8,128)S(1)}, f32[16,128]{1,0:T(8,128)S(1)}, s32[64]{0:T(128)S(1)}) custom-call(bf16[32,592,128]{2,1,0:T(8,128)(2,1)S(1)} %all_to_all.25.sent, bf16[32,288,128]{2,1,0:T(8,128)(2,1)S(1)} %copy-done, f32[16,4096]{1,0:T(8,128)S(1)} %copy-done.1), custom_call_target="tpu_custom_call" | custom-call | tf_op jit(solution)/shard_map/pallas_call | solution.py:371
  77.9 15.2 %all_to_all.26.got = f32[32,32,128]{2,1,0:T(8,128)S(1)} all-to-all(f32[32,32,128]{2,1,0:T(8,128)S(1)} %get-tuple-element.38), channel_id=1, replica_groups=mesh['wide'=32,'narrow'=4] {'wide'}, dimensions={0} | all-to-all | bytes 1048576 | tf_op jit(solution)/shard_map/all_to_all | solution.py:395
  93.1 0.0 copy-done.2
  93.1 0.9 shard_map.52
  94.0 1.5 collective-permute-start
  95.5 1.9 collective-permute-start.2
  97.4 2.0 collective-permute-done
  99.3 2.7 %collective-permute-start.1 = (f32[8,4096]{1,0:T(8,128)S(1)}, f32[8,4096]{1,0:T(8,128)S(1)}, u32[]{:S(2)}, u32[]{:S(2)}) collective-permute-start(f32[8,4096]{1,0:T(8,128)S(1)} %add.18.t0), channel_id=1, source_target_pairs={{0,3},{1,2},{2,1},{3,0},{4,7},{5,6},{6,5},{7,4},{8,11},{9,10},{10,... | collective-permute-start | bytes 393224 | tf_op jit(solution)/shard_map/ppermute | solution.py:436
  102.1 0.0 collective-permute-done.2
  102.1 0.1 collective-permute-start.3
  102.2 1.7 shard_map.53
  103.9 1.1 collective-permute-done.1.t1
  105.0 1.1 collective-permute-done.3.b1
  106.1 2.1 %shard_map.54 = (f32[16,4096]{1,0:T(8,128)S(1)}, f32[32,72,128]{2,1,0:T(8,128)S(1)}) custom-call(s32[2,64]{1,0:T(2,128)S(1)} %copy-done.2, s32[64]{0:T(128)S(1)} %get-tuple-element.37.ids, f32[8,4096]{1,0:T(8,128)S(1)} %add.18.t0, f32[8,4096]{1,0:T(8,128)S(1)} %collective-permute-done.1.t1, f32[8,4096]{1,0:T(8,128)S(1)} %add.19.b0, ...), custom_call_target="tpu_custom_call" | custom-call | tf_op jit(solution)/shard_map/pallas_call | solution.py:371
  108.3 24.1 %all_to_all.27.got = f32[32,72,128]{2,1,0:T(8,128)S(1)} all-to-all(f32[32,72,128]{2,1,0:T(8,128)S(1)} %get-tuple-element.46), channel_id=1, replica_groups=mesh['wide'=32,'narrow'=4] {'wide'}, dimensions={0} | all-to-all | bytes 2359296 | tf_op jit(solution)/shard_map/all_to_all | solution.py:395
  132.4 1.4 shard_map.55
  133.8 0.1 collective-permute-start.4
  133.9 1.5 collective-permute-start.6
  135.4 3.2 %collective-permute-done.4 = f32[8,4096]{1,0:T(8,128)S(1)} collective-permute-done((f32[8,4096]{1,0:T(8,128)S(1)}, f32[8,4096]{1,0:T(8,128)S(1)}, u32[]{:S(2)}, u32[]{:S(2)}) %collective-permute-start.4) | collective-permute-done | bytes 131104 | tf_op jit(solution)/shard_map/ppermute | solution.py:436
  138.5 1.5 collective-permute-start.5
  140.1 0.0 collective-permute-done.6
  140.1 0.1 collective-permute-start.7
  140.2 2.7 %shard_map.56 = (f32[16,16]{1,0:T(8,128)S(1)}, f32[16,16]{1,0:T(8,128)S(1)}, f32[16,16]{1,0:T(8,128)S(1)}, f32[16,4096]{1,0:T(8,128)S(1)}, f32[16,4096]{1,0:T(8,128)S(1)}, /*index=5*/f32[16,4096]{1,0:T(8,128)S(1)}) custom-call(f32[32,72,128]{2,1,0:T(8,128)S(1)} %all_to_all.27.got, f32[16,4096]{1,0:T(8,128)S(1)} %get-tuple-element.49.w0.y, ...), custom_call_target="tpu_custom_call" | custom-call | tf_op jit(solution)/shard_map/pallas_call | solution.py:371
  142.8 0.8 collective-permute-done.5.t1
  143.7 0.6 collective-permute-done.7.b1
  144.3 2.1 %shard_map.57 = (f32[16,4096]{1,0:T(8,128)S(1)}, f32[16,4096]{1,0:T(8,128)S(1)}, f32[32,72,128]{2,1,0:T(8,128)S(1)}) custom-call(s32[2,64]{1,0:T(2,128)S(1)} %copy-done.2, s32[64]{0:T(128)S(1)} %get-tuple-element.37.ids, f32[8,4096]{1,0:T(8,128)S(1)} %add.20.t0, f32[8,4096]{1,0:T(8,128)S(1)} %collective-permute-done.5.t1, f32[8,4096]{1,0:T(8,128)S(1)} %add.21.b0, ...), custom_call_target="tpu_custom_call" | custom-call | tf_op jit(solution)/shard_map/pallas_call | solution.py:371
  146.4 24.3 %all_to_all.28.got = f32[32,72,128]{2,1,0:T(8,128)S(1)} all-to-all(f32[32,72,128]{2,1,0:T(8,128)S(1)} %get-tuple-element.54), channel_id=1, replica_groups=mesh['wide'=32,'narrow'=4] {'wide'}, dimensions={0} | all-to-all | bytes 2359296 | tf_op jit(solution)/shard_map/all_to_all | solution.py:395
  170.8 1.4 shard_map.58
  172.2 0.5 collective-permute-start.8
  172.7 1.4 collective-permute-start.10
  174.1 2.8 %collective-permute-done.8 = f32[8,4096]{1,0:T(8,128)S(1)} collective-permute-done((f32[8,4096]{1,0:T(8,128)S(1)}, f32[8,4096]{1,0:T(8,128)S(1)}, u32[]{:S(2)}, u32[]{:S(2)}) %collective-permute-start.8) | collective-permute-done | bytes 131104 | tf_op jit(solution)/shard_map/ppermute | solution.py:436
  176.9 1.3 collective-permute-start.9
  178.3 0.0 collective-permute-done.10
  178.3 0.1 collective-permute-start.11
  178.4 3.4 %shard_map.59 = (f32[16,16]{1,0:T(8,128)S(1)}, f32[16,16]{1,0:T(8,128)S(1)}, f32[16,16]{1,0:T(8,128)S(1)}, f32[16,4096]{1,0:T(8,128)S(1)}, f32[16,4096]{1,0:T(8,128)S(1)}, /*index=5*/f32[16,4096]{1,0:T(8,128)}) custom-call(f32[32,72,128]{2,1,0:T(8,128)S(1)} %all_to_all.28.got, f32[16,4096]{1,0:T(8,128)S(1)} %get-tuple-element.57.w0, ...), custom_call_target="tpu_custom_call" | custom-call | tf_op jit(solution)/shard_map/pallas_call | solution.py:371
  181.8 0.3 collective-permute-done.9.t1
  182.1 0.1 collective-permute-done.11.b1
  182.2 1.3 shard_map.60
  183.5 13.4 %all_to_all.29.got = f32[32,8,128]{2,1,0:T(8,128)S(1)} all-to-all(f32[32,8,128]{2,1,0:T(8,128)S(1)} %get-tuple-element.62), channel_id=1, replica_groups=mesh['wide'=32,'narrow'=4] {'wide'}, dimensions={0} | all-to-all | bytes 262144 | tf_op jit(solution)/shard_map/all_to_all | solution.py:395
  196.9 3.4 %shard_map.61 = (f32[16,4096]{1,0:T(8,128)}, f32[3,2,16,16]{3,2,1,0:T(8,128)}) custom-call(f32[32,8,128]{2,1,0:T(8,128)S(1)} %all_to_all.29.got, f32[16,4096]{1,0:T(8,128)S(1)} %get-tuple-element.63.w0, f32[16,4096]{1,0:T(8,128)S(1)} %get-tuple-element.60.q, f32[16,16]{1,0:T(8,128)S(1)} %get-tuple-element.64.a0, f32[16,16]{1,0:T(8,128)S(1)} %get-tuple-element.65.l0, ...), custom_call_target="tpu_custom_call" | custom-call | tf_op jit(solution)/shard_map/pallas_call | solution.py:371
  (6 shorter events, 0.1 us)
Async XLA Ops:
  6.0 67.5 %copy-start = (bf16[32,288,128]{2,1,0:T(8,128)(2,1)S(1)}, bf16[32,288,128]{2,1,0:T(8,128)(2,1)}, u32[]{:S(2)}) copy-start(bf16[32,288,128]{2,1,0:T(8,128)(2,1)} %get-tuple-element.36.unit) | copy-start | bytes 7077892
  6.0 67.5 %copy-start.1 = (f32[16,4096]{1,0:T(8,128)S(1)}, f32[16,4096]{1,0:T(8,128)}, u32[]{:S(2)}) copy-start(f32[16,4096]{1,0:T(8,128)} %q_init.1) | copy-start | bytes 786436
  73.6 19.6 %copy-start.2 = (s32[2,64]{1,0:T(2,128)S(1)}, s32[2,64]{1,0:T(2,128)}, u32[]{:S(2)}) copy-start(s32[2,64]{1,0:T(2,128)} %pairs.13) | copy-start | bytes 1540
  94.0 5.3 %collective-permute-start = (f32[8,4096]{1,0:T(8,128)S(1)}, f32[8,4096]{1,0:T(8,128)S(1)}, u32[]{:S(2)}, u32[]{:S(2)}) collective-permute-start(f32[8,4096]{1,0:T(8,128)S(1)} %get-tuple-element.40), channel_id=1, source_target_pairs={{0,1},{1,0},{2,3},{3,2},{4,5},{5,4},{6,7},{7,6},{8,9},{9,8},{10,11... | collective-permute-start | bytes 393224 | tf_op jit(solution)/shard_map/ppermute | solution.py:436
  95.5 6.6 %collective-permute-start.2 = (f32[8,4096]{1,0:T(8,128)S(1)}, f32[8,4096]{1,0:T(8,128)S(1)}, u32[]{:S(2)}, u32[]{:S(2)}) collective-permute-start(f32[8,4096]{1,0:T(8,128)S(1)} %get-tuple-element.41), channel_id=1, source_target_pairs={{0,3},{1,2},{2,1},{3,0},{4,7},{5,6},{6,5},{7,4},{8,11},{9,10},{10,... | collective-permute-start | bytes 393224 | tf_op jit(solution)/shard_map/ppermute | solution.py:436
  99.3 5.7 %collective-permute-start.1 = (f32[8,4096]{1,0:T(8,128)S(1)}, f32[8,4096]{1,0:T(8,128)S(1)}, u32[]{:S(2)}, u32[]{:S(2)}) collective-permute-start(f32[8,4096]{1,0:T(8,128)S(1)} %add.18.t0), channel_id=1, source_target_pairs={{0,3},{1,2},{2,1},{3,0},{4,7},{5,6},{6,5},{7,4},{8,11},{9,10},{10,... | collective-permute-start | bytes 393224 | tf_op jit(solution)/shard_map/ppermute | solution.py:436
  102.1 4.0 %collective-permute-start.3 = (f32[8,4096]{1,0:T(8,128)S(1)}, f32[8,4096]{1,0:T(8,128)S(1)}, u32[]{:S(2)}, u32[]{:S(2)}) collective-permute-start(f32[8,4096]{1,0:T(8,128)S(1)} %add.19.b0), channel_id=1, source_target_pairs={{0,1},{1,0},{2,3},{3,2},{4,5},{5,4},{6,7},{7,6},{8,9},{9,8},{10,11... | collective-permute-start | bytes 393224 | tf_op jit(solution)/shard_map/ppermute | solution.py:436
  133.8 4.8 %collective-permute-start.4 = (f32[8,4096]{1,0:T(8,128)S(1)}, f32[8,4096]{1,0:T(8,128)S(1)}, u32[]{:S(2)}, u32[]{:S(2)}) collective-permute-start(f32[8,4096]{1,0:T(8,128)S(1)} %get-tuple-element.47), channel_id=1, source_target_pairs={{0,1},{1,0},{2,3},{3,2},{4,5},{5,4},{6,7},{7,6},{8,9},{9,8},{10,11... | collective-permute-start | bytes 393224 | tf_op jit(solution)/shard_map/ppermute | solution.py:436
  133.9 6.2 %collective-permute-start.6 = (f32[8,4096]{1,0:T(8,128)S(1)}, f32[8,4096]{1,0:T(8,128)S(1)}, u32[]{:S(2)}, u32[]{:S(2)}) collective-permute-start(f32[8,4096]{1,0:T(8,128)S(1)} %get-tuple-element.48), channel_id=1, source_target_pairs={{0,3},{1,2},{2,1},{3,0},{4,7},{5,6},{6,5},{7,4},{8,11},{9,10},{10,... | collective-permute-start | bytes 393224 | tf_op jit(solution)/shard_map/ppermute | solution.py:436
  138.5 5.1 %collective-permute-start.5 = (f32[8,4096]{1,0:T(8,128)S(1)}, f32[8,4096]{1,0:T(8,128)S(1)}, u32[]{:S(2)}, u32[]{:S(2)}) collective-permute-start(f32[8,4096]{1,0:T(8,128)S(1)} %add.20.t0), channel_id=1, source_target_pairs={{0,3},{1,2},{2,1},{3,0},{4,7},{5,6},{6,5},{7,4},{8,11},{9,10},{10,... | collective-permute-start | bytes 393224 | tf_op jit(solution)/shard_map/ppermute | solution.py:436
  140.1 4.2 %collective-permute-start.7 = (f32[8,4096]{1,0:T(8,128)S(1)}, f32[8,4096]{1,0:T(8,128)S(1)}, u32[]{:S(2)}, u32[]{:S(2)}) collective-permute-start(f32[8,4096]{1,0:T(8,128)S(1)} %add.21.b0), channel_id=1, source_target_pairs={{0,1},{1,0},{2,3},{3,2},{4,5},{5,4},{6,7},{7,6},{8,9},{9,8},{10,11... | collective-permute-start | bytes 393224 | tf_op jit(solution)/shard_map/ppermute | solution.py:436
  172.2 4.8 %collective-permute-start.8 = (f32[8,4096]{1,0:T(8,128)S(1)}, f32[8,4096]{1,0:T(8,128)S(1)}, u32[]{:S(2)}, u32[]{:S(2)}) collective-permute-start(f32[8,4096]{1,0:T(8,128)S(1)} %get-tuple-element.55), channel_id=1, source_target_pairs={{0,1},{1,0},{2,3},{3,2},{4,5},{5,4},{6,7},{7,6},{8,9},{9,8},{10,11... | collective-permute-start | bytes 393224 | tf_op jit(solution)/shard_map/ppermute | solution.py:436
  172.7 5.6 %collective-permute-start.10 = (f32[8,4096]{1,0:T(8,128)S(1)}, f32[8,4096]{1,0:T(8,128)S(1)}, u32[]{:S(2)}, u32[]{:S(2)}) collective-permute-start(f32[8,4096]{1,0:T(8,128)S(1)} %get-tuple-element.56), channel_id=1, source_target_pairs={{0,3},{1,2},{2,1},{3,0},{4,7},{5,6},{6,5},{7,4},{8,11},{9,10},{10,... | collective-permute-start | bytes 393224 | tf_op jit(solution)/shard_map/ppermute | solution.py:436
  176.9 5.1 %collective-permute-start.9 = (f32[8,4096]{1,0:T(8,128)S(1)}, f32[8,4096]{1,0:T(8,128)S(1)}, u32[]{:S(2)}, u32[]{:S(2)}) collective-permute-start(f32[8,4096]{1,0:T(8,128)S(1)} %add.22.t0), channel_id=1, source_target_pairs={{0,3},{1,2},{2,1},{3,0},{4,7},{5,6},{6,5},{7,4},{8,11},{9,10},{10,... | collective-permute-start | bytes 393224 | tf_op jit(solution)/shard_map/ppermute | solution.py:436
  178.3 3.9 %collective-permute-start.11 = (f32[8,4096]{1,0:T(8,128)S(1)}, f32[8,4096]{1,0:T(8,128)S(1)}, u32[]{:S(2)}, u32[]{:S(2)}) collective-permute-start(f32[8,4096]{1,0:T(8,128)S(1)} %add.23.b0), channel_id=1, source_target_pairs={{0,1},{1,0},{2,3},{3,2},{4,5},{5,4},{6,7},{7,6},{8,9},{9,8},{10,11... | collective-permute-start | bytes 393224 | tf_op jit(solution)/shard_map/ppermute | solution.py:436

commit v8 on v7

--- a/solution.py
+++ b/solution.py
@@ -16,7 +16,7 @@
 VMEM_START = 60 * 2**20
 VMEM_TILES = 30 * 2**20
 TAIL = 8
-CHUNKS = 8
+CHUNKS = 4
 BF = jnp.bfloat16
 F32 = jnp.float32
 NT = (((1,), (1,)), ((), ()))
@@ -192,7 +192,7 @@
         total[:, block(ids[s])] += to_second
 
 
-def tiles_kernel(peers, cap, sent, unit, q, tiles, back, total, gram, ids, got, labels, sems):
+def tiles_kernel(peers, cap, got, unit, q, tiles, back, total, gram, ids):
     wide = got.shape[0]
     vec_rows = q.shape[0]
     slot_rows = unit.shape[1]
@@ -200,19 +200,8 @@
     slots = range(peers * cap)
     steps = wide // peers
 
-    def load(k):
-        part = pl.ds(k * peers, peers)
-        here = pl.ds(0, cap * slot_rows)
-        return pltpu.make_async_copy(sent.at[part, here], got.at[part], sems.at[k])
-
-    first = pltpu.make_async_copy(
-        sent.at[:, pl.ds(cap * slot_rows, vec_rows)], labels, sems.at[steps]
-    )
-    first.start()
-    for k in range(steps):
-        load(k).start()
     total[...] = jnp.zeros_like(total)
-    first.wait()
+    labels = got.at[:, pl.ds(cap * slot_rows, vec_rows), :]
     gram[...] = jnp.sum(labels[...].astype(F32), axis=0)
     for p in range(wide):
         label = labels[p].astype(F32)
@@ -220,7 +209,6 @@
             ids[p * cap + c] = label[0, BS // 2 + c * (BS // 4)].astype(jnp.int32)
 
     def chunk(k, carry):
-        load(k).wait()
         peer = k * peers
         held = [ids[peer * cap + s] for s in slots]
         stacks = []
@@ -413,7 +401,7 @@
     )(pairs, points, q_init)
     vmem = pl.BlockSpec(memory_space=pltpu.VMEM)
     tiles, back, total, gram, ids = call(
-        functools.partial(tiles_kernel, peers * 2, cap),
+        functools.partial(tiles_kernel, peers * 4, cap),
         [
             ((pair_count, 2 * BS, BS), BF),
             reply,
@@ -423,13 +411,8 @@
         ],
         0,
         VMEM_TILES,
-        in_specs=[anywhere, vmem, vmem],
+        in_specs=[vmem, vmem, vmem],
         out_specs=(vmem, vmem, vmem, vmem, pl.BlockSpec(memory_space=pltpu.SMEM)),
-        scratch_shapes=[
-            pltpu.VMEM((wide, cap * slot_rows, BS), BF),
-            pltpu.VMEM((wide, vec_rows, BS), BF),
-            pltpu.SemaphoreType.DMA((wide // peers + 1,)),
-        ],
     )(exchange(sent), unit, q_init)
 
     def swap(x, mask):

time: 201 us -> 200 us (level)
  no operation moved by 1% of the time
where the time goes in v8:
time: 200 us
  blocking collectives  144 us (72%)
  Pallas kernels  29.3 us (15%)
  starting transfers between devices  12.8 us (6%)
  waiting for transfers between devices  12.6 us (6%)
    all_to_all x5, blocking collectives, exchange(): return lax.all_to_all(x, 'wide', split_axis=0, concat_axis=0, tiled=True)  144 us
    pallas_call x12, Pallas kernels, run(): pl.pallas_call(kernel, out_shape=shapes, compiler_params=params, **given)  29.3 us
    ppermute x12, starting transfers between devices, swap(): return lax.ppermute(x, 'narrow', [(i, i ^ mask) for i in range(narrow)])  12.8 us
    ppermute x12, waiting for transfers between devices, swap(): return lax.ppermute(x, 'narrow', [(i, i ^ mask) for i in range(narrow)])  12.6 us
  transfers between devices with their start and end apart: 12, of which 9 were waited for; matrix products, arithmetic and copies ran while one was open for 0% of the time, Pallas kernels for 4%

profile of v8, /device:TPU:1, one launch (start us, length us, event | category | flops | bytes accessed | tf_op | source)
XLA Modules:
  0.0 199.6 jit_solution(8236446033357821374)
XLA Ops:
  0.6 5.3 %shard_map.50 = (bf16[32,288,128]{2,1,0:T(8,128)(2,1)}, bf16[32,592,128]{2,1,0:T(8,128)(2,1)}) custom-call(s32[2,64]{1,0:T(2,128)} %pairs.13, bf16[4096,256]{1,0:T(8,128)(2,1)} %points.1, f32[16,4096]{1,0:T(8,128)} %q_init.1), custom_call_target="tpu_custom_call" | custom-call | tf_op jit(solution)/shard_map/pallas_call | solution.py:359
  5.9 0.0 copy-start
  5.9 0.0 copy-start.1
  5.9 67.4 %all_to_all.25.got = bf16[32,592,128]{2,1,0:T(8,128)(2,1)S(1)} all-to-all(bf16[32,592,128]{2,1,0:T(8,128)(2,1)} %get-tuple-element.35), channel_id=1, replica_groups=mesh['wide'=32,'narrow'=4] {'wide'}, dimensions={0} | all-to-all | bytes 9699328 | tf_op jit(solution)/shard_map/all_to_all | solution.py:383
  73.3 0.0 copy-done
  73.3 0.0 copy-done.1
  73.3 0.0 copy-start.2
  73.4 3.7 %shard_map.51 = (bf16[64,256,128]{2,1,0:T(8,128)(2,1)S(1)}, f32[32,32,128]{2,1,0:T(8,128)S(1)}, f32[16,4096]{1,0:T(8,128)S(1)}, f32[16,128]{1,0:T(8,128)S(1)}, s32[64]{0:T(128)S(1)}) custom-call(bf16[32,592,128]{2,1,0:T(8,128)(2,1)S(1)} %all_to_all.25.got, bf16[32,288,128]{2,1,0:T(8,128)(2,1)S(1)} %copy-done, f32[16,4096]{1,0:T(8,128)S(1)} %copy-done.1), custom_call_target="tpu_custom_call" | custom-call | tf_op jit(solution)/shard_map/pallas_call | solution.py:359
  77.1 15.1 %all_to_all.26.got = f32[32,32,128]{2,1,0:T(8,128)S(1)} all-to-all(f32[32,32,128]{2,1,0:T(8,128)S(1)} %get-tuple-element.38), channel_id=1, replica_groups=mesh['wide'=32,'narrow'=4] {'wide'}, dimensions={0} | all-to-all | bytes 1048576 | tf_op jit(solution)/shard_map/all_to_all | solution.py:383
  92.2 0.0 copy-done.2
  92.2 0.9 shard_map.52
  93.1 1.4 collective-permute-start
  94.5 1.9 collective-permute-start.2
  96.4 2.0 %collective-permute-done = f32[8,4096]{1,0:T(8,128)S(1)} collective-permute-done((f32[8,4096]{1,0:T(8,128)S(1)}, f32[8,4096]{1,0:T(8,128)S(1)}, u32[]{:S(2)}, u32[]{:S(2)}) %collective-permute-start) | collective-permute-done | bytes 131104 | tf_op jit(solution)/shard_map/ppermute | solution.py:419
  98.4 2.8 %collective-permute-start.1 = (f32[8,4096]{1,0:T(8,128)S(1)}, f32[8,4096]{1,0:T(8,128)S(1)}, u32[]{:S(2)}, u32[]{:S(2)}) collective-permute-start(f32[8,4096]{1,0:T(8,128)S(1)} %add.18.t0), channel_id=1, source_target_pairs={{0,3},{1,2},{2,1},{3,0},{4,7},{5,6},{6,5},{7,4},{8,11},{9,10},{10,... | collective-permute-start | bytes 393224 | tf_op jit(solution)/shard_map/ppermute | solution.py:419
  101.3 0.0 collective-permute-done.2
  101.3 0.1 collective-permute-start.3
  101.4 1.7 shard_map.53
  103.1 1.2 collective-permute-done.1.t1
  104.3 1.0 collective-permute-done.3.b1
  105.3 2.1 %shard_map.54 = (f32[16,4096]{1,0:T(8,128)S(1)}, f32[32,72,128]{2,1,0:T(8,128)S(1)}) custom-call(s32[2,64]{1,0:T(2,128)S(1)} %copy-done.2, s32[64]{0:T(128)S(1)} %get-tuple-element.37.ids, f32[8,4096]{1,0:T(8,128)S(1)} %add.18.t0, f32[8,4096]{1,0:T(8,128)S(1)} %collective-permute-done.1.t1, f32[8,4096]{1,0:T(8,128)S(1)} %add.19.b0, ...), custom_call_target="tpu_custom_call" | custom-call | tf_op jit(solution)/shard_map/pallas_call | solution.py:359
  107.5 24.1 %all_to_all.27.got = f32[32,72,128]{2,1,0:T(8,128)S(1)} all-to-all(f32[32,72,128]{2,1,0:T(8,128)S(1)} %get-tuple-element.46), channel_id=1, replica_groups=mesh['wide'=32,'narrow'=4] {'wide'}, dimensions={0} | all-to-all | bytes 2359296 | tf_op jit(solution)/shard_map/all_to_all | solution.py:383
  131.6 1.4 shard_map.55
  133.0 0.1 collective-permute-start.4
  133.0 1.3 collective-permute-start.6
  134.4 3.3 %collective-permute-done.4 = f32[8,4096]{1,0:T(8,128)S(1)} collective-permute-done((f32[8,4096]{1,0:T(8,128)S(1)}, f32[8,4096]{1,0:T(8,128)S(1)}, u32[]{:S(2)}, u32[]{:S(2)}) %collective-permute-start.4) | collective-permute-done | bytes 131104 | tf_op jit(solution)/shard_map/ppermute | solution.py:419
  137.7 1.3 collective-permute-start.5
  139.1 0.0 collective-permute-done.6
  139.1 0.3 collective-permute-start.7
  139.4 2.7 %shard_map.56 = (f32[16,16]{1,0:T(8,128)S(1)}, f32[16,16]{1,0:T(8,128)S(1)}, f32[16,16]{1,0:T(8,128)S(1)}, f32[16,4096]{1,0:T(8,128)S(1)}, f32[16,4096]{1,0:T(8,128)S(1)}, /*index=5*/f32[16,4096]{1,0:T(8,128)S(1)}) custom-call(f32[32,72,128]{2,1,0:T(8,128)S(1)} %all_to_all.27.got, f32[16,4096]{1,0:T(8,128)S(1)} %get-tuple-element.49.w0.y, ...), custom_call_target="tpu_custom_call" | custom-call | tf_op jit(solution)/shard_map/pallas_call | solution.py:359
  142.0 0.8 collective-permute-done.5.t1
  142.8 0.6 collective-permute-done.7.b1
  143.5 2.1 %shard_map.57 = (f32[16,4096]{1,0:T(8,128)S(1)}, f32[16,4096]{1,0:T(8,128)S(1)}, f32[32,72,128]{2,1,0:T(8,128)S(1)}) custom-call(s32[2,64]{1,0:T(2,128)S(1)} %copy-done.2, s32[64]{0:T(128)S(1)} %get-tuple-element.37.ids, f32[8,4096]{1,0:T(8,128)S(1)} %add.20.t0, f32[8,4096]{1,0:T(8,128)S(1)} %collective-permute-done.5.t1, f32[8,4096]{1,0:T(8,128)S(1)} %add.21.b0, ...), custom_call_target="tpu_custom_call" | custom-call | tf_op jit(solution)/shard_map/pallas_call | solution.py:359
  145.6 24.3 %all_to_all.28.got = f32[32,72,128]{2,1,0:T(8,128)S(1)} all-to-all(f32[32,72,128]{2,1,0:T(8,128)S(1)} %get-tuple-element.54), channel_id=1, replica_groups=mesh['wide'=32,'narrow'=4] {'wide'}, dimensions={0} | all-to-all | bytes 2359296 | tf_op jit(solution)/shard_map/all_to_all | solution.py:383
  170.0 1.4 shard_map.58
  171.4 0.7 collective-permute-start.8
  172.0 1.3 collective-permute-start.10
  173.3 2.8 %collective-permute-done.8 = f32[8,4096]{1,0:T(8,128)S(1)} collective-permute-done((f32[8,4096]{1,0:T(8,128)S(1)}, f32[8,4096]{1,0:T(8,128)S(1)}, u32[]{:S(2)}, u32[]{:S(2)}) %collective-permute-start.8) | collective-permute-done | bytes 131104 | tf_op jit(solution)/shard_map/ppermute | solution.py:419
  176.2 1.5 collective-permute-start.9
  177.7 0.0 collective-permute-done.10
  177.7 0.1 collective-permute-start.11
  177.8 3.4 %shard_map.59 = (f32[16,16]{1,0:T(8,128)S(1)}, f32[16,16]{1,0:T(8,128)S(1)}, f32[16,16]{1,0:T(8,128)S(1)}, f32[16,4096]{1,0:T(8,128)S(1)}, f32[16,4096]{1,0:T(8,128)S(1)}, /*index=5*/f32[16,4096]{1,0:T(8,128)}) custom-call(f32[32,72,128]{2,1,0:T(8,128)S(1)} %all_to_all.28.got, f32[16,4096]{1,0:T(8,128)S(1)} %get-tuple-element.57.w0, ...), custom_call_target="tpu_custom_call" | custom-call | tf_op jit(solution)/shard_map/pallas_call | solution.py:359
  181.2 0.1 collective-permute-done.9.t1
  181.3 0.6 collective-permute-done.11.b1
  181.9 1.3 shard_map.60
  183.2 13.1 %all_to_all.29.got = f32[32,8,128]{2,1,0:T(8,128)S(1)} all-to-all(f32[32,8,128]{2,1,0:T(8,128)S(1)} %get-tuple-element.62), channel_id=1, replica_groups=mesh['wide'=32,'narrow'=4] {'wide'}, dimensions={0} | all-to-all | bytes 262144 | tf_op jit(solution)/shard_map/all_to_all | solution.py:383
  196.3 3.4 %shard_map.61 = (f32[16,4096]{1,0:T(8,128)}, f32[3,2,16,16]{3,2,1,0:T(8,128)}) custom-call(f32[32,8,128]{2,1,0:T(8,128)S(1)} %all_to_all.29.got, f32[16,4096]{1,0:T(8,128)S(1)} %get-tuple-element.63.w0, f32[16,4096]{1,0:T(8,128)S(1)} %get-tuple-element.60.q, f32[16,16]{1,0:T(8,128)S(1)} %get-tuple-element.64.a0, f32[16,16]{1,0:T(8,128)S(1)} %get-tuple-element.65.l0, ...), custom_call_target="tpu_custom_call" | custom-call | tf_op jit(solution)/shard_map/pallas_call | solution.py:359
  (6 shorter events, 0.1 us)
Async XLA Ops:
  5.9 67.5 %copy-start = (bf16[32,288,128]{2,1,0:T(8,128)(2,1)S(1)}, bf16[32,288,128]{2,1,0:T(8,128)(2,1)}, u32[]{:S(2)}) copy-start(bf16[32,288,128]{2,1,0:T(8,128)(2,1)} %get-tuple-element.36.unit) | copy-start | bytes 7077892
  5.9 67.4 %copy-start.1 = (f32[16,4096]{1,0:T(8,128)S(1)}, f32[16,4096]{1,0:T(8,128)}, u32[]{:S(2)}) copy-start(f32[16,4096]{1,0:T(8,128)} %q_init.1) | copy-start | bytes 786436
  73.3 18.9 %copy-start.2 = (s32[2,64]{1,0:T(2,128)S(1)}, s32[2,64]{1,0:T(2,128)}, u32[]{:S(2)}) copy-start(s32[2,64]{1,0:T(2,128)} %pairs.13) | copy-start | bytes 1540
  93.1 5.3 %collective-permute-start = (f32[8,4096]{1,0:T(8,128)S(1)}, f32[8,4096]{1,0:T(8,128)S(1)}, u32[]{:S(2)}, u32[]{:S(2)}) collective-permute-start(f32[8,4096]{1,0:T(8,128)S(1)} %get-tuple-element.40), channel_id=1, source_target_pairs={{0,1},{1,0},{2,3},{3,2},{4,5},{5,4},{6,7},{7,6},{8,9},{9,8},{10,11... | collective-permute-start | bytes 393224 | tf_op jit(solution)/shard_map/ppermute | solution.py:419
  94.5 6.8 %collective-permute-start.2 = (f32[8,4096]{1,0:T(8,128)S(1)}, f32[8,4096]{1,0:T(8,128)S(1)}, u32[]{:S(2)}, u32[]{:S(2)}) collective-permute-start(f32[8,4096]{1,0:T(8,128)S(1)} %get-tuple-element.41), channel_id=1, source_target_pairs={{0,3},{1,2},{2,1},{3,0},{4,7},{5,6},{6,5},{7,4},{8,11},{9,10},{10,... | collective-permute-start | bytes 393224 | tf_op jit(solution)/shard_map/ppermute | solution.py:419
  98.4 5.9 %collective-permute-start.1 = (f32[8,4096]{1,0:T(8,128)S(1)}, f32[8,4096]{1,0:T(8,128)S(1)}, u32[]{:S(2)}, u32[]{:S(2)}) collective-permute-start(f32[8,4096]{1,0:T(8,128)S(1)} %add.18.t0), channel_id=1, source_target_pairs={{0,3},{1,2},{2,1},{3,0},{4,7},{5,6},{6,5},{7,4},{8,11},{9,10},{10,... | collective-permute-start | bytes 393224 | tf_op jit(solution)/shard_map/ppermute | solution.py:419
  101.3 4.0 %collective-permute-start.3 = (f32[8,4096]{1,0:T(8,128)S(1)}, f32[8,4096]{1,0:T(8,128)S(1)}, u32[]{:S(2)}, u32[]{:S(2)}) collective-permute-start(f32[8,4096]{1,0:T(8,128)S(1)} %add.19.b0), channel_id=1, source_target_pairs={{0,1},{1,0},{2,3},{3,2},{4,5},{5,4},{6,7},{7,6},{8,9},{9,8},{10,11... | collective-permute-start | bytes 393224 | tf_op jit(solution)/shard_map/ppermute | solution.py:419
  133.0 4.8 %collective-permute-start.4 = (f32[8,4096]{1,0:T(8,128)S(1)}, f32[8,4096]{1,0:T(8,128)S(1)}, u32[]{:S(2)}, u32[]{:S(2)}) collective-permute-start(f32[8,4096]{1,0:T(8,128)S(1)} %get-tuple-element.47), channel_id=1, source_target_pairs={{0,1},{1,0},{2,3},{3,2},{4,5},{5,4},{6,7},{7,6},{8,9},{9,8},{10,11... | collective-permute-start | bytes 393224 | tf_op jit(solution)/shard_map/ppermute | solution.py:419
  133.0 6.0 %collective-permute-start.6 = (f32[8,4096]{1,0:T(8,128)S(1)}, f32[8,4096]{1,0:T(8,128)S(1)}, u32[]{:S(2)}, u32[]{:S(2)}) collective-permute-start(f32[8,4096]{1,0:T(8,128)S(1)} %get-tuple-element.48), channel_id=1, source_target_pairs={{0,3},{1,2},{2,1},{3,0},{4,7},{5,6},{6,5},{7,4},{8,11},{9,10},{10,... | collective-permute-start | bytes 393224 | tf_op jit(solution)/shard_map/ppermute | solution.py:419
  137.7 5.1 %collective-permute-start.5 = (f32[8,4096]{1,0:T(8,128)S(1)}, f32[8,4096]{1,0:T(8,128)S(1)}, u32[]{:S(2)}, u32[]{:S(2)}) collective-permute-start(f32[8,4096]{1,0:T(8,128)S(1)} %add.20.t0), channel_id=1, source_target_pairs={{0,3},{1,2},{2,1},{3,0},{4,7},{5,6},{6,5},{7,4},{8,11},{9,10},{10,... | collective-permute-start | bytes 393224 | tf_op jit(solution)/shard_map/ppermute | solution.py:419
  139.1 4.4 %collective-permute-start.7 = (f32[8,4096]{1,0:T(8,128)S(1)}, f32[8,4096]{1,0:T(8,128)S(1)}, u32[]{:S(2)}, u32[]{:S(2)}) collective-permute-start(f32[8,4096]{1,0:T(8,128)S(1)} %add.21.b0), channel_id=1, source_target_pairs={{0,1},{1,0},{2,3},{3,2},{4,5},{5,4},{6,7},{7,6},{8,9},{9,8},{10,11... | collective-permute-start | bytes 393224 | tf_op jit(solution)/shard_map/ppermute | solution.py:419
  171.4 4.8 %collective-permute-start.8 = (f32[8,4096]{1,0:T(8,128)S(1)}, f32[8,4096]{1,0:T(8,128)S(1)}, u32[]{:S(2)}, u32[]{:S(2)}) collective-permute-start(f32[8,4096]{1,0:T(8,128)S(1)} %get-tuple-element.55), channel_id=1, source_target_pairs={{0,1},{1,0},{2,3},{3,2},{4,5},{5,4},{6,7},{7,6},{8,9},{9,8},{10,11... | collective-permute-start | bytes 393224 | tf_op jit(solution)/shard_map/ppermute | solution.py:419
  172.0 5.6 %collective-permute-start.10 = (f32[8,4096]{1,0:T(8,128)S(1)}, f32[8,4096]{1,0:T(8,128)S(1)}, u32[]{:S(2)}, u32[]{:S(2)}) collective-permute-start(f32[8,4096]{1,0:T(8,128)S(1)} %get-tuple-element.56), channel_id=1, source_target_pairs={{0,3},{1,2},{2,1},{3,0},{4,7},{5,6},{6,5},{7,4},{8,11},{9,10},{10,... | collective-permute-start | bytes 393224 | tf_op jit(solution)/shard_map/ppermute | solution.py:419
  176.2 5.1 %collective-permute-start.9 = (f32[8,4096]{1,0:T(8,128)S(1)}, f32[8,4096]{1,0:T(8,128)S(1)}, u32[]{:S(2)}, u32[]{:S(2)}) collective-permute-start(f32[8,4096]{1,0:T(8,128)S(1)} %add.22.t0), channel_id=1, source_target_pairs={{0,3},{1,2},{2,1},{3,0},{4,7},{5,6},{6,5},{7,4},{8,11},{9,10},{10,... | collective-permute-start | bytes 393224 | tf_op jit(solution)/shard_map/ppermute | solution.py:419
  177.7 4.2 %collective-permute-start.11 = (f32[8,4096]{1,0:T(8,128)S(1)}, f32[8,4096]{1,0:T(8,128)S(1)}, u32[]{:S(2)}, u32[]{:S(2)}) collective-permute-start(f32[8,4096]{1,0:T(8,128)S(1)} %add.23.b0), channel_id=1, source_target_pairs={{0,1},{1,0},{2,3},{3,2},{4,5},{5,4},{6,7},{7,6},{8,9},{9,8},{10,11... | collective-permute-start | bytes 393224 | tf_op jit(solution)/shard_map/ppermute | solution.py:419

commit v9 on v8

--- a/solution.py
+++ b/solution.py
@@ -45,7 +45,7 @@
 def apply_small(m, x):
     rows = m.shape[0]
     m_high, m_low = split(m)
-    left = cat([cat([m_high, m_high], axis=1), cat([m_low, jnp.zeros_like(m_low)], axis=1)], axis=0)
+    left = cat([cat([m_high, m_high], axis=1), cat([m_low, m_low], axis=1)], axis=0)
     out = mb(left, cat(split(x), axis=0), NN)
     return out[:rows] + out[rows:]
 
@@ -72,7 +72,8 @@
     n = q.shape[0]
     both = cat(split(cat([q, w], axis=0)), axis=0)
     g = mb(both, both, NT)
-    g = g[: 2 * n, : 2 * n] + (g[: 2 * n, 2 * n :] + g[2 * n :, : 2 * n])
+    m = 2 * n
+    g = g[:m, :m] + (g[:m, m:] + g[m:, :m] + g[m:, m:])
     parts = (g[:n, :n], g[:n, n:], g[n:, n:])
     pieces = [p[h : h + 8] for p in parts for h in (0, 8)]
     return cat(pieces + [jnp.zeros((8, BS - 6 * n), F32)], axis=1)
@@ -101,13 +102,13 @@
     high, low = second
     rows = high.shape[0]
     a = mb(cat([high, low], axis=0), stack, NT)
-    return a[:rows, :BS] + a[rows:, :BS] + a[:rows, BS:]
+    return a[:rows, :BS] + (a[rows:, :BS] + a[:rows, BS:] + a[rows:, BS:])
 
 
 def second_term(stack, first):
     high, low = first
     rows = high.shape[0]
-    left = cat([cat([high, high], axis=1), cat([low, jnp.zeros_like(low)], axis=1)], axis=0)
+    left = cat([cat([high, high], axis=1), cat([low, low], axis=1)], axis=0)
     b = mb(left, stack, NN)
     return b[:rows] + b[rows:]
 
@@ -166,7 +167,8 @@
     keep.start()
     both = cat([high, low], axis=0)
     gram = mb(both, both, NT)
-    gram = gram[:vec_rows, :vec_rows] + (gram[:vec_rows, vec_rows:] + gram[vec_rows:, :vec_rows])
+    n = vec_rows
+    gram = gram[:n, :n] + (gram[:n, n:] + gram[n:, :n] + gram[n:, n:])
     pieces = []
     for _ in range(3):
         pieces.append(gram.astype(BF).astype(F32))

time: 200 us -> 200 us (level)
  no operation moved by 1% of the time
where the time goes in v9:
time: 200 us
  blocking collectives  144 us (72%)
  Pallas kernels  29.3 us (15%)
  starting transfers between devices  12.8 us (6%)
  waiting for transfers between devices  12.6 us (6%)
    all_to_all x5, blocking collectives, exchange(): return lax.all_to_all(x, 'wide', split_axis=0, concat_axis=0, tiled=True)  144 us
    pallas_call x12, Pallas kernels, run(): pl.pallas_call(kernel, out_shape=shapes, compiler_params=params, **given)  29.3 us
    ppermute x12, starting transfers between devices, swap(): return lax.ppermute(x, 'narrow', [(i, i ^ mask) for i in range(narrow)])  12.8 us
    ppermute x12, waiting for transfers between devices, swap(): return lax.ppermute(x, 'narrow', [(i, i ^ mask) for i in range(narrow)])  12.6 us
  transfers between devices with their start and end apart: 12, of which 9 were waited for; matrix products, arithmetic and copies ran while one was open for 0% of the time, Pallas kernels for 4%

profile of v9, /device:TPU:1, one launch (start us, length us, event | category | flops | bytes accessed | tf_op | source)
XLA Modules:
  0.0 199.6 jit_solution(4700812224615346951)
XLA Ops:
  0.6 5.2 %shard_map.50 = (bf16[32,288,128]{2,1,0:T(8,128)(2,1)}, bf16[32,592,128]{2,1,0:T(8,128)(2,1)}) custom-call(s32[2,64]{1,0:T(2,128)} %pairs.13, bf16[4096,256]{1,0:T(8,128)(2,1)} %points.1, f32[16,4096]{1,0:T(8,128)} %q_init.1), custom_call_target="tpu_custom_call" | custom-call | tf_op jit(solution)/shard_map/pallas_call | solution.py:361
  5.9 0.0 copy-start
  5.9 0.0 copy-start.1
  5.9 67.5 %all_to_all.25.got = bf16[32,592,128]{2,1,0:T(8,128)(2,1)S(1)} all-to-all(bf16[32,592,128]{2,1,0:T(8,128)(2,1)} %get-tuple-element.35), channel_id=1, replica_groups=mesh['wide'=32,'narrow'=4] {'wide'}, dimensions={0} | all-to-all | bytes 9699328 | tf_op jit(solution)/shard_map/all_to_all | solution.py:385
  73.4 0.0 copy-done
  73.4 0.0 copy-done.1
  73.4 0.0 copy-start.2
  73.4 3.8 %shard_map.51 = (bf16[64,256,128]{2,1,0:T(8,128)(2,1)S(1)}, f32[32,32,128]{2,1,0:T(8,128)S(1)}, f32[16,4096]{1,0:T(8,128)S(1)}, f32[16,128]{1,0:T(8,128)S(1)}, s32[64]{0:T(128)S(1)}) custom-call(bf16[32,592,128]{2,1,0:T(8,128)(2,1)S(1)} %all_to_all.25.got, bf16[32,288,128]{2,1,0:T(8,128)(2,1)S(1)} %copy-done, f32[16,4096]{1,0:T(8,128)S(1)} %copy-done.1), custom_call_target="tpu_custom_call" | custom-call | tf_op jit(solution)/shard_map/pallas_call | solution.py:361
  77.2 15.1 %all_to_all.26.got = f32[32,32,128]{2,1,0:T(8,128)S(1)} all-to-all(f32[32,32,128]{2,1,0:T(8,128)S(1)} %get-tuple-element.38), channel_id=1, replica_groups=mesh['wide'=32,'narrow'=4] {'wide'}, dimensions={0} | all-to-all | bytes 1048576 | tf_op jit(solution)/shard_map/all_to_all | solution.py:385
  92.3 0.0 copy-done.2
  92.3 0.9 shard_map.52
  93.2 1.4 collective-permute-start
  94.5 1.9 collective-permute-start.2
  96.4 2.1 %collective-permute-done = f32[8,4096]{1,0:T(8,128)S(1)} collective-permute-done((f32[8,4096]{1,0:T(8,128)S(1)}, f32[8,4096]{1,0:T(8,128)S(1)}, u32[]{:S(2)}, u32[]{:S(2)}) %collective-permute-start) | collective-permute-done | bytes 131104 | tf_op jit(solution)/shard_map/ppermute | solution.py:421
  98.5 2.8 %collective-permute-start.1 = (f32[8,4096]{1,0:T(8,128)S(1)}, f32[8,4096]{1,0:T(8,128)S(1)}, u32[]{:S(2)}, u32[]{:S(2)}) collective-permute-start(f32[8,4096]{1,0:T(8,128)S(1)} %add.18.t0), channel_id=1, source_target_pairs={{0,3},{1,2},{2,1},{3,0},{4,7},{5,6},{6,5},{7,4},{8,11},{9,10},{10,... | collective-permute-start | bytes 393224 | tf_op jit(solution)/shard_map/ppermute | solution.py:421
  101.3 0.0 collective-permute-done.2
  101.3 0.1 collective-permute-start.3
  101.4 1.7 shard_map.53
  103.1 1.2 collective-permute-done.1.t1
  104.3 1.1 collective-permute-done.3.b1
  105.4 2.1 %shard_map.54 = (f32[16,4096]{1,0:T(8,128)S(1)}, f32[32,72,128]{2,1,0:T(8,128)S(1)}) custom-call(s32[2,64]{1,0:T(2,128)S(1)} %copy-done.2, s32[64]{0:T(128)S(1)} %get-tuple-element.37.ids, f32[8,4096]{1,0:T(8,128)S(1)} %add.18.t0, f32[8,4096]{1,0:T(8,128)S(1)} %collective-permute-done.1.t1, f32[8,4096]{1,0:T(8,128)S(1)} %add.19.b0, ...), custom_call_target="tpu_custom_call" | custom-call | tf_op jit(solution)/shard_map/pallas_call | solution.py:361
  107.5 24.1 %all_to_all.27.got = f32[32,72,128]{2,1,0:T(8,128)S(1)} all-to-all(f32[32,72,128]{2,1,0:T(8,128)S(1)} %get-tuple-element.46), channel_id=1, replica_groups=mesh['wide'=32,'narrow'=4] {'wide'}, dimensions={0} | all-to-all | bytes 2359296 | tf_op jit(solution)/shard_map/all_to_all | solution.py:385
  131.6 1.4 shard_map.55
  133.0 0.1 collective-permute-start.4
  133.1 1.4 collective-permute-start.6
  134.5 3.3 %collective-permute-done.4 = f32[8,4096]{1,0:T(8,128)S(1)} collective-permute-done((f32[8,4096]{1,0:T(8,128)S(1)}, f32[8,4096]{1,0:T(8,128)S(1)}, u32[]{:S(2)}, u32[]{:S(2)}) %collective-permute-start.4) | collective-permute-done | bytes 131104 | tf_op jit(solution)/shard_map/ppermute | solution.py:421
  137.8 1.4 collective-permute-start.5
  139.2 0.0 collective-permute-done.6
  139.2 0.3 collective-permute-start.7
  139.5 2.7 %shard_map.56 = (f32[16,16]{1,0:T(8,128)S(1)}, f32[16,16]{1,0:T(8,128)S(1)}, f32[16,16]{1,0:T(8,128)S(1)}, f32[16,4096]{1,0:T(8,128)S(1)}, f32[16,4096]{1,0:T(8,128)S(1)}, /*index=5*/f32[16,4096]{1,0:T(8,128)S(1)}) custom-call(f32[32,72,128]{2,1,0:T(8,128)S(1)} %all_to_all.27.got, f32[16,4096]{1,0:T(8,128)S(1)} %get-tuple-element.49.w0.y, ...), custom_call_target="tpu_custom_call" | custom-call | tf_op jit(solution)/shard_map/pallas_call | solution.py:361
  142.1 0.8 collective-permute-done.5.t1
  142.9 0.7 collective-permute-done.7.b1
  143.6 2.1 %shard_map.57 = (f32[16,4096]{1,0:T(8,128)S(1)}, f32[16,4096]{1,0:T(8,128)S(1)}, f32[32,72,128]{2,1,0:T(8,128)S(1)}) custom-call(s32[2,64]{1,0:T(2,128)S(1)} %copy-done.2, s32[64]{0:T(128)S(1)} %get-tuple-element.37.ids, f32[8,4096]{1,0:T(8,128)S(1)} %add.20.t0, f32[8,4096]{1,0:T(8,128)S(1)} %collective-permute-done.5.t1, f32[8,4096]{1,0:T(8,128)S(1)} %add.21.b0, ...), custom_call_target="tpu_custom_call" | custom-call | tf_op jit(solution)/shard_map/pallas_call | solution.py:361
  145.7 24.3 %all_to_all.28.got = f32[32,72,128]{2,1,0:T(8,128)S(1)} all-to-all(f32[32,72,128]{2,1,0:T(8,128)S(1)} %get-tuple-element.54), channel_id=1, replica_groups=mesh['wide'=32,'narrow'=4] {'wide'}, dimensions={0} | all-to-all | bytes 2359296 | tf_op jit(solution)/shard_map/all_to_all | solution.py:385
  170.0 1.4 shard_map.58
  171.4 0.6 collective-permute-start.8
  172.1 1.3 collective-permute-start.10
  173.4 2.8 %collective-permute-done.8 = f32[8,4096]{1,0:T(8,128)S(1)} collective-permute-done((f32[8,4096]{1,0:T(8,128)S(1)}, f32[8,4096]{1,0:T(8,128)S(1)}, u32[]{:S(2)}, u32[]{:S(2)}) %collective-permute-start.8) | collective-permute-done | bytes 131104 | tf_op jit(solution)/shard_map/ppermute | solution.py:421
  176.2 1.5 collective-permute-start.9
  177.7 0.0 collective-permute-done.10
  177.7 0.1 collective-permute-start.11
  177.8 3.4 %shard_map.59 = (f32[16,16]{1,0:T(8,128)S(1)}, f32[16,16]{1,0:T(8,128)S(1)}, f32[16,16]{1,0:T(8,128)S(1)}, f32[16,4096]{1,0:T(8,128)S(1)}, f32[16,4096]{1,0:T(8,128)S(1)}, /*index=5*/f32[16,4096]{1,0:T(8,128)}) custom-call(f32[32,72,128]{2,1,0:T(8,128)S(1)} %all_to_all.28.got, f32[16,4096]{1,0:T(8,128)S(1)} %get-tuple-element.57.w0, ...), custom_call_target="tpu_custom_call" | custom-call | tf_op jit(solution)/shard_map/pallas_call | solution.py:361
  181.2 0.1 collective-permute-done.9.t1
  181.3 0.6 collective-permute-done.11.b1
  181.9 1.3 shard_map.60
  183.2 13.1 %all_to_all.29.got = f32[32,8,128]{2,1,0:T(8,128)S(1)} all-to-all(f32[32,8,128]{2,1,0:T(8,128)S(1)} %get-tuple-element.62), channel_id=1, replica_groups=mesh['wide'=32,'narrow'=4] {'wide'}, dimensions={0} | all-to-all | bytes 262144 | tf_op jit(solution)/shard_map/all_to_all | solution.py:385
  196.3 3.4 %shard_map.61 = (f32[16,4096]{1,0:T(8,128)}, f32[3,2,16,16]{3,2,1,0:T(8,128)}) custom-call(f32[32,8,128]{2,1,0:T(8,128)S(1)} %all_to_all.29.got, f32[16,4096]{1,0:T(8,128)S(1)} %get-tuple-element.63.w0, f32[16,4096]{1,0:T(8,128)S(1)} %get-tuple-element.60.q, f32[16,16]{1,0:T(8,128)S(1)} %get-tuple-element.64.a0, f32[16,16]{1,0:T(8,128)S(1)} %get-tuple-element.65.l0, ...), custom_call_target="tpu_custom_call" | custom-call | tf_op jit(solution)/shard_map/pallas_call | solution.py:361
  (6 shorter events, 0.1 us)
Async XLA Ops:
  5.9 67.5 %copy-start = (bf16[32,288,128]{2,1,0:T(8,128)(2,1)S(1)}, bf16[32,288,128]{2,1,0:T(8,128)(2,1)}, u32[]{:S(2)}) copy-start(bf16[32,288,128]{2,1,0:T(8,128)(2,1)} %get-tuple-element.36.unit) | copy-start | bytes 7077892
  5.9 67.5 %copy-start.1 = (f32[16,4096]{1,0:T(8,128)S(1)}, f32[16,4096]{1,0:T(8,128)}, u32[]{:S(2)}) copy-start(f32[16,4096]{1,0:T(8,128)} %q_init.1) | copy-start | bytes 786436
  73.4 18.9 %copy-start.2 = (s32[2,64]{1,0:T(2,128)S(1)}, s32[2,64]{1,0:T(2,128)}, u32[]{:S(2)}) copy-start(s32[2,64]{1,0:T(2,128)} %pairs.13) | copy-start | bytes 1540
  93.2 5.3 %collective-permute-start = (f32[8,4096]{1,0:T(8,128)S(1)}, f32[8,4096]{1,0:T(8,128)S(1)}, u32[]{:S(2)}, u32[]{:S(2)}) collective-permute-start(f32[8,4096]{1,0:T(8,128)S(1)} %get-tuple-element.40), channel_id=1, source_target_pairs={{0,1},{1,0},{2,3},{3,2},{4,5},{5,4},{6,7},{7,6},{8,9},{9,8},{10,11... | collective-permute-start | bytes 393224 | tf_op jit(solution)/shard_map/ppermute | solution.py:421
  94.5 6.8 %collective-permute-start.2 = (f32[8,4096]{1,0:T(8,128)S(1)}, f32[8,4096]{1,0:T(8,128)S(1)}, u32[]{:S(2)}, u32[]{:S(2)}) collective-permute-start(f32[8,4096]{1,0:T(8,128)S(1)} %get-tuple-element.41), channel_id=1, source_target_pairs={{0,3},{1,2},{2,1},{3,0},{4,7},{5,6},{6,5},{7,4},{8,11},{9,10},{10,... | collective-permute-start | bytes 393224 | tf_op jit(solution)/shard_map/ppermute | solution.py:421
  98.5 5.8 %collective-permute-start.1 = (f32[8,4096]{1,0:T(8,128)S(1)}, f32[8,4096]{1,0:T(8,128)S(1)}, u32[]{:S(2)}, u32[]{:S(2)}) collective-permute-start(f32[8,4096]{1,0:T(8,128)S(1)} %add.18.t0), channel_id=1, source_target_pairs={{0,3},{1,2},{2,1},{3,0},{4,7},{5,6},{6,5},{7,4},{8,11},{9,10},{10,... | collective-permute-start | bytes 393224 | tf_op jit(solution)/shard_map/ppermute | solution.py:421
  101.3 4.0 %collective-permute-start.3 = (f32[8,4096]{1,0:T(8,128)S(1)}, f32[8,4096]{1,0:T(8,128)S(1)}, u32[]{:S(2)}, u32[]{:S(2)}) collective-permute-start(f32[8,4096]{1,0:T(8,128)S(1)} %add.19.b0), channel_id=1, source_target_pairs={{0,1},{1,0},{2,3},{3,2},{4,5},{5,4},{6,7},{7,6},{8,9},{9,8},{10,11... | collective-permute-start | bytes 393224 | tf_op jit(solution)/shard_map/ppermute | solution.py:421
  133.0 4.8 %collective-permute-start.4 = (f32[8,4096]{1,0:T(8,128)S(1)}, f32[8,4096]{1,0:T(8,128)S(1)}, u32[]{:S(2)}, u32[]{:S(2)}) collective-permute-start(f32[8,4096]{1,0:T(8,128)S(1)} %get-tuple-element.47), channel_id=1, source_target_pairs={{0,1},{1,0},{2,3},{3,2},{4,5},{5,4},{6,7},{7,6},{8,9},{9,8},{10,11... | collective-permute-start | bytes 393224 | tf_op jit(solution)/shard_map/ppermute | solution.py:421
  133.1 6.1 %collective-permute-start.6 = (f32[8,4096]{1,0:T(8,128)S(1)}, f32[8,4096]{1,0:T(8,128)S(1)}, u32[]{:S(2)}, u32[]{:S(2)}) collective-permute-start(f32[8,4096]{1,0:T(8,128)S(1)} %get-tuple-element.48), channel_id=1, source_target_pairs={{0,3},{1,2},{2,1},{3,0},{4,7},{5,6},{6,5},{7,4},{8,11},{9,10},{10,... | collective-permute-start | bytes 393224 | tf_op jit(solution)/shard_map/ppermute | solution.py:421
  137.8 5.1 %collective-permute-start.5 = (f32[8,4096]{1,0:T(8,128)S(1)}, f32[8,4096]{1,0:T(8,128)S(1)}, u32[]{:S(2)}, u32[]{:S(2)}) collective-permute-start(f32[8,4096]{1,0:T(8,128)S(1)} %add.20.t0), channel_id=1, source_target_pairs={{0,3},{1,2},{2,1},{3,0},{4,7},{5,6},{6,5},{7,4},{8,11},{9,10},{10,... | collective-permute-start | bytes 393224 | tf_op jit(solution)/shard_map/ppermute | solution.py:421
  139.2 4.4 %collective-permute-start.7 = (f32[8,4096]{1,0:T(8,128)S(1)}, f32[8,4096]{1,0:T(8,128)S(1)}, u32[]{:S(2)}, u32[]{:S(2)}) collective-permute-start(f32[8,4096]{1,0:T(8,128)S(1)} %add.21.b0), channel_id=1, source_target_pairs={{0,1},{1,0},{2,3},{3,2},{4,5},{5,4},{6,7},{7,6},{8,9},{9,8},{10,11... | collective-permute-start | bytes 393224 | tf_op jit(solution)/shard_map/ppermute | solution.py:421
  171.4 4.8 %collective-permute-start.8 = (f32[8,4096]{1,0:T(8,128)S(1)}, f32[8,4096]{1,0:T(8,128)S(1)}, u32[]{:S(2)}, u32[]{:S(2)}) collective-permute-start(f32[8,4096]{1,0:T(8,128)S(1)} %get-tuple-element.55), channel_id=1, source_target_pairs={{0,1},{1,0},{2,3},{3,2},{4,5},{5,4},{6,7},{7,6},{8,9},{9,8},{10,11... | collective-permute-start | bytes 393224 | tf_op jit(solution)/shard_map/ppermute | solution.py:421
  172.1 5.6 %collective-permute-start.10 = (f32[8,4096]{1,0:T(8,128)S(1)}, f32[8,4096]{1,0:T(8,128)S(1)}, u32[]{:S(2)}, u32[]{:S(2)}) collective-permute-start(f32[8,4096]{1,0:T(8,128)S(1)} %get-tuple-element.56), channel_id=1, source_target_pairs={{0,3},{1,2},{2,1},{3,0},{4,7},{5,6},{6,5},{7,4},{8,11},{9,10},{10,... | collective-permute-start | bytes 393224 | tf_op jit(solution)/shard_map/ppermute | solution.py:421
  176.2 5.1 %collective-permute-start.9 = (f32[8,4096]{1,0:T(8,128)S(1)}, f32[8,4096]{1,0:T(8,128)S(1)}, u32[]{:S(2)}, u32[]{:S(2)}) collective-permute-start(f32[8,4096]{1,0:T(8,128)S(1)} %add.22.t0), channel_id=1, source_target_pairs={{0,3},{1,2},{2,1},{3,0},{4,7},{5,6},{6,5},{7,4},{8,11},{9,10},{10,... | collective-permute-start | bytes 393224 | tf_op jit(solution)/shard_map/ppermute | solution.py:421
  177.7 4.2 %collective-permute-start.11 = (f32[8,4096]{1,0:T(8,128)S(1)}, f32[8,4096]{1,0:T(8,128)S(1)}, u32[]{:S(2)}, u32[]{:S(2)}) collective-permute-start(f32[8,4096]{1,0:T(8,128)S(1)} %add.23.b0), channel_id=1, source_target_pairs={{0,1},{1,0},{2,3},{3,2},{4,5},{5,4},{6,7},{7,6},{8,9},{9,8},{10,11... | collective-permute-start | bytes 393224 | tf_op jit(solution)/shard_map/ppermute | solution.py:421
